TPU v7x, 128 devices: a whole 4x4x4 slice. The times are simulated.
128 devices in a mesh: dp: 2 (over core), sp: 64 (over x, y, z).
Axes of the slice: x: 4, y: 4, z: 4, core: 2. Of those that a mesh axis runs over, the one named last changes fastest.
Arguments:
- latents: bfloat16 [256, 64, 64, 128], P(('dp', 'sp')), may hold values from -6 to 6
- cotangent: bfloat16 [256, 64, 64, 128], P(('dp', 'sp')), may hold values from -6 to 6
- frame_counts: int32 [2, 64], P('dp'), may hold values from 1 to 2, as said below
- spatial_weight: bfloat16 [3, 3, 128, 128], replicated, may hold values from -0.1875 to 0.1875
- temporal_weight: bfloat16 [3, 128, 128], replicated, may hold values from -0.3125 to 0.3125
Outputs:
- block_out: bfloat16 [256, 64, 64, 128], P(('dp', 'sp'))
- input_grad: bfloat16 [256, 64, 64, 128], P(('dp', 'sp'))
- spatial_grad: float32 [3, 3, 128, 128], replicated
- temporal_grad: float32 [3, 128, 128], replicated
Inputs may be any that keep to these rules, and one draw needn't show every extreme that they name: `frame_counts`: in each group every device holds 1 or 2 frames and the counts sum to 72; in each group some devices hold 2.
All inputs are finite; a program needn't handle non-finite values.
Results may differ from a plain program's by a relative error of at most 0.0054.
Values may be sent and summed in bfloat16 or wider, within the bound.
No kernel may reach another device: no remote copies, remote signals or barrier semaphores. Data moves between devices by JAX's collectives and lax.ppermute only.
A program may use at most 192 MiB of HBM per device.

v0:
```python
import jax
import jax.numpy as jnp
from jax import lax
from jax.sharding import PartitionSpec as P

FRAMES = 9


def spatial_apply(padded, kernel, rows, cols):
    total = jnp.zeros(padded.shape[:1] + (rows, cols, kernel.shape[3]), jnp.float32)
    for row_tap in range(3):
        for col_tap in range(3):
            window = padded[:, row_tap : row_tap + rows, col_tap : col_tap + cols]
            total = total + jnp.einsum(
                "fhwc,cd->fhwd",
                window,
                kernel[row_tap, col_tap],
                preferred_element_type=jnp.float32,
            )
    return total


def spatial_weights_grad(padded, upstream, rows, cols):
    grads = []
    for row_tap in range(3):
        for col_tap in range(3):
            window = padded[:, row_tap : row_tap + rows, col_tap : col_tap + cols]
            grads.append(
                jnp.einsum("fhwc,fhwd->cd", window, upstream, preferred_element_type=jnp.float32)
            )
    return jnp.stack(grads).reshape(3, 3, upstream.shape[3], upstream.shape[3])


def temporal_forward(frames, kernel):
    nclip = frames.shape[0] // FRAMES
    blocks = frames.reshape(nclip, FRAMES, -1, frames.shape[3])
    padded = jnp.pad(blocks, ((0, 0), (2, 0), (0, 0), (0, 0)))
    total = jnp.zeros(blocks.shape, jnp.float32)
    for tap_index in range(3):
        total = total + jnp.einsum(
            "cfpd,de->cfpe",
            padded[:, 2 - tap_index : 2 - tap_index + FRAMES],
            kernel[tap_index],
            preferred_element_type=jnp.float32,
        )
    return total.reshape(frames.shape)


def temporal_backward(grads, kernel):
    nclip = grads.shape[0] // FRAMES
    blocks = grads.reshape(nclip, FRAMES, -1, grads.shape[3])
    padded = jnp.pad(blocks, ((0, 0), (0, 2), (0, 0), (0, 0)))
    total = jnp.zeros(blocks.shape, jnp.float32)
    for tap_index in range(3):
        total = total + jnp.einsum(
            "cfpe,de->cfpd",
            padded[:, tap_index : tap_index + FRAMES],
            kernel[tap_index],
            preferred_element_type=jnp.float32,
        )
    return total.reshape(grads.shape)


def temporal_weights_grad(frames, grads):
    nclip = frames.shape[0] // FRAMES
    blocks = frames.reshape(nclip, FRAMES, -1, frames.shape[3])
    gblocks = grads.reshape(nclip, FRAMES, -1, grads.shape[3])
    padded = jnp.pad(blocks, ((0, 0), (2, 0), (0, 0), (0, 0)))
    result = []
    for tap_index in range(3):
        result.append(
            jnp.einsum(
                "cfpd,cfpe->de",
                padded[:, 2 - tap_index : 2 - tap_index + FRAMES],
                gblocks,
                preferred_element_type=jnp.float32,
            )
        )
    return jnp.stack(result)


def frame_index(counts_row, slots, nframes):
    sp_count = counts_row.shape[0]
    starts = jnp.cumsum(counts_row) - counts_row
    frame_ids = jnp.arange(nframes, dtype=jnp.int32)
    holder = jnp.sum((starts[None, :] <= frame_ids[:, None]).astype(jnp.int32), axis=1) - 1
    first_frame = jnp.sum(
        jnp.where(
            jnp.arange(sp_count, dtype=jnp.int32)[None, :] == holder[:, None], starts[None, :], 0
        ),
        axis=1,
    )
    return holder * slots + frame_ids - first_frame


def slot_layout(counts_row, slots):
    starts = jnp.cumsum(counts_row) - counts_row
    offset = jnp.arange(counts_row.shape[0] * slots, dtype=jnp.int32) % slots
    slot_frame = jnp.repeat(starts, slots) + offset
    is_live = offset < jnp.repeat(counts_row, slots)
    return (slot_frame, is_live)


def to_slots(frames, slot_frame, is_live):
    picked = jnp.take(frames, jnp.clip(slot_frame, 0, frames.shape[0] - 1), axis=0)
    return jnp.where(is_live[:, None, None, None], picked, jnp.zeros_like(picked))


def local(latents, cotangent, frame_counts, spatial_weight, temporal_weight):
    counts_row = frame_counts[0]
    slots = latents.shape[0]
    height = latents.shape[1]
    cols = latents.shape[2]
    sp_count = lax.axis_size("sp")
    nframes = sp_count // 8 * FRAMES
    index = frame_index(counts_row, slots, nframes)
    slot_frame, is_live = slot_layout(counts_row, slots)
    flipped = jnp.transpose(spatial_weight[::-1, ::-1], (0, 1, 3, 2))
    scale = float(lax.axis_size("dp") * nframes * height * cols) ** (-0.5)
    here = lax.axis_index("sp")
    own_count = jnp.sum(jnp.where(jnp.arange(sp_count, dtype=jnp.int32) == here, counts_row, 0))
    own_live = (jnp.arange(slots, dtype=jnp.int32) < own_count)[:, None, None, None]
    wide = latents.astype(jnp.float32)
    activated = jax.nn.silu(wide).astype(jnp.bfloat16)
    act_pad = jnp.pad(activated, ((0, 0), (1, 1), (1, 1), (0, 0)))
    spatial_out = spatial_apply(act_pad, spatial_weight, height, cols).astype(jnp.bfloat16)
    band_out, band_grad = (
        lax.all_to_all(spatial_out, "sp", split_axis=1, concat_axis=0, tiled=True),
        lax.all_to_all(cotangent, "sp", split_axis=1, concat_axis=0, tiled=True),
    )
    frames_out = jnp.take(band_out, index, axis=0)
    grads = jnp.take(band_grad, index, axis=0)
    temporal_out = temporal_forward(frames_out, temporal_weight).astype(jnp.bfloat16)
    upstream = temporal_backward(grads, temporal_weight).astype(jnp.bfloat16)
    temporal_sum = temporal_weights_grad(frames_out, grads)
    slab_out, slab_up = (
        lax.all_to_all(
            to_slots(temporal_out, slot_frame, is_live),
            "sp",
            split_axis=0,
            concat_axis=1,
            tiled=True,
        ),
        lax.all_to_all(
            to_slots(upstream, slot_frame, is_live), "sp", split_axis=0, concat_axis=1, tiled=True
        ),
    )
    result = (wide + slab_out.astype(jnp.float32)).astype(jnp.bfloat16)
    block_out = jnp.where(own_live, result, jnp.zeros_like(result))
    up_pad = jnp.pad(slab_up, ((0, 0), (1, 1), (1, 1), (0, 0)))
    back_spatial = spatial_apply(up_pad, flipped, height, cols)
    sig = jax.nn.sigmoid(wide)
    in_grad = (
        cotangent.astype(jnp.float32) + back_spatial * sig * (1.0 + wide * (1.0 - sig))
    ).astype(jnp.bfloat16)
    input_grad = jnp.where(own_live, in_grad, jnp.zeros_like(in_grad))
    spatial_sum = spatial_weights_grad(act_pad, slab_up, height, cols)
    spatial_total, temporal_total = lax.psum(
        (spatial_sum * scale, temporal_sum * scale), ("dp", "sp")
    )
    return (block_out, input_grad, spatial_total, temporal_total)


def solution(mesh):
    return jax.shard_map(
        local,
        mesh=mesh,
        in_specs=(
            P(("dp", "sp"), None, None, None),
            P(("dp", "sp"), None, None, None),
            P("dp", None),
            P(),
            P(),
        ),
        out_specs=(P(("dp", "sp"), None, None, None), P(("dp", "sp"), None, None, None), P(), P()),
        check_vma=False,
    )
```

profile of v0, /device:TPU:1, one launch (start us, length us, event | category | flops | bytes accessed | tf_op | source)
XLA Modules:
  0.0 363.2 jit_solution(17644631978763687256)
XLA Ops:
  7.2 3.2 copy.32
  10.3 12.2 %all-to-all-start.2 = ((bf16[2,64,64,128]{3,2,0,1:T(8,128)(2,1)}), bf16[2,64,64,128]{3,2,0,1:T(8,128)(2,1)}, u32[]{:S(2)}, u32[]{:S(2)}) async-start(bf16[2,64,64,128]{3,2,0,1:T(8,128)(2,1)} %copy.32), calls=%async_computation.2 | async-start | bytes 4194304 | tf_op jit(solution)/shard_map/all_to_all | solution.py:129
  22.6 2.7 fusion.3
  26.7 2.7 fusion.44
  29.4 2.7 fusion.40
  32.0 2.7 fusion.36
  34.7 2.6 fusion.32
  37.4 2.7 fusion.56
  40.0 2.6 fusion.146
  42.7 9.2 %add_convert_fusion = bf16[2,64,64,128]{3,2,1,0:T(8,128)(2,1)S(1)} fusion(f32[2,64,64,128]{3,2,1,0:T(8,128)} %fusion.32, f32[2,64,64,128]{3,2,1,0:T(8,128)} %fusion.36, f32[2,64,64,128]{3,2,1,0:T(8,128)} %fusion.40, f32[2,64,64,128]{3,2,1,0:T(8,128)} %fusion.146, f32[2,64,64,128]{3,2,1,0:T(8,128)} %fusion.44, f32[2,64,64,128]{3,2,1,0:T(8,128)S(1)} %fusion.48, ...), kind=kOutput, calls=%fused_computation.17 | convolution fusion | flops 277872640 | bytes 37781504 | tf_op jit(solution)/shard_map/fhwc,cd->fhwd/dot_general | solution.py:14
  53.5 10.3 %all-to-all-start = ((bf16[2,64,64,128]{3,2,0,1:T(8,128)(2,1)}), bf16[2,64,64,128]{3,2,0,1:T(8,128)(2,1)}, u32[]{:S(2)}, u32[]{:S(2)}) async-start(bf16[2,64,64,128]{3,2,0,1:T(8,128)(2,1)} %copy.29), calls=%async_computation | async-start | bytes 4194304 | tf_op jit(solution)/shard_map/all_to_all | solution.py:128
  65.4 3.4 gather_fusion.2
  68.8 21.1 %all-to-all-done = bf16[2,64,64,128]{3,2,0,1:T(8,128)(2,1)} async-done(((bf16[2,64,64,128]{3,2,0,1:T(8,128)(2,1)}), bf16[2,64,64,128]{3,2,0,1:T(8,128)(2,1)}, u32[]{:S(2)}, u32[]{:S(2)}) %all-to-all-start) | async-done | bytes 2097184 | tf_op jit(solution)/shard_map/all_to_all | solution.py:128
  89.9 3.4 gather_fusion
  101.4 3.4 gather_fusion.1
  104.8 3.9 %add_convert_fusion.1 = bf16[8,9,64,128]{3,2,1,0:T(8,128)(2,1)} fusion(f32[8,9,64,128]{3,2,1,0:T(8,128)} %fusion.158, f32[8,9,64,128]{3,2,1,0:T(8,128)} %fusion.154, bf16[8,9,64,128]{3,2,1,0:T(8,128)(2,1)S(1)} %bitcast.345, bf16[3,128,128]{2,1,0:T(8,128)(2,1)S(1)} %copy-done.8), kind=kOutput, calls=%fused_computation.18 | convolution fusion | flops 119209984 | bytes 7110656 | tf_op jit(solution)/shard_map/cfpe,de->cfpd/dot_general | solution.py:55
  108.7 3.4 gather_fusion.3
  112.1 4.0 %fusion.10 = (bf16[128,1,64,128]{3,2,1,0:T(8,128)(2,1)}, bf16[128,1,64,128]{3,2,1,0:T(8,128)(2,1)}) fusion(bf16[128,64,128]{2,1,0:T(8,128)(2,1)} %gather_fusion.3, pred[128]{0:T(512)(128)(4,1)S(1)} %get-tuple-element.8, pred[128]{0:T(512)(128)(4,1)S(1)} %get-tuple-element.18, bf16[128,64,128]{2,1,0:T(8,128)(2,1)} %gather_fusion.1), kind=kLoop, calls=%fused_computation.22 | loop fusion | flops 4194304 | bytes 8388864 | tf_op jit(solution)/shard_map/jit(_where)/select_n | solution.py:106
  116.1 8.2 %all-to-all-start.3 = ((bf16[128,1,64,128]{3,2,1,0:T(8,128)(2,1)}), bf16[128,1,64,128]{3,2,1,0:T(8,128)(2,1)}, u32[]{:S(2)}, u32[]{:S(2)}) async-start(bf16[128,1,64,128]{3,2,1,0:T(8,128)(2,1)} %get-tuple-element.12), calls=%async_computation.3 | async-start | bytes 4194304 | tf_op jit(solution)/shard_map/all_to_all | solution.py:144
  132.1 18.6 %all-to-all-done.3 = bf16[128,1,64,128]{3,2,1,0:T(8,128)(2,1)} async-done(((bf16[128,1,64,128]{3,2,1,0:T(8,128)(2,1)}), bf16[128,1,64,128]{3,2,1,0:T(8,128)(2,1)}, u32[]{:S(2)}, u32[]{:S(2)}) %all-to-all-start.3) | async-done | bytes 2097184 | tf_op jit(solution)/shard_map/all_to_all | solution.py:144
  150.7 8.2 %all-to-all-start.1 = ((bf16[128,1,64,128]{3,2,1,0:T(8,128)(2,1)}), bf16[128,1,64,128]{3,2,1,0:T(8,128)(2,1)}, u32[]{:S(2)}, u32[]{:S(2)}) async-start(bf16[128,1,64,128]{3,2,1,0:T(8,128)(2,1)} %get-tuple-element.13), calls=%async_computation.1 | async-start | bytes 4194304 | tf_op jit(solution)/shard_map/all_to_all | solution.py:137
  163.4 5.0 %fusion.141 = f32[2,64,64,128]{3,2,1,0:T(8,128)} fusion(bf16[3,3,128,128]{3,2,1,0:T(8,128)(2,1)S(1)} %copy-done.7, bf16[64,2,1,64,128]{4,3,1,0,2:T(8,128)(2,1)} %bitcast.67), kind=kOutput, calls=%fused_computation.131 | convolution fusion | flops 268435456 | bytes 6324224 | tf_op jit(solution)/shard_map/fhwc,cd->fhwd/dot_general | solution.py:14
  168.4 2.7 fusion.17
  171.0 2.7 fusion.15
  173.7 2.6 fusion.13
  176.4 2.7 fusion.23
  179.0 2.7 fusion.21
  181.7 2.7 fusion.19
  204.2 2.4 fusion.25
  207.6 12.8 %broadcast_select_fusion = bf16[2,64,64,128]{3,2,1,0:T(8,128)(2,1)} fusion(pred[2]{0:T(512)(128)(4,1)S(1)} %iota_compare_fusion.2, bf16[2,64,64,128]{3,2,1,0:T(8,128)(2,1)S(1)} %copy-done.4, bf16[2,64,64,128]{3,2,1,0:T(8,128)(2,1)S(1)} %bitcast.342, f32[2,64,64,128]{3,2,1,0:T(8,128)} %fusion.13, f32[2,64,64,128]{3,2,1,0:T(8,128)} %fusion.15, ...), kind=kOutput, calls=%fused_computation.41 | convolution fusion | flops 290455552 | bytes 41976320 | tf_op jit(solution)/shard_map/fhwc,cd->fhwd/dot_general | solution.py:14
  220.4 4.6 %fusion.9 = bf16[2,64,64,128]{3,2,1,0:T(8,128)(2,1)} fusion(bf16[2,64,64,128]{3,2,1,0:T(8,128)(2,1)} %param.9, pred[2]{0:T(512)(128)(4,1)S(1)} %iota_compare_fusion.2, bf16[64,2,1,64,128]{4,3,1,0,2:T(8,128)(2,1)} %bitcast.159), kind=kLoop, calls=%fused_computation.20 | loop fusion | flops 5242880 | bytes 6291458 | tf_op jit(solution)/shard_map/jit(_where)/select_n | solution.py:149
  225.0 127.8 %all-reduce.7.cloned.1.call-done = (f32[3,3,128,128]{3,2,1,0:T(8,128)}, f32[3,128,128]{2,1,0:T(8,128)}) async-done(((f32[3,3,128,128]{3,2,1,0:T(8,128)}, f32[3,128,128]{2,1,0:T(8,128)}), (f32[3,3,128,128]{3,2,1,0:T(8,128)}, f32[3,128,128]{2,1,0:T(8,128)})) %all-reduce.7.cloned.1.call-update) | async-done | bytes 786448 | tf_op jit(solution)/shard_map/psum | solution.py:158
  (69 shorter events, 48.9 us)
Async XLA Ops:
  10.3 43.2 %all-to-all-start.2 = ((bf16[2,64,64,128]{3,2,0,1:T(8,128)(2,1)}), bf16[2,64,64,128]{3,2,0,1:T(8,128)(2,1)}, u32[]{:S(2)}, u32[]{:S(2)}) async-start(bf16[2,64,64,128]{3,2,0,1:T(8,128)(2,1)} %copy.32), calls=%async_computation.2 | async-start | bytes 4194304 | tf_op jit(solution)/shard_map/all_to_all | solution.py:129
  22.6 2.7 copy-start.6
  53.5 10.3 %copy-start.9 = (s32[1,64]{1,0:T(1,128)S(1)}, s32[1,64]{1,0:T(1,128)}, u32[]{:S(2)}) copy-start(s32[1,64]{1,0:T(1,128)} %param.11) | copy-start | bytes 772
  53.5 36.5 %all-to-all-start = ((bf16[2,64,64,128]{3,2,0,1:T(8,128)(2,1)}), bf16[2,64,64,128]{3,2,0,1:T(8,128)(2,1)}, u32[]{:S(2)}, u32[]{:S(2)}) async-start(bf16[2,64,64,128]{3,2,0,1:T(8,128)(2,1)} %copy.29), calls=%async_computation | async-start | bytes 4194304 | tf_op jit(solution)/shard_map/all_to_all | solution.py:128
  93.3 2.0 copy-start.8
  95.3 4.7 %copy-start.2 = (bf16[72,1,64,128]{3,2,0,1:T(8,128)(2,1)}, bf16[72,1,64,128]{3,2,0,1:T(8,128)(2,1)S(1)}, u32[]{:S(2)}) copy-start(bf16[72,1,64,128]{3,2,0,1:T(8,128)(2,1)S(1)} %get-tuple-element.15) | copy-start | bytes 3538948
  116.1 34.6 %all-to-all-start.3 = ((bf16[128,1,64,128]{3,2,1,0:T(8,128)(2,1)}), bf16[128,1,64,128]{3,2,1,0:T(8,128)(2,1)}, u32[]{:S(2)}, u32[]{:S(2)}) async-start(bf16[128,1,64,128]{3,2,1,0:T(8,128)(2,1)} %get-tuple-element.12), calls=%async_computation.3 | async-start | bytes 4194304 | tf_op jit(solution)/shard_map/all_to_all | solution.py:144
  126.2 4.2 %copy-start.3 = (bf16[72,1,64,128]{3,2,0,1:T(8,128)(2,1)S(1)}, bf16[72,1,64,128]{3,2,0,1:T(8,128)(2,1)}, u32[]{:S(2)}) copy-start(bf16[72,1,64,128]{3,2,0,1:T(8,128)(2,1)} %copy-done.2) | copy-start | bytes 3538948
  150.7 69.8 %all-to-all-start.1 = ((bf16[128,1,64,128]{3,2,1,0:T(8,128)(2,1)}), bf16[128,1,64,128]{3,2,1,0:T(8,128)(2,1)}, u32[]{:S(2)}, u32[]{:S(2)}) async-start(bf16[128,1,64,128]{3,2,1,0:T(8,128)(2,1)} %get-tuple-element.13), calls=%async_computation.1 | async-start | bytes 4194304 | tf_op jit(solution)/shard_map/all_to_all | solution.py:137
  158.9 193.9 %all-reduce.7.cloned.1.call-start = ((), (), s32[]{:S(2)}) async-start(), calls=%async_computation.4 | async-start | bytes 1572864 | tf_op jit(solution)/shard_map/psum | solution.py:158
  161.5 1.8 copy-start.7
  163.4 18.3 %copy-start = (bf16[64,2,1,64,128]{4,3,0,1,2:T(8,128)(2,1)}, bf16[64,2,1,64,128]{4,3,0,1,2:T(8,128)(2,1)S(1)}, u32[]{:S(2)}) copy-start(bf16[64,2,1,64,128]{4,3,0,1,2:T(8,128)(2,1)S(1)} %copy.81) | copy-start | bytes 6291460
  204.1 2.7 copy-start.1
  204.1 2.8 copy-start.4
  204.1 3.5 copy-start.5
Sparse Core Ops, SparseCore 0:
  204.2 148.5 all-reduce.6
where the time goes:
time: 365 us; the launch traced here: 363 us
  waiting for transfers between devices  167 us (46%)
  matrix products  96.8 us (27%)
  starting transfers between devices  39.2 us (11%)
  local copies, waits for them, and re-layouts  28.5 us (8%)
  other arithmetic  16.7 us (5%)
  between operations  14.6 us (4%)
    psum x1, waiting for transfers between devices, local(): lax.psum((spatial_sum * scale, temporal_sum * scale), ('dp', 'sp'))  128 us
    dot_general x18, matrix products, spatial_apply(): jnp.einsum('fhwc,cd->fhwd', window, kernel[row_tap, col_tap], preferred_e...  62.8 us
    dot_general x9, matrix products, spatial_weights_grad(): jnp.einsum('fhwc,fhwd->cd', window, upstream, preferred_element_type=jnp....  21.2 us
    all_to_all x1, waiting for transfers between devices, local(): lax.all_to_all(spatial_out, 'sp', split_axis=1, concat_axis=0, tiled=True)  21.1 us
    all_to_all x1, waiting for transfers between devices, local(): lax.all_to_all(to_slots(upstream, slot_frame, is_live), 'sp', split_axis=...  18.6 us
    all_to_all x1, starting transfers between devices, local(): lax.all_to_all(cotangent, 'sp', split_axis=1, concat_axis=0, tiled=True)  12.2 us
    all_to_all x1, starting transfers between devices, local(): lax.all_to_all(spatial_out, 'sp', split_axis=1, concat_axis=0, tiled=True)  10.3 us
    unnamed x24, local copies, waits for them, and re-layouts  9.33 us
  transfers between devices with their start and end apart: 5, of which 3 were waited for; matrix products, arithmetic and copies ran while one was open for 30% of the time, Pallas kernels for 0%

commit v1 on v0

v1 whole, which is shorter than its diff:
```python
import functools

import jax
import jax.numpy as jnp
from jax import lax
from jax.experimental import pallas as pl
from jax.experimental.pallas import tpu as pltpu
from jax.sharding import PartitionSpec as P

FRAMES = 9
CH = 128
ROWS = 64
COLS = 64
PAIRS = ROWS // 2
BLK = 8
NBLK = PAIRS // BLK
PX = BLK * COLS
F32 = jnp.float32
BF16 = jnp.bfloat16
VMEM_BYTES = 48 * 1024 * 1024


def dot(a, b):
    return jnp.dot(a, b, preferred_element_type=F32)


def dot_t(a, b):
    return lax.dot_general(a, b, (((0,), (0,)), ((), ())), preferred_element_type=F32)


def clear_edges(wide):
    wide[0, :, 0 : 3 * CH] = jnp.zeros((COLS, 3 * CH), BF16)
    wide[PAIRS, :, 3 * CH : 6 * CH] = jnp.zeros((COLS, 3 * CH), BF16)


def put_row(wide, t, half, a):
    col = lax.broadcasted_iota(jnp.int32, a.shape, 1)
    before = jnp.where(col == 0, 0.0, pltpu.roll(a, 1, 1))
    after = jnp.where(col == COLS - 1, 0.0, pltpu.roll(a, COLS - 1, 1))
    at = pl.ds(t + half, BLK)
    base = 0 if half else 3 * CH
    wide[at, :, base : base + CH] = before.astype(BF16)
    wide[at, :, base + CH : base + 2 * CH] = a.astype(BF16)
    wide[at, :, base + 2 * CH : base + 3 * CH] = after.astype(BF16)


def silu(x):
    return x * jax.nn.sigmoid(x)


def fill_act(wide, x_ref):
    clear_edges(wide)

    def body(n, _):
        t = n * BLK
        for half in range(2):
            put_row(wide, t, half, silu(x_ref[pl.ds(t, BLK), half].astype(F32)))
        return 0

    lax.fori_loop(0, NBLK, body, 0)


def windows(wide, t):
    low = wide[pl.ds(t, BLK)].reshape(PX, 6 * CH)
    high = wide[pl.ds(t + 1, BLK)].reshape(PX, 6 * CH)
    return low, high


def conv(wide, w_ref, t):
    low, high = windows(wide, t)
    return dot(low, w_ref[0 : 6 * CH, :]) + dot(high, w_ref[6 * CH : 12 * CH, :])


def conv_to(out_ref, wide, w_ref):
    def body(n, _):
        t = n * BLK
        out_ref[pl.ds(t, BLK)] = conv(wide, w_ref, t).astype(BF16).reshape(BLK, COLS, 2 * CH)
        return 0

    lax.fori_loop(0, NBLK, body, 0)


def pair(ref, t):
    v = ref[pl.ds(t, BLK)]
    return jnp.concatenate([v[:, 0], v[:, 1]], axis=-1).reshape(PX, 2 * CH)


def flat(ref, t):
    return ref[pl.ds(t, BLK)].reshape(PX, 2 * CH)


def frame_spec(lead=()):
    return lead + (PAIRS, 2, COLS, CH)


def forward_kernel(info, x_ref, w_ref, s_ref, wide):
    fill_act(wide, x_ref.at[0])
    conv_to(s_ref.at[0], wide, w_ref)

    @pl.when(info[0] == 2)
    def _():
        fill_act(wide, x_ref.at[1])
        conv_to(s_ref.at[1], wide, w_ref)


def grad_kernel(info, x_ref, g_ref, xh_ref, gn_ref, s_ref, w_ref, tw_ref, out_ref, sh_ref, wide, gsel, vw, acc, tacc, *, scale):
    two = info[0] == 2
    acc[...] = jnp.zeros_like(acc)
    tacc[...] = jnp.zeros_like(tacc)
    def choose(n, _):
        t = n * BLK
        gsel[pl.ds(t, BLK)] = jnp.where(two, g_ref[1, pl.ds(t, BLK)], gn_ref[pl.ds(t, BLK)])
        return 0

    lax.fori_loop(0, NBLK, choose, 0)

    def masked(k, keep):
        vw[k] = jnp.where(keep, tw_ref[k], jnp.zeros_like(tw_ref[k]))

    def add_spatial(value, t):
        low, high = windows(wide, t)
        v = value.astype(BF16)
        acc[:, 0 : 6 * CH] += dot_t(v, low)
        acc[:, 6 * CH : 12 * CH] += dot_t(v, high)

    def add_temporal(s0, s1, g0, g1, keep0, keep1, t):
        for half in range(2):
            lanes = slice(half * CH, half * CH + CH)
            a0 = s0[pl.ds(t, BLK), :, lanes].reshape(PX, CH)
            a1 = s1[pl.ds(t, BLK), :, lanes].reshape(PX, CH)
            b0 = g0[pl.ds(t, BLK), half].reshape(PX, CH)
            b1 = g1[pl.ds(t, BLK), half].reshape(PX, CH)
            a1 = jnp.where(keep0, a1, jnp.zeros_like(a1))
            b1 = jnp.where(keep1, b1, jnp.zeros_like(b1))
            tacc[...] += dot_t(jnp.concatenate([a0, a1], -1), jnp.concatenate([b0, b1], -1))

    before, after0, after1, after2 = (info[k] == 1 for k in range(1, 5))

    fill_act(wide, xh_ref)
    conv_to(sh_ref, wide, w_ref)
    masked(2, jnp.logical_and(before, after0))

    def from_halo(n, _):
        t = n * BLK
        add_spatial(dot(pair(gsel, t), vw[2]), t)
        add_temporal(s_ref.at[0], sh_ref, g_ref.at[0], gsel, before, after0, t)
        return 0

    lax.fori_loop(0, NBLK, from_halo, 0)

    fill_act(wide, x_ref.at[0])
    masked(1, after0)
    masked(2, jnp.logical_and(two, after1))

    def from_first(n, _):
        t = n * BLK
        value = dot(pair(g_ref.at[0], t), tw_ref[0]) + dot(pair(gsel, t), vw[1]) + dot(pair(gn_ref, t), vw[2])
        add_spatial(value, t)
        return 0

    lax.fori_loop(0, NBLK, from_first, 0)

    @pl.when(two)
    def _():
        fill_act(wide, x_ref.at[1])
        masked(1, after2)

        def from_second(n, _):
            t = n * BLK
            value = dot(pair(g_ref.at[1], t), tw_ref[0]) + dot(pair(gn_ref, t), vw[1])
            add_spatial(value, t)
            add_temporal(s_ref.at[1], s_ref.at[0], g_ref.at[1], gn_ref, after0, after2, t)
            return 0

        lax.fori_loop(0, NBLK, from_second, 0)

    for p in range(3):
        for q in range(3):
            first = (p * 3 + q) * CH
            second = ((p + 1) * 3 + q) * CH
            both = acc[0:CH, first : first + CH] + acc[CH : 2 * CH, second : second + CH]
            out_ref[p * 3 + q] = both.T * scale
    out_ref[9] = tacc[0:CH, 0:CH] * scale
    out_ref[10] = tacc[0:CH, CH : 2 * CH] * scale
    out_ref[11] = tacc[CH : 2 * CH, CH : 2 * CH] * scale


def output_kernel(info, x_ref, s_ref, sh_ref, xh_ref, w_ref, tw_ref, out_ref, wide, s2, mw):
    fill_act(wide, xh_ref)
    conv_to(s2, wide, w_ref)

    def slot(j, here, back1, back2, keep1, keep2):
        mw[0] = jnp.where(keep1, tw_ref[1], jnp.zeros_like(tw_ref[1]))
        mw[1] = jnp.where(keep2, tw_ref[2], jnp.zeros_like(tw_ref[2]))

        def body(n, _):
            t = n * BLK
            value = dot(flat(here, t), tw_ref[0]) + dot(flat(back1, t), mw[0]) + dot(flat(back2, t), mw[1])
            value = value.astype(BF16).astype(F32).reshape(BLK, COLS, 2 * CH)
            for half in range(2):
                wide_x = x_ref[j, pl.ds(t, BLK), half].astype(F32)
                out_ref[j, pl.ds(t, BLK), half] = (wide_x + value[:, :, half * CH : half * CH + CH]).astype(BF16)
            return 0

        lax.fori_loop(0, NBLK, body, 0)

    slot(0, s_ref.at[0], sh_ref, s2, info[1] == 1, info[2] == 1)

    @pl.when(info[0] == 2)
    def _():
        slot(1, s_ref.at[1], s_ref.at[0], sh_ref, info[3] == 1, info[4] == 1)

    @pl.when(info[0] != 2)
    def _():
        out_ref[1] = jnp.zeros_like(out_ref[1])


def input_kernel(info, x_ref, g_ref, gn_ref, gnn_ref, w_ref, tw_ref, out_ref, wide, mw):
    two = info[0] == 2

    def slot(j, next1, next2, keep1, keep2):
        mw[0] = jnp.where(keep1, tw_ref[1], jnp.zeros_like(tw_ref[1]))
        mw[1] = jnp.where(keep2, tw_ref[2], jnp.zeros_like(tw_ref[2]))
        clear_edges(wide)

        def up(n, _):
            t = n * BLK
            value = dot(pair(g_ref.at[j], t), tw_ref[0]) + dot(next1(t), mw[0]) + dot(next2(t), mw[1])
            value = value.reshape(BLK, COLS, 2 * CH)
            for half in range(2):
                put_row(wide, t, half, value[:, :, half * CH : half * CH + CH])
            return 0

        lax.fori_loop(0, NBLK, up, 0)

        def down(n, _):
            t = n * BLK
            back = conv(wide, w_ref, t).reshape(BLK, COLS, 2 * CH)
            for half in range(2):
                x = x_ref[j, pl.ds(t, BLK), half].astype(F32)
                g = g_ref[j, pl.ds(t, BLK), half].astype(F32)
                sig = jax.nn.sigmoid(x)
                b = back[:, :, half * CH : half * CH + CH]
                out_ref[j, pl.ds(t, BLK), half] = (g + b * (sig * (1.0 + x * (1.0 - sig)))).astype(BF16)
            return 0

        lax.fori_loop(0, NBLK, down, 0)

    slot(
        0,
        lambda t: jnp.where(two, pair(g_ref.at[1], t), pair(gn_ref, t)),
        lambda t: jnp.where(two, pair(gn_ref, t), pair(gnn_ref, t)),
        info[1] == 1,
        info[2] == 1,
    )

    @pl.when(two)
    def _():
        slot(1, lambda t: pair(gn_ref, t), lambda t: pair(gnn_ref, t), info[3] == 1, info[4] == 1)

    @pl.when(info[0] != 2)
    def _():
        out_ref[1] = jnp.zeros_like(out_ref[1])


WIDE = pltpu.VMEM((PAIRS + 1, COLS, 6 * CH), BF16)
SMEM = pl.BlockSpec(memory_space=pltpu.SMEM)
VMEM = pl.BlockSpec(memory_space=pltpu.VMEM)


def call(kernel, n_in, outs, scratch, name):
    return pl.pallas_call(
        kernel,
        in_specs=[SMEM] + [VMEM] * n_in,
        out_specs=[VMEM] * len(outs),
        out_shape=[jax.ShapeDtypeStruct(s, d) for s, d in outs],
        scratch_shapes=scratch,
        compiler_params=pltpu.CompilerParams(vmem_limit_bytes=VMEM_BYTES),
        name=name,
    )


S_SHAPE = (PAIRS, COLS, 2 * CH)


def forward(info, x, w):
    return call(forward_kernel, 2, [((2,) + S_SHAPE, BF16)], [WIDE], "forward")(info, x, w)[0]


def grads(info, x, g, xh, gn, s, w, tw, scale):
    scratch = [
        WIDE,
        pltpu.VMEM((PAIRS, 2, COLS, CH), BF16),
        pltpu.VMEM((3, 2 * CH, 2 * CH), BF16),
        pltpu.VMEM((2 * CH, 12 * CH), F32),
        pltpu.VMEM((2 * CH, 2 * CH), F32),
    ]
    outs = [((12, CH, CH), F32), (S_SHAPE, BF16)]
    return call(functools.partial(grad_kernel, scale=scale), 7, outs, scratch, "grads")(info, x, g, xh, gn, s, w, tw)


def output(info, x, s, sh, xh, w, tw):
    scratch = [WIDE, pltpu.VMEM(S_SHAPE, BF16), pltpu.VMEM((2, 2 * CH, 2 * CH), BF16)]
    return call(output_kernel, 6, [(frame_spec((2,)), BF16)], scratch, "output")(info, x, s, sh, xh, w, tw)[0]


def input_grads(info, x, g, gn, gnn, w, tw):
    scratch = [WIDE, pltpu.VMEM((2, 2 * CH, 2 * CH), BF16)]
    return call(input_kernel, 6, [(frame_spec((2,)), BF16)], scratch, "input_grads")(info, x, g, gn, gnn, w, tw)[0]


def pair_weight(w):
    zero = jnp.zeros((1, 3, CH, CH), w.dtype)
    first = jnp.concatenate([w, zero], 0).reshape(12 * CH, CH)
    second = jnp.concatenate([zero, w], 0).reshape(12 * CH, CH)
    return jnp.concatenate([first, second], 1)


def twice(w):
    zero = jnp.zeros_like(w)
    return jnp.concatenate([jnp.concatenate([w, zero], 2), jnp.concatenate([zero, w], 2)], 1)


def total(part, sp_count):
    core = lax.axis_index("dp")
    swap = [(0, 1), (1, 0)]
    halves = part.reshape(2, 6 * CH, CH)
    own = lax.dynamic_index_in_dim(halves, core, 0, keepdims=False)
    other = lax.dynamic_index_in_dim(halves, 1 - core, 0, keepdims=False)
    own = own + lax.ppermute(other, "dp", swap)
    rows = 6 * CH // sp_count
    pieces = lax.all_to_all(own.reshape(sp_count, rows, CH), "sp", 0, 0, tiled=True)
    piece = jnp.sum(pieces, axis=0)
    spread = lax.all_to_all(jnp.broadcast_to(piece[None], (sp_count, rows, CH)), "sp", 0, 0, tiled=True)
    mine = spread.reshape(6 * CH, CH)
    theirs = lax.ppermute(mine, "dp", swap)
    both = jnp.where(core == 0, jnp.stack([mine, theirs]), jnp.stack([theirs, mine]))
    return both.reshape(12, CH, CH)


def local(latents, cotangent, frame_counts, spatial_weight, temporal_weight):
    sp_count = lax.axis_size("sp")
    nframes = sp_count // 8 * FRAMES
    scale = float(lax.axis_size("dp") * nframes * ROWS * COLS) ** (-0.5)
    counts = frame_counts[0]
    here = lax.axis_index("sp")
    order = jnp.arange(sp_count, dtype=jnp.int32)
    count = jnp.sum(jnp.where(order == here, counts, 0))
    place = jnp.sum(jnp.where(order < here, counts, 0)) % FRAMES
    place1 = (place + 1) % FRAMES
    two = count == 2

    def flags(*conditions):
        return jnp.stack([count] + [c.astype(jnp.int32) for c in conditions])

    x = latents.reshape(2, PAIRS, 2, COLS, CH)
    g = cotangent.reshape(2, PAIRS, 2, COLS, CH)
    low = [(i, i + 1) for i in range(0, sp_count, 2)] + [(i + 1, i) for i in range(0, sp_count, 2)]
    high = [(i, (i + 1) % sp_count) for i in range(1, sp_count, 2)] + [((i + 1) % sp_count, i) for i in range(1, sp_count, 2)]
    even = here % 2 == 0

    def exchange(up, down):
        from_high = lax.ppermute(jnp.where(even, down, up), "sp", high)
        from_low = lax.ppermute(jnp.where(even, up, down), "sp", low)
        return jnp.where(even, from_high, from_low), jnp.where(even, from_low, from_high)

    x_last = jnp.where(two, x[1], x[0])
    xh, gn = exchange(x_last, g[0])
    xhh, gnn = exchange(jnp.where(two, x[0], xh), jnp.where(two, g[1], gn))

    w_fwd = pair_weight(spatial_weight)
    w_bwd = pair_weight(jnp.transpose(spatial_weight[::-1, ::-1], (0, 1, 3, 2)))
    tw_fwd = twice(temporal_weight)
    tw_bwd = twice(jnp.swapaxes(temporal_weight, 1, 2))

    s = forward(flags(), x, w_fwd)
    last = FRAMES - 1
    part, sh = grads(
        flags(place >= 1, place + 1 <= last, place + 2 <= last, place1 + 1 <= last),
        x, g, xh, gn, s, w_fwd, tw_bwd, scale,
    )
    summed = total(part, sp_count)
    block_out = output(flags(place >= 1, place >= 2, place1 >= 1, place1 >= 2), x, s, sh, xhh, w_fwd, tw_fwd)
    input_grad = input_grads(
        flags(place + 1 <= last, place + 2 <= last, place1 + 1 <= last, place1 + 2 <= last),
        x, g, gn, gnn, w_bwd, tw_bwd,
    )
    return (
        block_out.reshape(latents.shape),
        input_grad.reshape(latents.shape),
        summed[:9].reshape(3, 3, CH, CH),
        summed[9:],
    )


def solution(mesh):
    return jax.shard_map(
        local,
        mesh=mesh,
        in_specs=(
            P(("dp", "sp"), None, None, None),
            P(("dp", "sp"), None, None, None),
            P("dp", None),
            P(),
            P(),
        ),
        out_specs=(P(("dp", "sp"), None, None, None), P(("dp", "sp"), None, None, None), P(), P()),
        check_vma=False,
    )
```

time: 365 us -> 154 us (0.42)
  waiting for transfers between devices: 167 us -> 24.4 us
  matrix products: 96.8 us -> 0 us
  Pallas kernels: 0 us -> 35.3 us
  blocking collectives: 0 us -> 31.7 us
  local copies, waits for them, and re-layouts: 28.5 us -> 15.4 us
  between operations: 14.6 us -> 2.18 us
  starting transfers between devices: 39.2 us -> 32.4 us
    psum x1 -> x0, waiting for transfers between devices: 128 us -> none  [local(): lax.psum((spatial_sum * scale, temporal_sum * scale), ('dp', 'sp'))]
    dot_general x36 -> x0, matrix products: 96.8 us -> none  [the longest x18 62.8 us: spatial_apply(): jnp.einsum('fhwc,cd->fhwd', window, kernel[row_tap, col_tap], preferred_e...]
    pallas_call x0 -> x4, Pallas kernels: none -> 35.3 us  [the longest x1 16.5 us: grads(): call(functools.partial(grad_kernel, scale=scale), 7, outs, scratch, 'grads')]
    all_to_all x0 -> x1, blocking collectives: none -> 31.7 us  [total(): lax.all_to_all(own.reshape(sp_count, rows, CH), 'sp', 0, 0, tiled=True)]
    all_to_all x4 -> x1, waiting for transfers between devices: 39.7 us -> 9.02 us  [total(): lax.all_to_all(jnp.broadcast_to(piece[None], (sp_count, rows, CH)), 'sp',...]
    all_to_all x4 -> x1, starting transfers between devices: 38.9 us -> 8.9 us  [total(): lax.all_to_all(jnp.broadcast_to(piece[None], (sp_count, rows, CH)), 'sp',...]
    ppermute x0 -> x6, starting transfers between devices: none -> 23.5 us  [the longest x2 20 us: exchange(): from_high = lax.ppermute(jnp.where(even, down, up), 'sp', high)]
    ppermute x0 -> x6, waiting for transfers between devices: none -> 15.4 us  [the longest x2 14.6 us: exchange(): from_high = lax.ppermute(jnp.where(even, down, up), 'sp', high)]
  transfers between devices with their start and end apart: 5 -> 7, of which waited for: 3 -> 3; matrix products, arithmetic and copies ran while one was open for 30% -> 8% of each run, Pallas kernels for 0% -> 12%
where the time goes in v1:
time: 154 us; the launch traced here: 155 us
  Pallas kernels  35.3 us (23%)
  starting transfers between devices  32.4 us (21%)
  blocking collectives  31.7 us (21%)
  waiting for transfers between devices  24.4 us (16%)
  local copies, waits for them, and re-layouts  15.4 us (10%)
  other arithmetic  13.2 us (9%)
  between operations  2.18 us (1%)
    all_to_all x1, blocking collectives, total(): lax.all_to_all(own.reshape(sp_count, rows, CH), 'sp', 0, 0, tiled=True)  31.7 us
    ppermute x2, starting transfers between devices, exchange(): from_high = lax.ppermute(jnp.where(even, down, up), 'sp', high)  20 us
    pallas_call x1, Pallas kernels, grads(): call(functools.partial(grad_kernel, scale=scale), 7, outs, scratch, 'grads')  16.5 us
    ppermute x2, waiting for transfers between devices, exchange(): from_high = lax.ppermute(jnp.where(even, down, up), 'sp', high)  14.6 us
    all_to_all x1, waiting for transfers between devices, total(): lax.all_to_all(jnp.broadcast_to(piece[None], (sp_count, rows, CH)), 'sp',...  9.02 us
    all_to_all x1, starting transfers between devices, total(): lax.all_to_all(jnp.broadcast_to(piece[None], (sp_count, rows, CH)), 'sp',...  8.9 us
    pallas_call x1, Pallas kernels, output(): call(output_kernel, 6, [(frame_spec((2,)), BF16)], scratch, 'output')  7.83 us
    pallas_call x1, Pallas kernels, input_grads(): call(input_kernel, 6, [(frame_spec((2,)), BF16)], scratch, 'input_grads')  7.14 us
  transfers between devices with their start and end apart: 7, of which 3 were waited for; matrix products, arithmetic and copies ran while one was open for 8% of the time, Pallas kernels for 12%

profile of v1, /device:TPU:1, one launch (start us, length us, event | category | flops | bytes accessed | tf_op | source)
XLA Modules:
  0.0 154.5 jit_solution(11645672124986914644)
XLA Ops:
  0.6 1.4 fusion.7
  2.6 1.9 %fusion.8 = (bf16[1,64,64,128]{3,2,1,0:T(8,128)(2,1)S(1)}, bf16[1,64,64,128]{3,2,1,0:T(8,128)(2,1)S(1)}) fusion(bf16[2,64,64,128]{3,2,1,0:T(8,128)(2,1)} %param.5), kind=kLoop, calls=%fused_computation.29 | loop fusion | bytes 4194304 | tf_op jit(solution)/shard_map/slice | solution.py:367
  4.9 1.3 fusion.9
  6.2 1.5 broadcast_select_fusion.10
  7.7 9.2 %collective-permute-start = (bf16[32,2,64,128]{3,2,1,0:T(8,128)(2,1)}, bf16[32,2,64,128]{3,2,1,0:T(8,128)(2,1)}, u32[]{:S(2)}, u32[]{:S(2)}) collective-permute-start(bf16[32,2,64,128]{3,2,1,0:T(8,128)(2,1)} %get-tuple-element.13), channel_id=1, source_target_pairs={{1,2},{3,4},{5,6},{7,8},{9,10},{11,12},{13,14},{15,16},{17,18},{19... | collective-permute-start | bytes 3145736 | tf_op jit(solution)/shard_map/ppermute | solution.py:363
  18.1 1.1 fusion.10
  19.7 3.8 %forward.1.s_ref = bf16[2,32,64,256]{3,2,1,0:T(8,128)(2,1)S(1)} custom-call(s32[1]{0:T(128)} %bitcast.1.info, bf16[2,32,2,64,128]{4,3,2,1,0:T(8,128)(2,1)S(1)} %bitcast.36, bf16[1536,256]{1,0:T(8,128)(2,1)S(1)} %pad_maximum_fusion.w_ref), custom_call_target="tpu_custom_call" | custom-call | tf_op jit(solution)/shard_map/forward/pallas_call | solution.py:287
  23.5 1.3 copy-done.2
  25.6 14.6 %collective-permute-done = bf16[32,2,64,128]{3,2,1,0:T(8,128)(2,1)} collective-permute-done((bf16[32,2,64,128]{3,2,1,0:T(8,128)(2,1)}, bf16[32,2,64,128]{3,2,1,0:T(8,128)(2,1)}, u32[]{:S(2)}, u32[]{:S(2)}) %collective-permute-start) | collective-permute-done | bytes 1048608 | tf_op jit(solution)/shard_map/ppermute | solution.py:363
  40.1 0.8 collective-permute-done.1
  41.0 2.8 %broadcast_select_fusion.5 = (bf16[32,2,64,128]{3,2,1,0:T(8,128)(2,1)}, bf16[32,2,64,128]{3,2,1,0:T(8,128)(2,1)S(1)}, bf16[32,2,64,128]{3,2,1,0:T(8,128)(2,1)S(1)}) fusion(pred[]{:T(512)S(6)} %eq.21, bf16[32,2,64,128]{3,2,1,0:T(8,128)(2,1)} %bitcast.46, pred[]{:T(512)S(6)} %eq.22, bf16[32,2,64,128]{3,2,1,0:T(8,128)(2,1)} %bitcast.44, ...), kind=kLoop, calls=%fused_computation.5 | loop fusion | flops 2621440 | bytes 7340034 | tf_op jit(solution)/shard_map/jit(_where)/select_n | solution.py:364
  43.7 16.5 %grads.1 = (f32[12,128,128]{2,1,0:T(8,128)S(1)}, bf16[32,64,256]{2,1,0:T(8,128)(2,1)S(1)}) custom-call(s32[5]{0:T(128)S(1)} %stack.93.info, bf16[2,32,2,64,128]{4,3,2,1,0:T(8,128)(2,1)} %bitcast.35, bf16[2,32,2,64,128]{4,3,2,1,0:T(8,128)(2,1)} %bitcast.41, bf16[32,2,64,128]{3,2,1,0:T(8,128)(2,1)S(1)} %get-tuple-element.12.xh_ref, ...), custom_call_target="tpu_custom_call" | custom-call | tf_op jit(solution)/shard_map/grads/pallas_call | solution.py:299
  60.2 1.0 copy-done.4
  61.2 0.9 copy-done.6
  62.1 0.8 dynamic-slice_bitcast_fusion
  62.9 1.9 %collective-permute-start.4 = (f32[768,128]{1,0:T(8,128)}, f32[768,128]{1,0:T(8,128)}, u32[]{:S(2)}, u32[]{:S(2)}) collective-permute-start(f32[768,128]{1,0:T(8,128)} %dynamic-slice_bitcast_fusion), channel_id=1, source_target_pairs={{0,64},{64,0},{1,65},{65,1},{2,66},{66,2},{3,67},{67,3},{4,68},{68... | collective-permute-start | bytes 1179656 | tf_op jit(solution)/shard_map/ppermute | solution.py:330
  64.7 1.2 broadcast_select_fusion.6
  65.9 10.8 %collective-permute-start.2 = (bf16[32,2,64,128]{3,2,1,0:T(8,128)(2,1)}, bf16[32,2,64,128]{3,2,1,0:T(8,128)(2,1)}, u32[]{:S(2)}, u32[]{:S(2)}) collective-permute-start(bf16[32,2,64,128]{3,2,1,0:T(8,128)(2,1)} %broadcast_select_fusion.6), channel_id=1, source_target_pairs={{1,2},{3,4},{5,6},{7,8},{9,10},{11,12},{13,14},{15,16},{17,18},{19... | collective-permute-start | bytes 3145736 | tf_op jit(solution)/shard_map/ppermute | solution.py:363
  76.7 1.0 bitcast_add_fusion
  77.8 31.7 %all_to_all.10 = f32[64,12,128]{2,1,0:T(8,128)S(1)} all-to-all(f32[64,12,128]{2,1,0:T(8,128)S(1)} %reshape.67), channel_id=1, replica_groups=mesh['dp'=2,'sp'=64] {'sp'}, dimensions={0} | all-to-all | bytes 786432 | tf_op jit(solution)/shard_map/all_to_all | solution.py:332
  109.6 0.8 broadcast_in_dim.12
  110.5 8.9 %all-to-all-start.1 = ((f32[64,12,128]{2,1,0:T(8,128)}), f32[64,12,128]{2,1,0:T(8,128)S(1)}, u32[]{:S(2)}, u32[]{:S(2)}) async-start(f32[64,12,128]{2,1,0:T(8,128)} %broadcast_in_dim.12), calls=%async_computation.1 | async-start | bytes 1048576 | tf_op jit(solution)/shard_map/all_to_all | solution.py:334
  119.4 0.7 stack.96.info
  120.8 2.1 %pad_maximum_fusion.1.w_ref = bf16[1536,256]{1,0:T(8,128)(2,1)} fusion(bf16[1536,128]{1,0:T(8,128)(2,1)} %bitcast.55, bf16[1536,128]{1,0:T(8,128)(2,1)} %bitcast.54), kind=kLoop, calls=%fused_computation.18 | loop fusion | flops 1572864 | bytes 1572864 | tf_op jit(solution)/shard_map/concatenate | solution.py:316
  122.9 9.0 %all-to-all-done.1 = f32[64,12,128]{2,1,0:T(8,128)S(1)} async-done(((f32[64,12,128]{2,1,0:T(8,128)}), f32[64,12,128]{2,1,0:T(8,128)S(1)}, u32[]{:S(2)}, u32[]{:S(2)}) %all-to-all-start.1) | async-done | bytes 393248 | tf_op jit(solution)/shard_map/all_to_all | solution.py:334
  131.9 0.8 reshape.68
  132.7 1.5 collective-permute-start.5
  134.4 1.8 %broadcast_select_fusion.3 = (bf16[32,2,64,128]{3,2,1,0:T(8,128)(2,1)S(1)}, bf16[32,2,64,128]{3,2,1,0:T(8,128)(2,1)S(1)}) fusion(bf16[32,2,64,128]{3,2,1,0:T(8,128)(2,1)} %collective-permute-done.3, bf16[32,2,64,128]{3,2,1,0:T(8,128)(2,1)} %collective-permute-done.2, pred[]{:T(512)S(6)} %eq.21), kind=kLoop, calls=%fused_computation.3 | loop fusion | flops 1048576 | bytes 4194305 | tf_op jit(solution)/shard_map/jit(_where)/select_n | solution.py:365
  136.7 7.1 %input_grads.1 = bf16[2,32,2,64,128]{4,3,2,1,0:T(8,128)(2,1)} custom-call(s32[5]{0:T(128)S(1)} %stack.96.info, bf16[2,32,2,64,128]{4,3,2,1,0:T(8,128)(2,1)S(1)} %bitcast.37, bf16[2,32,2,64,128]{4,3,2,1,0:T(8,128)(2,1)} %bitcast.42, bf16[32,2,64,128]{3,2,1,0:T(8,128)(2,1)S(1)} %get-tuple-element.11.gn_ref, ...), custom_call_target="tpu_custom_call" | custom-call | tf_op jit(solution)/shard_map/input_grads/pallas_call | solution.py:309
  143.9 7.8 %output.1 = bf16[2,32,2,64,128]{4,3,2,1,0:T(8,128)(2,1)} custom-call(s32[5]{0:T(128)S(1)} %stack.86.info, bf16[2,32,2,64,128]{4,3,2,1,0:T(8,128)(2,1)S(1)} %bitcast.38, bf16[2,32,64,256]{3,2,1,0:T(8,128)(2,1)} %copy-done.2, bf16[32,64,256]{2,1,0:T(8,128)(2,1)S(1)} %copy-done.5, bf16[32,2,64,128]{3,2,1,0:T(8,128)(2,1)S(1)} %get-tuple-element.16.xh_ref, ...), custom_call_target="tpu_custom_call" | custom-call | tf_op jit(solution)/shard_map/output/pallas_call | solution.py:304
  151.8 1.2 maximum_select_fusion
  153.7 0.9 slice.29
  (43 shorter events, 4.1 us)
Async XLA Ops:
  2.6 2.2 %copy-start.8 = (bf16[2,64,64,128]{3,2,1,0:T(8,128)(2,1)S(1)}, bf16[2,64,64,128]{3,2,1,0:T(8,128)(2,1)}, u32[]{:S(2)}) copy-start(bf16[2,64,64,128]{3,2,1,0:T(8,128)(2,1)} %param.6) | copy-start | bytes 6291460
  4.9 1.3 copy-start.9
  6.2 11.5 %copy-start.13 = (bf16[3,128,128]{2,1,0:T(8,128)(2,1)S(1)}, bf16[3,128,128]{2,1,0:T(8,128)(2,1)}, u32[]{:S(2)}) copy-start(bf16[3,128,128]{2,1,0:T(8,128)(2,1)} %param.9) | copy-start | bytes 294916
  6.2 11.6 %copy-start.12 = (bf16[3,3,128,128]{3,2,1,0:T(8,128)(2,1)S(1)}, bf16[3,3,128,128]{3,2,1,0:T(8,128)(2,1)}, u32[]{:S(2)}) copy-start(bf16[3,3,128,128]{3,2,1,0:T(8,128)(2,1)} %param.8) | copy-start | bytes 884740
  7.7 32.4 %collective-permute-start = (bf16[32,2,64,128]{3,2,1,0:T(8,128)(2,1)}, bf16[32,2,64,128]{3,2,1,0:T(8,128)(2,1)}, u32[]{:S(2)}, u32[]{:S(2)}) collective-permute-start(bf16[32,2,64,128]{3,2,1,0:T(8,128)(2,1)} %get-tuple-element.13), channel_id=1, source_target_pairs={{1,2},{3,4},{5,6},{7,8},{9,10},{11,12},{13,14},{15,16},{17,18},{19... | collective-permute-start | bytes 3145736 | tf_op jit(solution)/shard_map/ppermute | solution.py:363
  16.9 24.0 %collective-permute-start.1 = (bf16[32,2,64,128]{3,2,1,0:T(8,128)(2,1)}, bf16[32,2,64,128]{3,2,1,0:T(8,128)(2,1)}, u32[]{:S(2)}, u32[]{:S(2)}) collective-permute-start(bf16[32,2,64,128]{3,2,1,0:T(8,128)(2,1)} %get-tuple-element.14), channel_id=1, source_target_pairs={{0,1},{2,3},{4,5},{6,7},{8,9},{10,11},{12,13},{14,15},{16,17},{18,... | collective-permute-start | bytes 3145736 | tf_op jit(solution)/shard_map/ppermute | solution.py:364
  17.8 1.9 %copy-start = (bf16[2,64,64,128]{3,2,1,0:T(8,128)(2,1)S(1)}, bf16[2,64,64,128]{3,2,1,0:T(8,128)(2,1)}, u32[]{:S(2)}) copy-start(bf16[2,64,64,128]{3,2,1,0:T(8,128)(2,1)} %param.5) | copy-start | bytes 6291460
  23.5 1.3 copy-start.2
  60.2 1.0 copy-start.4
  61.2 0.9 copy-start.6
  62.9 13.8 %collective-permute-start.4 = (f32[768,128]{1,0:T(8,128)}, f32[768,128]{1,0:T(8,128)}, u32[]{:S(2)}, u32[]{:S(2)}) collective-permute-start(f32[768,128]{1,0:T(8,128)} %dynamic-slice_bitcast_fusion), channel_id=1, source_target_pairs={{0,64},{64,0},{1,65},{65,1},{2,66},{66,2},{3,67},{67,3},{4,68},{68... | collective-permute-start | bytes 1179656 | tf_op jit(solution)/shard_map/ppermute | solution.py:330
  64.7 12.0 %copy-start.7 = (f32[12,128,128]{2,1,0:T(8,128)S(1)}, f32[12,128,128]{2,1,0:T(8,128)}, u32[]{:S(2)}) copy-start(f32[12,128,128]{2,1,0:T(8,128)} %copy-done.6) | copy-start | bytes 2359300
  64.7 69.6 %collective-permute-start.3 = (bf16[32,2,64,128]{3,2,1,0:T(8,128)(2,1)}, bf16[32,2,64,128]{3,2,1,0:T(8,128)(2,1)}, u32[]{:S(2)}, u32[]{:S(2)}) collective-permute-start(bf16[32,2,64,128]{3,2,1,0:T(8,128)(2,1)} %get-tuple-element.10), channel_id=1, source_target_pairs={{0,1},{2,3},{4,5},{6,7},{8,9},{10,11},{12,13},{14,15},{16,17},{18,... | collective-permute-start | bytes 3145736 | tf_op jit(solution)/shard_map/ppermute | solution.py:364
  65.9 68.5 %collective-permute-start.2 = (bf16[32,2,64,128]{3,2,1,0:T(8,128)(2,1)}, bf16[32,2,64,128]{3,2,1,0:T(8,128)(2,1)}, u32[]{:S(2)}, u32[]{:S(2)}) collective-permute-start(bf16[32,2,64,128]{3,2,1,0:T(8,128)(2,1)} %broadcast_select_fusion.6), channel_id=1, source_target_pairs={{1,2},{3,4},{5,6},{7,8},{9,10},{11,12},{13,14},{15,16},{17,18},{19... | collective-permute-start | bytes 3145736 | tf_op jit(solution)/shard_map/ppermute | solution.py:363
  110.5 21.4 %all-to-all-start.1 = ((f32[64,12,128]{2,1,0:T(8,128)}), f32[64,12,128]{2,1,0:T(8,128)S(1)}, u32[]{:S(2)}, u32[]{:S(2)}) async-start(f32[64,12,128]{2,1,0:T(8,128)} %broadcast_in_dim.12), calls=%async_computation.1 | async-start | bytes 1048576 | tf_op jit(solution)/shard_map/all_to_all | solution.py:334
  131.9 2.5 %copy-start.10 = (f32[64,12,128]{2,1,0:T(8,128)}, f32[64,12,128]{2,1,0:T(8,128)S(1)}, u32[]{:S(2)}) copy-start(f32[64,12,128]{2,1,0:T(8,128)S(1)} %all-to-all-done.1) | copy-start | bytes 1179652
  132.7 19.0 %collective-permute-start.5 = (f32[768,128]{1,0:T(8,128)}, f32[768,128]{1,0:T(8,128)}, u32[]{:S(2)}, u32[]{:S(2)}) collective-permute-start(f32[768,128]{1,0:T(8,128)} %reshape.68), channel_id=1, source_target_pairs={{0,64},{64,0},{1,65},{65,1},{2,66},{66,2},{3,67},{67,3},{4,68},{68... | collective-permute-start | bytes 1179656 | tf_op jit(solution)/shard_map/ppermute | solution.py:336
  134.3 2.2 %copy-start.1 = (bf16[2,64,64,128]{3,2,1,0:T(8,128)(2,1)S(1)}, bf16[2,64,64,128]{3,2,1,0:T(8,128)(2,1)}, u32[]{:S(2)}) copy-start(bf16[2,64,64,128]{3,2,1,0:T(8,128)(2,1)} %param.5) | copy-start | bytes 6291460
  134.3 2.4 %copy-start.3 = (bf16[1536,256]{1,0:T(8,128)(2,1)S(1)}, bf16[1536,256]{1,0:T(8,128)(2,1)}, u32[]{:S(2)}) copy-start(bf16[1536,256]{1,0:T(8,128)(2,1)} %pad_maximum_fusion.1.w_ref) | copy-start | bytes 2359300
  136.7 7.1 %copy-start.5 = (bf16[32,64,256]{2,1,0:T(8,128)(2,1)S(1)}, bf16[32,64,256]{2,1,0:T(8,128)(2,1)}, u32[]{:S(2)}) copy-start(bf16[32,64,256]{2,1,0:T(8,128)(2,1)} %copy-done.4) | copy-start | bytes 3145732
  143.9 7.8 %copy-start.11 = (f32[64,12,128]{2,1,0:T(8,128)S(1)}, f32[64,12,128]{2,1,0:T(8,128)}, u32[]{:S(2)}) copy-start(f32[64,12,128]{2,1,0:T(8,128)} %copy-done.10) | copy-start | bytes 1179652

commit v2 on v0

v2 whole, which is shorter than its diff:
```python
import functools

import jax
import jax.numpy as jnp
from jax import lax
from jax.experimental import pallas as pl
from jax.experimental.pallas import tpu as pltpu
from jax.sharding import Mesh
from jax.sharding import PartitionSpec as P

FRAMES = 9
CLIPS = 8
CH = 128
ROWS = 64
COLS = 64
N_SP = 64
SIDE = 4
PAIRS = ROWS // 2
F32 = jnp.float32
BF16 = jnp.bfloat16
VMEM_BYTES = 32 * 1024 * 1024
SCALE = float(2 * CLIPS * FRAMES * ROWS * COLS) ** (-0.5)
HALF = 6 * CH
PIECE = HALF // (SIDE * SIDE)

COUNT, EVEN, BACK1, BACK2, NEXT1, NEXT2, LBACK1, LBACK2, LNEXT1, LNEXT2, CORE, AT_X, AT_Y = range(13)
INFO = 16

FILL = 8
MID = 16
FULL = 32


def dot(a, b):
    return jnp.dot(a, b, preferred_element_type=F32)


def dot_t(a, b):
    return lax.dot_general(a, b, (((0,), (0,)), ((), ())), preferred_element_type=F32)


def steps(block, body):
    def one(n, _):
        body(n * block)
        return 0

    lax.fori_loop(0, PAIRS // block, one, 0)


def clear_edges(wide):
    wide[0, :, 0 : 3 * CH] = jnp.zeros((COLS, 3 * CH), BF16)
    wide[PAIRS, :, 3 * CH : 6 * CH] = jnp.zeros((COLS, 3 * CH), BF16)


def put_row(wide, t, half, a):
    col = lax.broadcasted_iota(jnp.int32, a.shape, 1)
    before = jnp.where(col == 0, 0.0, pltpu.roll(a, 1, 1))
    after = jnp.where(col == COLS - 1, 0.0, pltpu.roll(a, COLS - 1, 1))
    at = pl.ds(t + half, a.shape[0])
    base = 0 if half else 3 * CH
    wide[at, :, base : base + CH] = before.astype(BF16)
    wide[at, :, base + CH : base + 2 * CH] = a.astype(BF16)
    wide[at, :, base + 2 * CH : base + 3 * CH] = after.astype(BF16)


def fill_act(wide, rows):
    def body(t):
        for half in range(2):
            x = rows(t, half).astype(F32)
            put_row(wide, t, half, x * jax.nn.sigmoid(x))

    steps(FILL, body)


def windows(wide, t, block):
    low = wide[pl.ds(t, block)].reshape(block * COLS, 6 * CH)
    high = wide[pl.ds(t + 1, block)].reshape(block * COLS, 6 * CH)
    return low, high


def conv(wide, w_ref, t, block):
    low, high = windows(wide, t, block)
    return dot(low, w_ref[0 : 6 * CH, :]) + dot(high, w_ref[6 * CH : 12 * CH, :])


def conv_to(out_ref, wide, w_ref):
    def body(t):
        out_ref[pl.ds(t, FULL)] = conv(wide, w_ref, t, FULL).astype(BF16).reshape(FULL, COLS, 2 * CH)

    steps(FULL, body)


def pair(v):
    return jnp.concatenate([v[:, 0], v[:, 1]], axis=-1).reshape(v.shape[0] * COLS, 2 * CH)


def flat(v):
    return v.reshape(v.shape[0] * COLS, 2 * CH)


def add_spatial(acc, wide, v_ref):
    def body(t):
        low, high = windows(wide, t, FULL)
        v = flat(v_ref[pl.ds(t, FULL)])
        acc[:, 0 : 6 * CH] += dot_t(v, low)
        acc[:, 6 * CH : 12 * CH] += dot_t(v, high)

    steps(FULL, body)


def correlate(s, gs):
    total = None
    for half in range(2):
        a = s[:, :, half * CH : half * CH + CH].reshape(PAIRS * COLS, CH)
        b = gs(half)
        one = dot_t(a, b.reshape(PAIRS * COLS, b.shape[-1]))
        total = one if total is None else total + one
    return total


def begin(copies, sems):
    found = [pltpu.make_async_copy(a, b, sems.at[n]) for n, (a, b) in enumerate(copies)]
    for c in found:
        c.start()
    return found


def begin_either(first, a, b, target, sem):
    @pl.when(first)
    def _():
        pltpu.make_async_copy(a, target, sem).start()

    @pl.when(jnp.logical_not(first))
    def _():
        pltpu.make_async_copy(b, target, sem).start()

    return pltpu.make_async_copy(a, target, sem)


def prep_kernel(counts, place, x_ref, g_ref, info, high_ref, low_ref, sems):
    here = place[0]

    def add(n, carry):
        total, own = carry
        c = counts[0, n]
        return total + jnp.where(n < here, c, 0), own + jnp.where(n == here, c, 0)

    start, count = lax.fori_loop(0, N_SP, add, (jnp.int32(0), jnp.int32(0)), unroll=8)
    first = start % FRAMES
    second = (first + 1) % FRAMES
    final = FRAMES - 1
    even = here % 2 == 0
    values = {
        COUNT: count,
        EVEN: even.astype(jnp.int32),
        BACK1: (first >= 1).astype(jnp.int32),
        BACK2: (first >= 2).astype(jnp.int32),
        NEXT1: (first + 1 <= final).astype(jnp.int32),
        NEXT2: (first + 2 <= final).astype(jnp.int32),
        LBACK1: (second >= 1).astype(jnp.int32),
        LBACK2: (second >= 2).astype(jnp.int32),
        LNEXT1: (second + 1 <= final).astype(jnp.int32),
        LNEXT2: (second + 2 <= final).astype(jnp.int32),
        CORE: place[1],
        AT_X: here // (SIDE * SIDE),
        AT_Y: (here // SIDE) % SIDE,
    }
    for at, value in values.items():
        info[at] = value
    for at in range(len(values), INFO):
        info[at] = 0
    last = jnp.where(count == 2, 1, 0)

    def send(up_ref, down_ref):
        up = pltpu.make_async_copy(x_ref.at[last], up_ref, sems.at[0])
        down = pltpu.make_async_copy(g_ref.at[0], down_ref, sems.at[1])
        up.start()
        down.start()
        up.wait()
        down.wait()

    @pl.when(even)
    def _():
        send(low_ref, high_ref)

    @pl.when(jnp.logical_not(even))
    def _():
        send(high_ref, low_ref)


def forward_kernel(
    info, x_any, g_any, w_any, tw_any, s_ref, acc, tacc, wf, wb, tf, tb, wide, v_ref, mw, x_ref, g_ref, w_ref, tw_ref, sems
):
    need_w, need_tw, need_x, need_g = begin([(w_any, w_ref), (tw_any, tw_ref), (x_any, x_ref), (g_any, g_ref)], sems)
    need_w.wait()
    need_tw.wait()
    zero = jnp.zeros((CH, CH), BF16)
    for a in range(4):
        for q in range(3):
            rows = slice((a * 3 + q) * CH, (a * 3 + q + 1) * CH)
            for b in range(2):
                lanes = slice(b * CH, b * CH + CH)
                inside = 0 <= a - b <= 2
                wf[rows, lanes] = w_ref[a - b, q] if inside else zero
                wb[rows, lanes] = w_ref[2 - (a - b), 2 - q].T if inside else zero
    for k in range(3):
        for a in range(2):
            rows = slice((2 * k + a) * CH, (2 * k + a + 1) * CH)
            for b in range(2):
                lanes = slice(b * CH, b * CH + CH)
                tf[rows, lanes] = tw_ref[k] if a == b else zero
                tb[rows, lanes] = tw_ref[k].T if a == b else zero

    acc[...] = jnp.zeros_like(acc)
    tacc[...] = jnp.zeros_like(tacc)
    clear_edges(wide)
    mw[0 : 2 * CH] = tb[0 : 2 * CH]
    need_x.wait()
    need_g.wait()

    def slot(j, _):
        keep = jnp.logical_and(j == 0, jnp.logical_and(info[COUNT] == 2, info[NEXT1] == 1))
        mw[2 * CH : 4 * CH] = jnp.where(keep, tb[2 * CH : 4 * CH], jnp.zeros((2 * CH, 2 * CH), BF16))
        fill_act(wide, lambda t, half: x_ref[j, pl.ds(t, FILL), half])
        conv_to(s_ref.at[j], wide, wf)

        def upstream(t):
            at = pl.ds(t, MID)
            both = jnp.concatenate([pair(g_ref[j, at]), pair(g_ref[1, at])], axis=-1)
            v_ref[at] = dot(both, mw[...]).astype(BF16).reshape(MID, COLS, 2 * CH)

        steps(MID, upstream)
        add_spatial(acc, wide, v_ref)
        found = correlate(s_ref[j], lambda half: jnp.concatenate([g_ref[j, :, half], g_ref[1, :, half]], axis=-1))
        tacc[:, 0:CH] += found[:, 0:CH]
        tacc[:, CH : 2 * CH] += jnp.where(keep, found[:, CH : 2 * CH], 0.0)
        return 0

    lax.fori_loop(0, info[COUNT], slot, 0)


def prep2_kernel(info, x_ref, g_ref, high_in, low_in, after, info_out, high_ref, low_ref, sems):
    for n in range(INFO):
        info_out[n] = info[n]
    two = info[COUNT] == 2
    even = info[EVEN] == 1

    def send(for_high, for_low):
        for c in begin([(for_high, high_ref), (for_low, low_ref)], sems):
            c.wait()

    @pl.when(jnp.logical_not(two))
    def _():
        send(low_in, high_in)

    @pl.when(jnp.logical_and(two, even))
    def _():
        send(g_ref.at[1], x_ref.at[0])

    @pl.when(jnp.logical_and(two, jnp.logical_not(even)))
    def _():
        send(x_ref.at[0], g_ref.at[1])


def grad_kernel(
    info, high_in, low_in, x_any, g_any, s_any, acc_any, tacc_any, wf_any, tb_any, own_ref, other_ref, sh_out,
    wide, xh, gn, x, g, s, v, sh, acc, tacc, wf, tb, mw, both, sems,
):
    two = info[COUNT] == 2
    even = info[EVEN] == 1
    back = info[BACK1] == 1
    cross = jnp.logical_and(back, info[NEXT1] == 1)
    need_x = begin_either(even, high_in, low_in, xh, sems.at[0])
    need = begin(
        [(wf_any, wf), (tb_any, tb), (g_any, g), (acc_any, acc), (tacc_any, tacc), (x_any.at[0], x), (s_any.at[0], s)],
        sems.at[pl.ds(2, 7)],
    )
    need_n = begin_either(even, low_in, high_in, gn, sems.at[1])
    clear_edges(wide)
    need_x.wait()
    fill_act(wide, lambda t, half: xh[pl.ds(t, FILL), half])
    need[0].wait()
    conv_to(sh, wide, wf)
    keep_sh = pltpu.make_async_copy(sh, sh_out, sems.at[9])
    keep_sh.start()
    for c in need[1:3] + [need_n]:
        c.wait()
    nothing = jnp.zeros((2 * CH, 2 * CH), BF16)
    mw[0 : 2 * CH] = jnp.where(back, tb[2 * CH : 4 * CH], nothing)
    mw[2 * CH : 4 * CH] = jnp.where(cross, tb[4 * CH : 6 * CH], nothing)

    def upstream(t):
        at = pl.ds(t, MID)
        u = jnp.concatenate([pair(g[0, at]), pair(jnp.where(two, g[1, at], gn[at]))], axis=-1)
        v[at] = dot(u, mw[...]).astype(BF16).reshape(MID, COLS, 2 * CH)

    steps(MID, upstream)
    for c in need[3:5]:
        c.wait()
    add_spatial(acc, wide, v)

    def two_frames(half):
        return jnp.concatenate([g[0, :, half], jnp.where(two, g[1, :, half], gn[:, half])], axis=-1)

    found = correlate(sh[...], two_frames)
    tacc[:, CH : 2 * CH] += jnp.where(back, found[:, 0:CH], 0.0)
    tacc[:, 2 * CH : 3 * CH] += jnp.where(cross, found[:, CH : 2 * CH], 0.0)
    for c in need[5:] + [keep_sh]:
        c.wait()

    @pl.when(jnp.logical_and(two, info[NEXT2] == 1))
    def _():
        fill_act(wide, lambda t, half: x[pl.ds(t, FILL), half])

        def up(t):
            at = pl.ds(t, MID)
            v[at] = dot(pair(gn[at]), tb[4 * CH : 6 * CH]).astype(BF16).reshape(MID, COLS, 2 * CH)

        steps(MID, up)
        add_spatial(acc, wide, v)
        tacc[:, 2 * CH : 3 * CH] += correlate(s[...], lambda half: gn[:, half])

    at_x, at_y, core = info[AT_X], info[AT_Y], info[CORE]
    for p in range(3):
        for q in range(3):
            first = (p * 3 + q) * CH
            second = ((p + 1) * 3 + q) * CH
            found = acc[0:CH, first : first + CH] + acc[CH : 2 * CH, second : second + CH]
            n = p * 3 + q
            both[n // 6, (n % 6) * CH : (n % 6 + 1) * CH] = found.T * SCALE
    for k in range(3):
        both[1, (3 + k) * CH : (4 + k) * CH] = tacc[:, k * CH : k * CH + CH] * SCALE
    for i in range(SIDE):
        for j in range(SIDE):
            piece = lax.rem(at_x + i, SIDE) * SIDE + lax.rem(at_y + j, SIDE)
            source = pl.ds(pl.multiple_of(piece * PIECE, PIECE), PIECE)
            own_ref[i, j] = both[core, source]
            other_ref[i, j] = both[1 - core, source]


def add_x(x, out, t, value):
    at = pl.ds(t, MID)
    value = value.astype(BF16).astype(F32).reshape(MID, COLS, 2 * CH)
    for half in range(2):
        out[at, half] = (x[at, half].astype(F32) + value[:, :, half * CH : half * CH + CH]).astype(BF16)


def mask_taps(mw, taps, keep1, keep2):
    nothing = jnp.zeros((2 * CH, 2 * CH), BF16)
    mw[0 : 2 * CH] = taps[0 : 2 * CH]
    mw[2 * CH : 4 * CH] = jnp.where(keep1, taps[2 * CH : 4 * CH], nothing)
    mw[4 * CH : 6 * CH] = jnp.where(keep2, taps[4 * CH : 6 * CH], nothing)


def input_rows(wide, wb, upstream, x, g, out, first, count):
    clear_edges(wide)

    def up(t, n):
        value = upstream(t, n).reshape(n, COLS, 2 * CH)
        for half in range(2):
            put_row(wide, t, half, value[:, :, half * CH : half * CH + CH])

    def up_full(n, _):
        up(first + n * FILL, FILL)
        return 0

    lax.fori_loop(0, count // FILL, up_full, 0)
    if first > 0:
        up(first - 1, 1)
    if first + count < PAIRS:
        up(first + count, 1)

    def down(n, _):
        t = first + n * MID
        at = pl.ds(t, MID)
        back = conv(wide, wb, t, MID).reshape(MID, COLS, 2 * CH)
        for half in range(2):
            xv = x[at, half].astype(F32)
            sig = jax.nn.sigmoid(xv)
            b = back[:, :, half * CH : half * CH + CH]
            out[at, half] = (g[at, half].astype(F32) + b * (sig * (1.0 + xv * (1.0 - sig)))).astype(BF16)
        return 0

    lax.fori_loop(0, count // MID, down, 0)


def early_out_kernel(info, x_any, s_any, sh_any, tf_any, after, out_any, token, x, s, sh, tf, mw, out, sems):
    @pl.when(info[COUNT] == 2)
    def _():
        for c in begin([(x_any.at[1], x), (s_any, s), (sh_any, sh), (tf_any, tf)], sems):
            c.wait()
        mask_taps(mw, tf, info[LBACK1] == 1, info[LBACK2] == 1)

        def body(t):
            at = pl.ds(t, MID)
            v = jnp.concatenate([flat(s[1, at]), flat(s[0, at]), flat(sh[at])], axis=-1)
            add_x(x, out, t, dot(v, mw[...]))

        steps(MID, body)

    @pl.when(info[COUNT] != 2)
    def _():
        out[...] = jnp.zeros_like(out)

    pltpu.sync_copy(out, out_any.at[1])
    token[...] = jnp.zeros_like(token)


def early_in_kernel(info, x_any, g_any, high_in, low_in, wb_any, tb_any, after, out_any, token, x, g, gn, wb, tb, mw, wide, out, sems):
    two = info[COUNT] == 2

    @pl.when(two)
    def _():
        need_n = begin_either(info[EVEN] == 1, low_in, high_in, gn, sems.at[4])
        for c in begin([(tb_any, tb), (g_any, g), (x_any.at[0], x), (wb_any, wb)], sems.at[pl.ds(0, 4)]) + [need_n]:
            c.wait()
        mask_taps(mw, tb, info[NEXT1] == 1, info[NEXT2] == 1)

        def upstream(t, n):
            at = pl.ds(t, n)
            return dot(jnp.concatenate([pair(g[0, at]), pair(g[1, at]), pair(gn[at])], axis=-1), mw[...])

        input_rows(wide, wb, upstream, x, g.at[0], out, 0, PAIRS)
        pltpu.sync_copy(out, out_any.at[0])

    @pl.when(jnp.logical_not(two))
    def _():
        out[...] = jnp.zeros_like(out)
        pltpu.sync_copy(out, out_any.at[1])
    token[...] = jnp.zeros_like(token)


def second_kernel(info, high_in, low_in, wf_any, out_ref, wide, xh, wf, sems):
    need_x = begin_either(info[EVEN] == 1, high_in, low_in, xh, sems.at[0])
    need_w = begin([(wf_any, wf)], sems.at[pl.ds(1, 1)])[0]
    clear_edges(wide)
    need_x.wait()
    fill_act(wide, lambda t, half: xh[pl.ds(t, FILL), half])
    need_w.wait()
    conv_to(out_ref, wide, wf)


def output_kernel(info, x_any, s_any, sh_any, s2_any, tf_any, early, out_any, token, x, s, sh, s2, tf, mw, out, sems):
    for c in begin([(x_any.at[0], x), (s_any.at[0], s), (sh_any, sh), (s2_any, s2), (tf_any, tf)], sems):
        c.wait()
    mask_taps(mw, tf, info[BACK1] == 1, info[BACK2] == 1)

    def body(t):
        at = pl.ds(t, MID)
        v = jnp.concatenate([flat(s[at]), flat(sh[at]), flat(s2[at])], axis=-1)
        add_x(x, out, t, dot(v, mw[...]))

    steps(MID, body)
    pltpu.sync_copy(out, out_any.at[0])
    token[...] = jnp.zeros_like(token)


def input_kernel(
    info, x_any, g_any, high1, low1, high2, low2, wb_any, tb_any, early, out_any, token,
    x, g, gn, gnn, wb, tb, mw, wide, out, sems, *, first
):
    two = info[COUNT] == 2
    even = info[EVEN] == 1
    last = jnp.where(two, 1, 0)
    need_n = begin_either(even, low1, high1, gn, sems.at[4])
    need_nn = begin_either(even, low2, high2, gnn, sems.at[5])
    need = begin([(tb_any, tb), (g_any.at[last], g), (wb_any, wb), (x_any.at[last], x)], sems.at[pl.ds(0, 4)])
    for c in need + [need_n, need_nn]:
        c.wait()
    mask_taps(
        mw, tb,
        jnp.where(two, info[LNEXT1], info[NEXT1]) == 1,
        jnp.where(two, info[LNEXT2], info[NEXT2]) == 1,
    )

    def upstream(t, n):
        at = pl.ds(t, n)
        return dot(jnp.concatenate([pair(g[at]), pair(gn[at]), pair(gnn[at])], axis=-1), mw[...])

    input_rows(wide, wb, upstream, x, g, out, first, PAIRS // 2)
    rows = pl.ds(first, PAIRS // 2)
    pltpu.sync_copy(out.at[rows], out_any.at[last, rows])
    token[...] = jnp.zeros_like(token)


def place_kernel(info, mine, theirs, spatial, temporal_out):
    at_x, at_y, core = info[AT_X], info[AT_Y], info[CORE]
    for half in range(2):
        for i in range(SIDE):
            for j in range(SIDE):
                a = lax.rem(at_x + SIDE - i, SIDE)
                b = lax.rem(at_y + SIDE - j, SIDE)
                piece = jnp.where(core == half, mine[a, b], theirs[a, b])
                row = half * HALF + (i * SIDE + j) * PIECE
                if row < 9 * CH:
                    spatial[row : row + PIECE] = piece
                else:
                    temporal_out[row - 9 * CH : row - 9 * CH + PIECE] = piece


FRAME = (PAIRS, 2, COLS, CH)
S_SHAPE = (PAIRS, COLS, 2 * CH)
WIDE = pltpu.VMEM((PAIRS + 1, COLS, 6 * CH), BF16)
VALUES = pltpu.VMEM(S_SHAPE, BF16)
W_SHAPE = (12 * CH, 2 * CH)
T_SHAPE = (6 * CH, 2 * CH)
TAPS = pltpu.VMEM(T_SHAPE, BF16)
TAPS2 = pltpu.VMEM((4 * CH, 2 * CH), BF16)
ACC = (2 * CH, 12 * CH)
TACC = (CH, 3 * CH)
PIECES = (SIDE, SIDE, PIECE, CH)
SMEM = pl.BlockSpec(memory_space=pltpu.SMEM)
VMEM = pl.BlockSpec(memory_space=pltpu.VMEM)
ANY = pl.BlockSpec(memory_space=pl.ANY)
HBM = pl.BlockSpec(memory_space=pltpu.HBM)
FRAME1 = pltpu.VMEM(FRAME, BF16)
FRAME2 = pltpu.VMEM((2,) + FRAME, BF16)
VALUES2 = pltpu.VMEM((2,) + S_SHAPE, BF16)
TAP = pltpu.VMEM((2 * CH, 2 * CH), BF16)
WEIGHT = pltpu.VMEM(W_SHAPE, BF16)


def shape(s, d=BF16):
    return jax.ShapeDtypeStruct(s, d)


def in_hbm(value):
    return pltpu.with_memory_space_constraint(value, pltpu.HBM)


def sems(n):
    return pltpu.SemaphoreType.DMA((n,))


def call(kernel, in_specs, outs, scratch, name, out_specs=None, aliases=None):
    return pl.pallas_call(
        kernel,
        in_specs=in_specs,
        out_specs=out_specs or [VMEM] * len(outs),
        out_shape=outs,
        scratch_shapes=scratch,
        input_output_aliases=aliases or {},
        compiler_params=pltpu.CompilerParams(vmem_limit_bytes=VMEM_BYTES),
        cost_estimate=pl.CostEstimate(flops=1, transcendentals=0, bytes_accessed=1),
        name=name,
    )


def shifts(value, axis, k):
    return lax.ppermute(value, axis, [(i, (i + k) % SIDE) for i in range(SIDE)])


def to_sum(parts, axis):
    return [parts[0]] + [shifts(parts[k], axis, k) for k in range(1, SIDE)]


def gather(part, axis):
    return [part] + [shifts(part, axis, k) for k in range(1, SIDE)]


def split_call(name, n_sum, n_out, out, n_after=0):
    def kernel(*refs):
        ins, outs = refs[:n_sum], refs[n_sum + n_after :]
        for n, out_ref in enumerate(outs):
            v = [r[n] if n_out > 1 else r[...] for r in ins]
            out_ref[...] = v[0] + v[1] if n_sum == 2 else (v[0] + v[2]) + (v[1] + v[3])

    return call(kernel, [VMEM] * n_sum + [ANY] * n_after, [shape(out, F32)] * n_out, [], name)


def stack_call(name, out, n_after):
    def kernel(*refs):
        for n in range(SIDE):
            refs[-1][n] = refs[n][...]

    run = call(kernel, [VMEM] * SIDE + [ANY] * n_after, [shape(out, F32)], [], name)
    return lambda *a: run(*a)[0]


def local(latents, cotangent, frame_counts, spatial_weight, temporal_weight):
    axes = ("x", "y", "z")
    here = lax.axis_index(axes)
    place = jnp.stack([here, lax.axis_index("dp")]).astype(jnp.int32)
    x = in_hbm(latents.reshape((2,) + FRAME))
    g = in_hbm(cotangent.reshape((2,) + FRAME))
    lows = range(0, N_SP, 2)
    low = [(i, i + 1) for i in lows] + [(i + 1, i) for i in lows]
    high = [(i + 1, (i + 2) % N_SP) for i in lows] + [((i + 2) % N_SP, i + 1) for i in lows]
    swap = [(0, 1), (1, 0)]

    info, for_high, for_low = call(
        prep_kernel,
        [SMEM, SMEM, HBM, HBM],
        [shape((INFO,), jnp.int32), shape(FRAME), shape(FRAME)],
        [sems(2)],
        "prep",
        [SMEM, ANY, ANY],
    )(frame_counts, place, x, g)
    high1 = lax.ppermute(for_high, axes, high)
    low1 = lax.ppermute(for_low, axes, low)

    s, acc, tacc, wf, wb, tf, tb = call(
        forward_kernel,
        [SMEM] + [HBM] * 4,
        [shape((2,) + S_SHAPE), shape(ACC, F32), shape(TACC, F32), shape(W_SHAPE), shape(W_SHAPE), shape(T_SHAPE), shape(T_SHAPE)],
        [
            WIDE, VALUES, TAPS2, FRAME2, FRAME2,
            pltpu.VMEM((3, 3, CH, CH), BF16), pltpu.VMEM((3, CH, CH), BF16), sems(4),
        ],
        "forward",
    )(info, x, g, spatial_weight, temporal_weight)

    info2, for_high, for_low = call(
        prep2_kernel,
        [SMEM] + [ANY] * 5,
        [shape((INFO,), jnp.int32), shape(FRAME), shape(FRAME)],
        [sems(2)],
        "prep2",
        [SMEM, ANY, ANY],
    )(info, x, g, high1, low1, tacc)
    high2 = lax.ppermute(for_high, axes, high)
    low2 = lax.ppermute(for_low, axes, low)

    own, other, sh = call(
        grad_kernel,
        [SMEM] + [ANY] * 9,
        [shape(PIECES, F32), shape(PIECES, F32), shape(S_SHAPE)],
        [
            WIDE, FRAME1, FRAME1, FRAME1, FRAME2, VALUES, VALUES, VALUES,
            pltpu.VMEM(ACC, F32), pltpu.VMEM(TACC, F32), WEIGHT, TAPS, TAPS2, pltpu.VMEM((2, HALF, CH), F32), sems(10),
        ],
        "grads",
        [VMEM, VMEM, ANY],
    )(info2, high1, low1, x, g, s, acc, tacc, wf, tb)

    chunks = split_call("core_sum", 2, SIDE, PIECES[1:])(own, lax.ppermute(other, "dp", swap))
    frames = [pltpu.HBM((2,) + FRAME, BF16), shape((8, CH), F32)]
    early_out, done_a = call(
        early_out_kernel,
        [SMEM] + [ANY] * 5,
        frames,
        [FRAME1, VALUES2, VALUES, TAPS, TAPS, FRAME1, sems(4)],
        "early_out",
        [ANY, VMEM],
    )(info, x, s, sh, tf, chunks[0])
    early_in, done_b = call(
        early_in_kernel,
        [SMEM] + [ANY] * 7,
        frames,
        [FRAME1, FRAME2, FRAME1, WEIGHT, TAPS, TAPS, WIDE, FRAME1, sems(5)],
        "early_in",
        [ANY, VMEM],
    )(info, x, g, high1, low1, wb, tb, chunks[0])
    chunks = split_call("x_sum", SIDE, SIDE, PIECES[2:], 2)(*to_sum(chunks, "x"), done_a, done_b)
    s2 = call(second_kernel, [SMEM] + [ANY] * 3, [shape(S_SHAPE)], [WIDE, FRAME1, WEIGHT, sems(2)], "second")(info, high2, low2, wf)[0]
    part = split_call("y_sum", SIDE, 1, PIECES[2:], 1)(*to_sum(chunks, "y"), s2)[0]
    block_out, done_c = call(
        output_kernel,
        [SMEM] + [ANY] * 6,
        frames,
        [FRAME1, VALUES, VALUES, VALUES, TAPS, TAPS, FRAME1, sems(5)],
        "output",
        [ANY, VMEM],
        {6: 0},
    )(info, x, s, sh, s2, tf, in_hbm(early_out))
    part = split_call("z_sum", SIDE, 1, PIECES[2:], 1)(*to_sum([part] * SIDE, "z"), done_c)[0]

    def input_half(first, so_far):
        return call(
            functools.partial(input_kernel, first=first),
            [SMEM] + [ANY] * 9,
            frames,
            [FRAME1, FRAME1, FRAME1, FRAME1, WEIGHT, TAPS, TAPS, WIDE, FRAME1, sems(6)],
            "input_grad",
            [ANY, VMEM],
            {9: 0},
        )(info, x, g, high1, low1, high2, low2, wb, tb, in_hbm(so_far))

    input_grad, done_d = input_half(0, early_in)
    own = stack_call("y_stack", PIECES[1:], 1)(*gather(part, "y"), done_d)
    input_grad, done_e = input_half(PAIRS // 2, input_grad)
    own = stack_call("x_stack", PIECES, 1)(*gather(own, "x"), done_e)
    theirs = lax.ppermute(own, "dp", swap)
    spatial_grad, temporal_grad = call(
        place_kernel, [SMEM, VMEM, VMEM], [shape((9 * CH, CH), F32), shape((3 * CH, CH), F32)], [], "place"
    )(info, own, theirs)
    return (
        block_out.reshape(latents.shape),
        input_grad.reshape(latents.shape),
        spatial_grad.reshape(3, 3, CH, CH),
        temporal_grad.reshape(3, CH, CH),
    )


def solution(mesh):
    chips = Mesh(mesh.devices.reshape(2, SIDE, SIDE, SIDE), ("dp", "x", "y", "z"))
    held = P(("dp", "x", "y", "z"), None, None, None)
    return jax.shard_map(
        local,
        mesh=chips,
        in_specs=(held, held, P("dp", None), P(), P()),
        out_specs=(held, held, P(), P()),
        check_vma=False,
    )
```

time: 365 us -> 111 us (0.30)
  waiting for transfers between devices: 167 us -> 27.3 us
  matrix products: 96.8 us -> 0 us
  Pallas kernels: 0 us -> 43.5 us
  local copies, waits for them, and re-layouts: 28.5 us -> 0.66 us
  other arithmetic: 16.7 us -> 0.08 us
  between operations: 14.6 us -> 0.9 us
    psum x1 -> x0, waiting for transfers between devices: 128 us -> none  [local(): lax.psum((spatial_sum * scale, temporal_sum * scale), ('dp', 'sp'))]
    dot_general x36 -> x0, matrix products: 96.8 us -> none  [the longest x18 62.8 us: spatial_apply(): jnp.einsum('fhwc,cd->fhwd', window, kernel[row_tap, col_tap], preferred_e...]
    pallas_call x0 -> x17, Pallas kernels: none -> 43.5 us  [the longest x2 10.7 us: input_half(): call(functools.partial(input_kernel, first=first), [SMEM] + [ANY] * 9, fr...]
    all_to_all x4 -> x0, waiting for transfers between devices: 39.7 us -> none  [the longest x1 21.1 us: local(): lax.all_to_all(spatial_out, 'sp', split_axis=1, concat_axis=0, tiled=True)]
    all_to_all x4 -> x0, starting transfers between devices: 38.9 us -> none  [the longest x1 12.2 us: local(): lax.all_to_all(cotangent, 'sp', split_axis=1, concat_axis=0, tiled=True)]
    ppermute x0 -> x21, starting transfers between devices: none -> 38.7 us  [the longest x15 15.6 us: shifts(): return lax.ppermute(value, axis, [(i, (i + k) % SIDE) for i in range(SIDE)])]
    ppermute x0 -> x21, waiting for transfers between devices: none -> 27.3 us  [the longest x1 14.2 us: local(): high1 = lax.ppermute(for_high, axes, high)]
    gather x4 -> x0, local copies, waits for them, and re-layouts: 13.6 us -> none  [the longest x2 6.8 us: to_slots(): jnp.take(frames, jnp.clip(slot_frame, 0, frames.shape[0] - 1), axis=0)]
  transfers between devices with their start and end apart: 5 -> 21, of which waited for: 3 -> 6; matrix products, arithmetic and copies ran while one was open for 30% -> 0% of each run, Pallas kernels for 0% -> 34%
where the time goes in v2:
time: 111 us
  Pallas kernels  43.5 us (39%)
  starting transfers between devices  38.7 us (35%)
  waiting for transfers between devices  27.3 us (25%)
    ppermute x15, starting transfers between devices, shifts(): return lax.ppermute(value, axis, [(i, (i + k) % SIDE) for i in range(SIDE)])  15.6 us
    ppermute x1, waiting for transfers between devices, local(): high1 = lax.ppermute(for_high, axes, high)  14.2 us
    pallas_call x2, Pallas kernels, input_half(): call(functools.partial(input_kernel, first=first), [SMEM] + [ANY] * 9, fr...  10.7 us
    ppermute x15, waiting for transfers between devices, shifts(): return lax.ppermute(value, axis, [(i, (i + k) % SIDE) for i in range(SIDE)])  9.5 us
    ppermute x1, starting transfers between devices, local(): high1 = lax.ppermute(for_high, axes, high)  9.31 us
    pallas_call x1, Pallas kernels, local(): call(forward_kernel, [SMEM] + [HBM] * 4, [shape((2,) + S_SHAPE), shape(AC...  8.63 us
    pallas_call x1, Pallas kernels, local(): call(grad_kernel, [SMEM] + [ANY] * 9, [shape(PIECES, F32), shape(PIECES,...  7.64 us
    ppermute x1, starting transfers between devices, local(): theirs = lax.ppermute(own, 'dp', swap)  6.02 us
  transfers between devices with their start and end apart: 21, of which 6 were waited for; matrix products, arithmetic and copies ran while one was open for 0% of the time, Pallas kernels for 34%

profile of v2, /device:TPU:1, one launch (start us, length us, event | category | flops | bytes accessed | tf_op | source)
XLA Modules:
  0.0 111.1 jit_solution(10418970850359915239)
XLA Ops:
  0.7 0.7 copy-done.2
  1.4 2.9 %prep.1 = (s32[16]{0:T(128)S(1)}, bf16[32,2,64,128]{3,2,1,0:T(8,128)(2,1)S(1)}, bf16[32,2,64,128]{3,2,1,0:T(8,128)(2,1)S(1)}) custom-call(s32[1,64]{1,0:T(1,128)S(1)} %copy-done.2, s32[2]{0:T(128)S(1)} %pad_add_fusion.place, bf16[2,32,2,64,128]{4,3,2,1,0:T(8,128)(2,1)} %bitcast.8, bf16[2,32,2,64,128]{4,3,2,1,0:T(8,128)(2,1)} %bitcast.17), custom_call_target="tpu_custom_call" | custom-call | flops 1 | bytes 1 | tf_op jit(solution)/shard_map/prep/pallas_call | solution.py:591
  4.3 9.3 %collective-permute-start = (bf16[32,2,64,128]{3,2,1,0:T(8,128)(2,1)S(1)}, bf16[32,2,64,128]{3,2,1,0:T(8,128)(2,1)S(1)}, u32[]{:S(2)}, u32[]{:S(2)}) collective-permute-start(bf16[32,2,64,128]{3,2,1,0:T(8,128)(2,1)S(1)} %get-tuple-element.42), channel_id=1, source_target_pairs={{1,2},{3,4},{5,6},{7,8},{9,10},{11,12},{13,14},{15,16},{17,18},{19... | collective-permute-start | bytes 3145736 | tf_op jit(solution)/shard_map/ppermute | solution.py:599
  13.6 8.6 %forward.1 = (bf16[2,32,64,256]{3,2,1,0:T(8,128)(2,1)S(1)}, f32[256,1536]{1,0:T(8,128)S(1)}, f32[128,384]{1,0:T(8,128)S(1)}, bf16[1536,256]{1,0:T(8,128)(2,1)S(1...) custom-call(s32[16]{0:T(128)S(1)} %get-tuple-element.40.info, ...), custom_call_target="tpu_custom_call" | custom-call | flops 1 | bytes 1 | tf_op jit(solution)/shard_map/forward/pallas_call | solution.py:602
  22.2 14.2 %collective-permute-done.high_in.high1 = bf16[32,2,64,128]{3,2,1,0:T(8,128)(2,1)S(1)} collective-permute-done((bf16[32,2,64,128]{3,2,1,0:T(8,128)(2,1)S(1)}, bf16[32,2,64,128]{3,2,1,0:T(8,128)(2,1)S(1)}, u32[]{:S(2)}, u32[]{:S(2)}) %collective-permute-start) | collective-permute-done | bytes 1048608 | tf_op jit(solution)/shard_map/ppermute | solution.py:599
  36.5 0.8 collective-permute-done.1.low_in.low1
  37.3 1.3 %prep2.1 = (s32[16]{0:T(128)S(1)}, bf16[32,2,64,128]{3,2,1,0:T(8,128)(2,1)S(1)}, bf16[32,2,64,128]{3,2,1,0:T(8,128)(2,1)S(1)}) custom-call(s32[16]{0:T(128)S(1)} %get-tuple-element.40.info, bf16[2,32,2,64,128]{4,3,2,1,0:T(8,128)(2,1)} %bitcast.10, bf16[2,32,2,64,128]{4,3,2,1,0:T(8,128)(2,1)} %bitcast.19, ...), custom_call_target="tpu_custom_call" | custom-call | flops 1 | bytes 1 | tf_op jit(solution)/shard_map/prep2/pallas_call | solution.py:613
  38.6 5.8 %collective-permute-start.2 = (bf16[32,2,64,128]{3,2,1,0:T(8,128)(2,1)S(1)}, bf16[32,2,64,128]{3,2,1,0:T(8,128)(2,1)S(1)}, u32[]{:S(2)}, u32[]{:S(2)}) collective-permute-start(bf16[32,2,64,128]{3,2,1,0:T(8,128)(2,1)S(1)} %get-tuple-element.50), channel_id=1, source_target_pairs={{1,2},{3,4},{5,6},{7,8},{9,10},{11,12},{13,14},{15,16},{17,18},{19... | collective-permute-start | bytes 3145736 | tf_op jit(solution)/shard_map/ppermute | solution.py:621
  44.5 7.6 %grads.1 = (f32[4,4,48,128]{3,2,1,0:T(8,128)S(1)}, f32[4,4,48,128]{3,2,1,0:T(8,128)S(1)}, bf16[32,64,256]{2,1,0:T(8,128)(2,1)S(1)}) custom-call(s32[16]{0:T(128)S(1)} %get-tuple-element.45.info, bf16[32,2,64,128]{3,2,1,0:T(8,128)(2,1)S(1)} %collective-permute-done.high_in.high1, bf16[32,2,64,128]{3,2,1,0:T(8,128)(2,1)S(1)} %collective-permute-done.1.low_in.low1, ...), custom_call_target="tpu_custom_call" | custom-call | flops 1 | bytes 1 | tf_op jit(solution)/shard_map/grads/pallas_call | solution.py:624
  52.1 1.9 %collective-permute-start.4 = (f32[4,4,48,128]{3,2,1,0:T(8,128)S(1)}, f32[4,4,48,128]{3,2,1,0:T(8,128)S(1)}, u32[]{:S(2)}, u32[]{:S(2)}) collective-permute-start(f32[4,4,48,128]{3,2,1,0:T(8,128)S(1)} %get-tuple-element.54), channel_id=1, source_target_pairs={{0,64},{64,0},{1,65},{65,1},{2,66},{66,2},{3,67},{67,3},{4,68},{68... | collective-permute-start | bytes 1179656 | tf_op jit(solution)/shard_map/ppermute | solution.py:636
  54.0 1.3 %collective-permute-done.4.refs_1_ = f32[4,4,48,128]{3,2,1,0:T(8,128)S(1)} collective-permute-done((f32[4,4,48,128]{3,2,1,0:T(8,128)S(1)}, f32[4,4,48,128]{3,2,1,0:T(8,128)S(1)}, u32[]{:S(2)}, u32[]{:S(2)}) %collective-permute-start.4) | collective-permute-done | bytes 393248 | tf_op jit(solution)/shard_map/ppermute | solution.py:636
  55.5 0.5 collective-permute-start.6
  56.0 2.2 %collective-permute-start.7 = (f32[4,48,128]{2,1,0:T(8,128)S(1)}, f32[4,48,128]{2,1,0:T(8,128)S(1)}, u32[]{:S(2)}, u32[]{:S(2)}) collective-permute-start(f32[4,48,128]{2,1,0:T(8,128)S(1)} %get-tuple-element.64), channel_id=1, source_target_pairs={{0,48},{16,0},{32,16},{48,32},{1,49},{17,1},{33,17},{49,33},{2,50}... | collective-permute-start | bytes 294920 | tf_op jit(solution)/shard_map/ppermute | solution.py:550
  58.2 1.7 %early_out.1 = (bf16[2,32,2,64,128]{4,3,2,1,0:T(8,128)(2,1)}, f32[8,128]{1,0:T(8,128)S(1)}) custom-call(s32[16]{0:T(128)S(1)} %get-tuple-element.40.info, bf16[2,32,2,64,128]{4,3,2,1,0:T(8,128)(2,1)} %bitcast.12, bf16[2,32,64,256]{3,2,1,0:T(8,128)(2,1)S(1)} %get-tuple-element.41.s_any, bf16[32,64,256]{2,1,0:T(8,128)(2,1)S(1)} %get-tuple-element.49.sh_any, ...), custom_call_target="tpu_custom_call" | custom-call | flops 1 | bytes 1 | tf_op jit(solution)/shard_map/early_out/pallas_call | solution.py:638
  59.9 1.7 %early_in.1 = (bf16[2,32,2,64,128]{4,3,2,1,0:T(8,128)(2,1)}, f32[8,128]{1,0:T(8,128)S(1)}) custom-call(s32[16]{0:T(128)S(1)} %get-tuple-element.40.info, bf16[2,32,2,64,128]{4,3,2,1,0:T(8,128)(2,1)} %bitcast.13, bf16[2,32,2,64,128]{4,3,2,1,0:T(8,128)(2,1)} %bitcast.21, bf16[32,2,64,128]{3,2,1,0:T(8,128)(2,1)S(1)} %collective-permute-done.high_in.high1, ...), custom_call_target="tpu_custom_call" | custom-call | flops 1 | bytes 1 | tf_op jit(solution)/shard_map/early_in/pallas_call | solution.py:646
  61.6 1.6 %collective-permute-done.5.refs_1_ = f32[4,48,128]{2,1,0:T(8,128)S(1)} collective-permute-done((f32[4,48,128]{2,1,0:T(8,128)S(1)}, f32[4,48,128]{2,1,0:T(8,128)S(1)}, u32[]{:S(2)}, u32[]{:S(2)}) %collective-permute-start.5) | collective-permute-done | bytes 98336 | tf_op jit(solution)/shard_map/ppermute | solution.py:550
  63.2 7.9 %collective-permute-done.7.refs_3_ = f32[4,48,128]{2,1,0:T(8,128)S(1)} collective-permute-done((f32[4,48,128]{2,1,0:T(8,128)S(1)}, f32[4,48,128]{2,1,0:T(8,128)S(1)}, u32[]{:S(2)}, u32[]{:S(2)}) %collective-permute-start.7) | collective-permute-done | bytes 98336 | tf_op jit(solution)/shard_map/ppermute | solution.py:550
  71.1 0.2 collective-permute-start.9
  71.4 2.4 %collective-permute-start.10 = (f32[48,128]{1,0:T(8,128)S(1)}, f32[48,128]{1,0:T(8,128)S(1)}, u32[]{:S(2)}, u32[]{:S(2)}) collective-permute-start(f32[48,128]{1,0:T(8,128)S(1)} %get-tuple-element.70), channel_id=1, source_target_pairs={{0,12},{4,0},{8,4},{12,8},{1,13},{5,1},{9,5},{13,9},{2,14},{6,2},{... | collective-permute-start | bytes 73736 | tf_op jit(solution)/shard_map/ppermute | solution.py:550
  73.8 3.3 %second.1.s2_any.refs_4_ = bf16[32,64,256]{2,1,0:T(8,128)(2,1)S(1)} custom-call(s32[16]{0:T(128)S(1)} %get-tuple-element.40.info, bf16[32,2,64,128]{3,2,1,0:T(8,128)(2,1)S(1)} %collective-permute-done.2.high_in.high2, bf16[32,2,64,128]{3,2,1,0:T(8,128)(2,1)S(1)} %collective-permute-done.3.low_in.low2, bf16[1536,256]{1,0:T(8,128)(2,1)S(1)} %get-tuple-element.47.wf_any), custom_call_target="tpu_custom_call" | custom-call | flops 1 | bytes 1 | tf_op jit(solution)/shard_map/second/pallas_call | solution.py:655
  77.3 0.5 collective-permute-start.12
  77.7 2.2 %collective-permute-start.13 = (f32[48,128]{1,0:T(8,128)S(1)}, f32[48,128]{1,0:T(8,128)S(1)}, u32[]{:S(2)}, u32[]{:S(2)}) collective-permute-start(f32[48,128]{1,0:T(8,128)S(1)} %y_sum.1.refs_0_), channel_id=1, source_target_pairs={{0,3},{1,0},{2,1},{3,2},{4,7},{5,4},{6,5},{7,6},{8,11},{9,8},{10,9... | collective-permute-start | bytes 73736 | tf_op jit(solution)/shard_map/ppermute | solution.py:550
  79.9 4.0 %output.1 = (bf16[2,32,2,64,128]{4,3,2,1,0:T(8,128)(2,1)}, f32[8,128]{1,0:T(8,128)S(1)}) custom-call(s32[16]{0:T(128)S(1)} %get-tuple-element.40.info, bf16[2,32,2,64,128]{4,3,2,1,0:T(8,128)(2,1)} %bitcast.14, bf16[2,32,64,256]{3,2,1,0:T(8,128)(2,1)S(1)} %get-tuple-element.41.s_any, ...), custom_call_target="tpu_custom_call", output_to_operand_aliasing={{0}: (6, {})} | custom-call | flops 1 | bytes 1 | tf_op jit(solution)/shard_map/output/pallas_call | solution.py:657
  84.0 1.3 %collective-permute-start.14 = (f32[48,128]{1,0:T(8,128)S(1)}, f32[48,128]{1,0:T(8,128)S(1)}, u32[]{:S(2)}, u32[]{:S(2)}) collective-permute-start(f32[48,128]{1,0:T(8,128)S(1)} %z_sum.1.refs_0_), channel_id=1, source_target_pairs={{0,4},{4,8},{8,12},{12,0},{1,5},{5,9},{9,13},{13,1},{2,6},{6,10},{... | collective-permute-start | bytes 73736 | tf_op jit(solution)/shard_map/ppermute | solution.py:550
  85.3 1.2 %collective-permute-start.15 = (f32[48,128]{1,0:T(8,128)S(1)}, f32[48,128]{1,0:T(8,128)S(1)}, u32[]{:S(2)}, u32[]{:S(2)}) collective-permute-start(f32[48,128]{1,0:T(8,128)S(1)} %z_sum.1.refs_0_), channel_id=1, source_target_pairs={{0,8},{4,12},{8,0},{12,4},{1,9},{5,13},{9,1},{13,5},{2,10},{6,14},... | collective-permute-start | bytes 73736 | tf_op jit(solution)/shard_map/ppermute | solution.py:550
  86.5 2.0 %collective-permute-start.16 = (f32[48,128]{1,0:T(8,128)S(1)}, f32[48,128]{1,0:T(8,128)S(1)}, u32[]{:S(2)}, u32[]{:S(2)}) collective-permute-start(f32[48,128]{1,0:T(8,128)S(1)} %z_sum.1.refs_0_), channel_id=1, source_target_pairs={{0,12},{4,0},{8,4},{12,8},{1,13},{5,1},{9,5},{13,9},{2,14},{6,2},{... | collective-permute-start | bytes 73736 | tf_op jit(solution)/shard_map/ppermute | solution.py:550
  88.5 5.3 %input_grad.2 = (bf16[2,32,2,64,128]{4,3,2,1,0:T(8,128)(2,1)}, f32[8,128]{1,0:T(8,128)S(1)}) custom-call(s32[16]{0:T(128)S(1)} %get-tuple-element.40.info, bf16[2,32,2,64,128]{4,3,2,1,0:T(8,128)(2,1)} %bitcast.15, bf16[2,32,2,64,128]{4,3,2,1,0:T(8,128)(2,1)} %bitcast.22, ...), custom_call_target="tpu_custom_call", output_to_operand_aliasing={{0}: (9, {})} | custom-call | flops 1 | bytes 1 | tf_op jit(solution)/shard_map/input_grad/pallas_call | solution.py:669
  93.9 2.8 %collective-permute-start.18 = (f32[4,48,128]{2,1,0:T(8,128)S(1)}, f32[4,48,128]{2,1,0:T(8,128)S(1)}, u32[]{:S(2)}, u32[]{:S(2)}) collective-permute-start(f32[4,48,128]{2,1,0:T(8,128)S(1)} %y_stack.1.refs_0_), channel_id=1, source_target_pairs={{0,32},{16,48},{32,0},{48,16},{1,33},{17,49},{33,1},{49,17},{2,34}... | collective-permute-start | bytes 294920 | tf_op jit(solution)/shard_map/ppermute | solution.py:550
  96.8 5.3 %input_grad.3 = (bf16[2,32,2,64,128]{4,3,2,1,0:T(8,128)(2,1)}, f32[8,128]{1,0:T(8,128)S(1)}) custom-call(s32[16]{0:T(128)S(1)} %get-tuple-element.40.info, bf16[2,32,2,64,128]{4,3,2,1,0:T(8,128)(2,1)} %bitcast.16, bf16[2,32,2,64,128]{4,3,2,1,0:T(8,128)(2,1)} %bitcast.23, ...), custom_call_target="tpu_custom_call", output_to_operand_aliasing={{0}: (9, {})} | custom-call | flops 1 | bytes 1 | tf_op jit(solution)/shard_map/input_grad/pallas_call | solution.py:669
  102.2 6.0 %collective-permute-start.20 = (f32[4,4,48,128]{3,2,1,0:T(8,128)S(1)}, f32[4,4,48,128]{3,2,1,0:T(8,128)S(1)}, u32[]{:S(2)}, u32[]{:S(2)}) collective-permute-start(f32[4,4,48,128]{3,2,1,0:T(8,128)S(1)} %x_stack.1.mine), channel_id=1, source_target_pairs={{0,64},{64,0},{1,65},{65,1},{2,66},{66,2},{3,67},{67,3},{4,68},{68... | collective-permute-start | bytes 1179656 | tf_op jit(solution)/shard_map/ppermute | solution.py:683
  108.2 1.3 %collective-permute-done.20.theirs = f32[4,4,48,128]{3,2,1,0:T(8,128)S(1)} collective-permute-done((f32[4,4,48,128]{3,2,1,0:T(8,128)S(1)}, f32[4,4,48,128]{3,2,1,0:T(8,128)S(1)}, u32[]{:S(2)}, u32[]{:S(2)}) %collective-permute-start.20) | collective-permute-done | bytes 393248 | tf_op jit(solution)/shard_map/ppermute | solution.py:683
  109.6 1.5 %place.1 = (f32[1152,128]{1,0:T(8,128)}, f32[384,128]{1,0:T(8,128)}) custom-call(s32[16]{0:T(128)S(1)} %get-tuple-element.40.info, f32[4,4,48,128]{3,2,1,0:T(8,128)S(1)} %x_stack.1.mine, f32[4,4,48,128]{3,2,1,0:T(8,128)S(1)} %collective-permute-done.20.theirs), custom_call_target="tpu_custom_call" | custom-call | flops 1 | bytes 1 | tf_op jit(solution)/shard_map/place/pallas_call | solution.py:684
  (34 shorter events, 0.6 us)
Async XLA Ops:
  0.7 0.7 copy-start.2
  1.4 12.2 %copy-start = (bf16[3,3,128,128]{3,2,1,0:T(8,128)(2,1)S(1)}, bf16[3,3,128,128]{3,2,1,0:T(8,128)(2,1)}, u32[]{:S(2)}) copy-start(bf16[3,3,128,128]{3,2,1,0:T(8,128)(2,1)} %w_any.1) | copy-start | bytes 884740
  1.4 12.2 %copy-start.1 = (bf16[3,128,128]{2,1,0:T(8,128)(2,1)S(1)}, bf16[3,128,128]{2,1,0:T(8,128)(2,1)}, u32[]{:S(2)}) copy-start(bf16[3,128,128]{2,1,0:T(8,128)(2,1)} %tw_any.1) | copy-start | bytes 294916
  4.3 32.2 %collective-permute-start = (bf16[32,2,64,128]{3,2,1,0:T(8,128)(2,1)S(1)}, bf16[32,2,64,128]{3,2,1,0:T(8,128)(2,1)S(1)}, u32[]{:S(2)}, u32[]{:S(2)}) collective-permute-start(bf16[32,2,64,128]{3,2,1,0:T(8,128)(2,1)S(1)} %get-tuple-element.42), channel_id=1, source_target_pairs={{1,2},{3,4},{5,6},{7,8},{9,10},{11,12},{13,14},{15,16},{17,18},{19... | collective-permute-start | bytes 3145736 | tf_op jit(solution)/shard_map/ppermute | solution.py:599
  13.6 23.7 %collective-permute-start.1 = (bf16[32,2,64,128]{3,2,1,0:T(8,128)(2,1)S(1)}, bf16[32,2,64,128]{3,2,1,0:T(8,128)(2,1)S(1)}, u32[]{:S(2)}, u32[]{:S(2)}) collective-permute-start(bf16[32,2,64,128]{3,2,1,0:T(8,128)(2,1)S(1)} %get-tuple-element.43), channel_id=1, source_target_pairs={{0,1},{2,3},{4,5},{6,7},{8,9},{10,11},{12,13},{14,15},{16,17},{18,... | collective-permute-start | bytes 3145736 | tf_op jit(solution)/shard_map/ppermute | solution.py:600
  38.6 35.2 %collective-permute-start.2 = (bf16[32,2,64,128]{3,2,1,0:T(8,128)(2,1)S(1)}, bf16[32,2,64,128]{3,2,1,0:T(8,128)(2,1)S(1)}, u32[]{:S(2)}, u32[]{:S(2)}) collective-permute-start(bf16[32,2,64,128]{3,2,1,0:T(8,128)(2,1)S(1)} %get-tuple-element.50), channel_id=1, source_target_pairs={{1,2},{3,4},{5,6},{7,8},{9,10},{11,12},{13,14},{15,16},{17,18},{19... | collective-permute-start | bytes 3145736 | tf_op jit(solution)/shard_map/ppermute | solution.py:621
  44.5 29.4 %collective-permute-start.3 = (bf16[32,2,64,128]{3,2,1,0:T(8,128)(2,1)S(1)}, bf16[32,2,64,128]{3,2,1,0:T(8,128)(2,1)S(1)}, u32[]{:S(2)}, u32[]{:S(2)}) collective-permute-start(bf16[32,2,64,128]{3,2,1,0:T(8,128)(2,1)S(1)} %get-tuple-element.51), channel_id=1, source_target_pairs={{0,1},{2,3},{4,5},{6,7},{8,9},{10,11},{12,13},{14,15},{16,17},{18,... | collective-permute-start | bytes 3145736 | tf_op jit(solution)/shard_map/ppermute | solution.py:622
  52.1 3.3 %collective-permute-start.4 = (f32[4,4,48,128]{3,2,1,0:T(8,128)S(1)}, f32[4,4,48,128]{3,2,1,0:T(8,128)S(1)}, u32[]{:S(2)}, u32[]{:S(2)}) collective-permute-start(f32[4,4,48,128]{3,2,1,0:T(8,128)S(1)} %get-tuple-element.54), channel_id=1, source_target_pairs={{0,64},{64,0},{1,65},{65,1},{2,66},{66,2},{3,67},{67,3},{4,68},{68... | collective-permute-start | bytes 1179656 | tf_op jit(solution)/shard_map/ppermute | solution.py:636
  55.4 7.7 %collective-permute-start.5 = (f32[4,48,128]{2,1,0:T(8,128)S(1)}, f32[4,48,128]{2,1,0:T(8,128)S(1)}, u32[]{:S(2)}, u32[]{:S(2)}) collective-permute-start(f32[4,48,128]{2,1,0:T(8,128)S(1)} %get-tuple-element.62), channel_id=1, source_target_pairs={{0,16},{16,32},{32,48},{48,0},{1,17},{17,33},{33,49},{49,1},{2,18}... | collective-permute-start | bytes 294920 | tf_op jit(solution)/shard_map/ppermute | solution.py:550
  55.5 7.7 %collective-permute-start.6 = (f32[4,48,128]{2,1,0:T(8,128)S(1)}, f32[4,48,128]{2,1,0:T(8,128)S(1)}, u32[]{:S(2)}, u32[]{:S(2)}) collective-permute-start(f32[4,48,128]{2,1,0:T(8,128)S(1)} %get-tuple-element.63), channel_id=1, source_target_pairs={{0,32},{16,48},{32,0},{48,16},{1,33},{17,49},{33,1},{49,17},{2,34}... | collective-permute-start | bytes 294920 | tf_op jit(solution)/shard_map/ppermute | solution.py:550
  56.0 15.0 %collective-permute-start.7 = (f32[4,48,128]{2,1,0:T(8,128)S(1)}, f32[4,48,128]{2,1,0:T(8,128)S(1)}, u32[]{:S(2)}, u32[]{:S(2)}) collective-permute-start(f32[4,48,128]{2,1,0:T(8,128)S(1)} %get-tuple-element.64), channel_id=1, source_target_pairs={{0,48},{16,0},{32,16},{48,32},{1,49},{17,1},{33,17},{49,33},{2,50}... | collective-permute-start | bytes 294920 | tf_op jit(solution)/shard_map/ppermute | solution.py:550
  71.1 6.1 %collective-permute-start.8 = (f32[48,128]{1,0:T(8,128)S(1)}, f32[48,128]{1,0:T(8,128)S(1)}, u32[]{:S(2)}, u32[]{:S(2)}) collective-permute-start(f32[48,128]{1,0:T(8,128)S(1)} %get-tuple-element.68), channel_id=1, source_target_pairs={{0,4},{4,8},{8,12},{12,0},{1,5},{5,9},{9,13},{13,1},{2,6},{6,10},{... | collective-permute-start | bytes 73736 | tf_op jit(solution)/shard_map/ppermute | solution.py:550
  71.1 6.0 %collective-permute-start.9 = (f32[48,128]{1,0:T(8,128)S(1)}, f32[48,128]{1,0:T(8,128)S(1)}, u32[]{:S(2)}, u32[]{:S(2)}) collective-permute-start(f32[48,128]{1,0:T(8,128)S(1)} %get-tuple-element.69), channel_id=1, source_target_pairs={{0,8},{4,12},{8,0},{12,4},{1,9},{5,13},{9,1},{13,5},{2,10},{6,14},... | collective-permute-start | bytes 73736 | tf_op jit(solution)/shard_map/ppermute | solution.py:550
  71.4 5.8 %collective-permute-start.10 = (f32[48,128]{1,0:T(8,128)S(1)}, f32[48,128]{1,0:T(8,128)S(1)}, u32[]{:S(2)}, u32[]{:S(2)}) collective-permute-start(f32[48,128]{1,0:T(8,128)S(1)} %get-tuple-element.70), channel_id=1, source_target_pairs={{0,12},{4,0},{8,4},{12,8},{1,13},{5,1},{9,5},{13,9},{2,14},{6,2},{... | collective-permute-start | bytes 73736 | tf_op jit(solution)/shard_map/ppermute | solution.py:550
  77.2 6.7 %collective-permute-start.11 = (f32[48,128]{1,0:T(8,128)S(1)}, f32[48,128]{1,0:T(8,128)S(1)}, u32[]{:S(2)}, u32[]{:S(2)}) collective-permute-start(f32[48,128]{1,0:T(8,128)S(1)} %y_sum.1.refs_0_), channel_id=1, source_target_pairs={{0,1},{1,2},{2,3},{3,0},{4,5},{5,6},{6,7},{7,4},{8,9},{9,10},{10,1... | collective-permute-start | bytes 73736 | tf_op jit(solution)/shard_map/ppermute | solution.py:550
  77.3 6.7 %collective-permute-start.12 = (f32[48,128]{1,0:T(8,128)S(1)}, f32[48,128]{1,0:T(8,128)S(1)}, u32[]{:S(2)}, u32[]{:S(2)}) collective-permute-start(f32[48,128]{1,0:T(8,128)S(1)} %y_sum.1.refs_0_), channel_id=1, source_target_pairs={{0,2},{1,3},{2,0},{3,1},{4,6},{5,7},{6,4},{7,5},{8,10},{9,11},{10,... | collective-permute-start | bytes 73736 | tf_op jit(solution)/shard_map/ppermute | solution.py:550
  77.7 6.2 %collective-permute-start.13 = (f32[48,128]{1,0:T(8,128)S(1)}, f32[48,128]{1,0:T(8,128)S(1)}, u32[]{:S(2)}, u32[]{:S(2)}) collective-permute-start(f32[48,128]{1,0:T(8,128)S(1)} %y_sum.1.refs_0_), channel_id=1, source_target_pairs={{0,3},{1,0},{2,1},{3,2},{4,7},{5,4},{6,5},{7,6},{8,11},{9,8},{10,9... | collective-permute-start | bytes 73736 | tf_op jit(solution)/shard_map/ppermute | solution.py:550
  84.0 9.9 %collective-permute-start.14 = (f32[48,128]{1,0:T(8,128)S(1)}, f32[48,128]{1,0:T(8,128)S(1)}, u32[]{:S(2)}, u32[]{:S(2)}) collective-permute-start(f32[48,128]{1,0:T(8,128)S(1)} %z_sum.1.refs_0_), channel_id=1, source_target_pairs={{0,4},{4,8},{8,12},{12,0},{1,5},{5,9},{9,13},{13,1},{2,6},{6,10},{... | collective-permute-start | bytes 73736 | tf_op jit(solution)/shard_map/ppermute | solution.py:550
  85.3 8.5 %collective-permute-start.15 = (f32[48,128]{1,0:T(8,128)S(1)}, f32[48,128]{1,0:T(8,128)S(1)}, u32[]{:S(2)}, u32[]{:S(2)}) collective-permute-start(f32[48,128]{1,0:T(8,128)S(1)} %z_sum.1.refs_0_), channel_id=1, source_target_pairs={{0,8},{4,12},{8,0},{12,4},{1,9},{5,13},{9,1},{13,5},{2,10},{6,14},... | collective-permute-start | bytes 73736 | tf_op jit(solution)/shard_map/ppermute | solution.py:550
  86.5 7.4 %collective-permute-start.16 = (f32[48,128]{1,0:T(8,128)S(1)}, f32[48,128]{1,0:T(8,128)S(1)}, u32[]{:S(2)}, u32[]{:S(2)}) collective-permute-start(f32[48,128]{1,0:T(8,128)S(1)} %z_sum.1.refs_0_), channel_id=1, source_target_pairs={{0,12},{4,0},{8,4},{12,8},{1,13},{5,1},{9,5},{13,9},{2,14},{6,2},{... | collective-permute-start | bytes 73736 | tf_op jit(solution)/shard_map/ppermute | solution.py:550
  93.9 8.3 %collective-permute-start.17 = (f32[4,48,128]{2,1,0:T(8,128)S(1)}, f32[4,48,128]{2,1,0:T(8,128)S(1)}, u32[]{:S(2)}, u32[]{:S(2)}) collective-permute-start(f32[4,48,128]{2,1,0:T(8,128)S(1)} %y_stack.1.refs_0_), channel_id=1, source_target_pairs={{0,16},{16,32},{32,48},{48,0},{1,17},{17,33},{33,49},{49,1},{2,18}... | collective-permute-start | bytes 294920 | tf_op jit(solution)/shard_map/ppermute | solution.py:550
  93.9 8.2 %collective-permute-start.18 = (f32[4,48,128]{2,1,0:T(8,128)S(1)}, f32[4,48,128]{2,1,0:T(8,128)S(1)}, u32[]{:S(2)}, u32[]{:S(2)}) collective-permute-start(f32[4,48,128]{2,1,0:T(8,128)S(1)} %y_stack.1.refs_0_), channel_id=1, source_target_pairs={{0,32},{16,48},{32,0},{48,16},{1,33},{17,49},{33,1},{49,17},{2,34}... | collective-permute-start | bytes 294920 | tf_op jit(solution)/shard_map/ppermute | solution.py:550
  96.8 5.4 %collective-permute-start.19 = (f32[4,48,128]{2,1,0:T(8,128)S(1)}, f32[4,48,128]{2,1,0:T(8,128)S(1)}, u32[]{:S(2)}, u32[]{:S(2)}) collective-permute-start(f32[4,48,128]{2,1,0:T(8,128)S(1)} %y_stack.1.refs_0_), channel_id=1, source_target_pairs={{0,48},{16,0},{32,16},{48,32},{1,49},{17,1},{33,17},{49,33},{2,50}... | collective-permute-start | bytes 294920 | tf_op jit(solution)/shard_map/ppermute | solution.py:550
  102.2 7.4 %collective-permute-start.20 = (f32[4,4,48,128]{3,2,1,0:T(8,128)S(1)}, f32[4,4,48,128]{3,2,1,0:T(8,128)S(1)}, u32[]{:S(2)}, u32[]{:S(2)}) collective-permute-start(f32[4,4,48,128]{3,2,1,0:T(8,128)S(1)} %x_stack.1.mine), channel_id=1, source_target_pairs={{0,64},{64,0},{1,65},{65,1},{2,66},{66,2},{3,67},{67,3},{4,68},{68... | collective-permute-start | bytes 1179656 | tf_op jit(solution)/shard_map/ppermute | solution.py:683

commit v3 on v2

v3 whole, which is shorter than its diff:
```python
import functools

import jax
import jax.numpy as jnp
from jax import lax
from jax.experimental import pallas as pl
from jax.experimental.pallas import tpu as pltpu
from jax.sharding import Mesh
from jax.sharding import PartitionSpec as P

FRAMES = 9
CLIPS = 8
CH = 128
ROWS = 64
COLS = 64
N_SP = 64
SIDE = 4
PAIRS = ROWS // 2
F32 = jnp.float32
BF16 = jnp.bfloat16
VMEM_BYTES = 24 * 1024 * 1024
SCALE = float(2 * CLIPS * FRAMES * ROWS * COLS) ** (-0.5)
HALF = 6 * CH
PIECE = HALF // SIDE

COUNT, EVEN, BACK1, NEXT1, NEXT2, LBACK1, LBACK2, LNEXT1, CORE, AT_X = range(10)
INFO = (8, 128)

FILL = 8
MID = 16
FULL = 32


def dot(a, b):
    return jnp.dot(a, b, preferred_element_type=F32)


def dot_t(a, b):
    return lax.dot_general(a, b, (((0,), (0,)), ((), ())), preferred_element_type=F32)


def steps(block, body):
    def one(n, _):
        body(n * block)
        return 0

    lax.fori_loop(0, PAIRS // block, one, 0)


def clear_edges(wide):
    wide[0, :, 0 : 3 * CH] = jnp.zeros((COLS, 3 * CH), BF16)
    wide[PAIRS, :, 3 * CH : 6 * CH] = jnp.zeros((COLS, 3 * CH), BF16)


def put_row(wide, t, half, a):
    col = lax.broadcasted_iota(jnp.int32, a.shape, 1)
    before = jnp.where(col == 0, 0.0, pltpu.roll(a, 1, 1))
    after = jnp.where(col == COLS - 1, 0.0, pltpu.roll(a, COLS - 1, 1))
    at = pl.ds(t + half, a.shape[0])
    base = 0 if half else 3 * CH
    wide[at, :, base : base + CH] = before.astype(BF16)
    wide[at, :, base + CH : base + 2 * CH] = a.astype(BF16)
    wide[at, :, base + 2 * CH : base + 3 * CH] = after.astype(BF16)


def fill_act(wide, rows):
    def body(t):
        for half in range(2):
            x = rows(t, half).astype(F32)
            put_row(wide, t, half, x * jax.nn.sigmoid(x))

    steps(FILL, body)


def windows(wide, t, block):
    low = wide[pl.ds(t, block)].reshape(block * COLS, 6 * CH)
    high = wide[pl.ds(t + 1, block)].reshape(block * COLS, 6 * CH)
    return low, high


def conv(wide, w_ref, t, block):
    low, high = windows(wide, t, block)
    return dot(low, w_ref[0 : 6 * CH, :]) + dot(high, w_ref[6 * CH : 12 * CH, :])


def conv_to(out_ref, wide, w_ref):
    def body(t):
        out_ref[pl.ds(t, FULL)] = conv(wide, w_ref, t, FULL).astype(BF16).reshape(FULL, COLS, 2 * CH)

    steps(FULL, body)


def pair(v):
    return jnp.concatenate([v[:, 0], v[:, 1]], axis=-1).reshape(v.shape[0] * COLS, 2 * CH)


def flat(v):
    return v.reshape(v.shape[0] * COLS, 2 * CH)


def add_spatial(acc, wide, v_ref):
    def body(t):
        low, high = windows(wide, t, FULL)
        v = flat(v_ref[pl.ds(t, FULL)])
        acc[:, 0 : 6 * CH] += dot_t(v, low)
        acc[:, 6 * CH : 12 * CH] += dot_t(v, high)

    steps(FULL, body)


def correlate(s, gs):
    total = None
    for half in range(2):
        a = s[:, :, half * CH : half * CH + CH].reshape(PAIRS * COLS, CH)
        b = gs(half)
        one = dot_t(a, b.reshape(PAIRS * COLS, b.shape[-1]))
        total = one if total is None else total + one
    return total


def copy_either(first, a, b, sem):
    @pl.when(first)
    def _():
        pltpu.make_async_copy(*a, sem).start()

    @pl.when(jnp.logical_not(first))
    def _():
        pltpu.make_async_copy(*b, sem).start()

    return pltpu.make_async_copy(*a, sem)


def is_two(info):
    return info[0, COUNT] == 2


def is_set(info, n):
    return info[0, n] == 1


def either(first, a, b):
    return lambda *at: jnp.where(first, a[at], b[at])


def prep_kernel(counts, x_hbm, g_hbm, info, high_ref, low_ref, sems):
    here = (lax.axis_index("x") * SIDE + lax.axis_index("y")) * SIDE + lax.axis_index("z")
    even = here % 2 == 0

    def put(source, for_high, sem):
        return copy_either(for_high, (source, high_ref), (source, low_ref), sem)

    down = put(g_hbm.at[0], even, sems.at[0])
    c = counts[...].astype(F32)
    order = lax.broadcasted_iota(jnp.int32, c.shape, 1)
    start = jnp.sum(jnp.where(order < here, c, 0.0)).astype(jnp.int32)
    count = jnp.sum(jnp.where(order == here, c, 0.0)).astype(jnp.int32)
    up = put(x_hbm.at[jnp.where(count == 2, 1, 0)], jnp.logical_not(even), sems.at[1])
    first = start % FRAMES
    second = (first + 1) % FRAMES
    final = FRAMES - 1
    values = {
        COUNT: count,
        EVEN: even.astype(jnp.int32),
        BACK1: (first >= 1).astype(jnp.int32),
        NEXT1: (first + 1 <= final).astype(jnp.int32),
        NEXT2: (first + 2 <= final).astype(jnp.int32),
        LBACK1: (second >= 1).astype(jnp.int32),
        LBACK2: (second >= 2).astype(jnp.int32),
        LNEXT1: (second + 1 <= final).astype(jnp.int32),
        CORE: lax.axis_index("dp"),
        AT_X: lax.axis_index("x"),
    }
    lane = lax.broadcasted_iota(jnp.int32, INFO, 1)
    found = jnp.zeros(INFO, jnp.int32)
    for n, value in values.items():
        found = jnp.where(lane == n, value, found)
    info[...] = found
    down.wait()
    up.wait()


def forward_kernel(info, x_ref, g_ref, w_ref, tw_ref, s_ref, acc, tacc, wf, wb, tf, tb, wide, v_ref, mw):
    zero = jnp.zeros((CH, CH), BF16)
    for a in range(4):
        for q in range(3):
            rows = slice((a * 3 + q) * CH, (a * 3 + q + 1) * CH)
            for b in range(2):
                lanes = slice(b * CH, b * CH + CH)
                inside = 0 <= a - b <= 2
                wf[rows, lanes] = w_ref[a - b, q] if inside else zero
                wb[rows, lanes] = w_ref[2 - (a - b), 2 - q].T if inside else zero
    for k in range(3):
        for a in range(2):
            rows = slice((2 * k + a) * CH, (2 * k + a + 1) * CH)
            for b in range(2):
                lanes = slice(b * CH, b * CH + CH)
                tf[rows, lanes] = tw_ref[k] if a == b else zero
                tb[rows, lanes] = tw_ref[k].T if a == b else zero

    acc[...] = jnp.zeros_like(acc)
    tacc[...] = jnp.zeros_like(tacc)
    clear_edges(wide)
    mw[0 : 2 * CH] = tb[0 : 2 * CH]

    def slot(j, _):
        keep = jnp.logical_and(j == 0, jnp.logical_and(is_two(info), is_set(info, NEXT1)))
        mw[2 * CH : 4 * CH] = jnp.where(keep, tb[2 * CH : 4 * CH], jnp.zeros((2 * CH, 2 * CH), BF16))
        fill_act(wide, lambda t, half: x_ref[j, pl.ds(t, FILL), half])
        conv_to(s_ref.at[j], wide, wf)

        def upstream(t):
            at = pl.ds(t, MID)
            both = jnp.concatenate([pair(g_ref[j, at]), pair(g_ref[1, at])], axis=-1)
            v_ref[at] = dot(both, mw[...]).astype(BF16).reshape(MID, COLS, 2 * CH)

        steps(MID, upstream)
        add_spatial(acc, wide, v_ref)
        found = correlate(s_ref[j], lambda half: jnp.concatenate([g_ref[j, :, half], g_ref[1, :, half]], axis=-1))
        tacc[:, 0:CH] += found[:, 0:CH]
        tacc[:, CH : 2 * CH] += jnp.where(keep, found[:, CH : 2 * CH], 0.0)
        return 0

    lax.fori_loop(0, info[0, COUNT], slot, 0)


def mid_kernel(info, high_in, low_in, s, g, wf, tf, tb, sent, sh, wide, mw):
    two = is_two(info)
    even = is_set(info, EVEN)
    back = is_set(info, BACK1)
    before, after = either(even, high_in, low_in), either(even, low_in, high_in)
    clear_edges(wide)
    fill_act(wide, lambda t, half: before(pl.ds(t, FILL), half))
    conv_to(sh, wide, wf)

    down = jnp.where(even, 0, 1)
    nothing = jnp.zeros((2 * CH, 2 * CH), BF16)
    mw[0 : 2 * CH] = jnp.where(back, tb[2 * CH : 4 * CH], nothing)
    mw[2 * CH : 4 * CH] = jnp.where(jnp.logical_and(back, is_set(info, NEXT1)), tb[4 * CH : 6 * CH], nothing)

    def upstream(t):
        at = pl.ds(t, FULL)
        v = jnp.concatenate([pair(g[0, at]), pair(jnp.where(two, g[1, at], after(at)))], axis=-1)
        sent[down, at] = dot(v, mw[...]).astype(BF16).reshape(FULL, COLS, 2 * CH)

    steps(FULL, upstream)
    keep1 = jnp.where(two, info[0, LNEXT1], info[0, NEXT1]) == 1
    keep2 = jnp.logical_and(keep1, jnp.where(two, info[0, LBACK1], info[0, BACK1]) == 1)
    mw[0 : 2 * CH] = jnp.where(keep1, tf[2 * CH : 4 * CH], nothing)
    mw[2 * CH : 4 * CH] = jnp.where(keep2, tf[4 * CH : 6 * CH], nothing)

    def ahead(t):
        at = pl.ds(t, FULL)
        v = jnp.concatenate([flat(jnp.where(two, s[1, at], s[0, at])), flat(jnp.where(two, s[0, at], sh[at]))], axis=-1)
        sent[1 - down, at] = dot(v, mw[...]).astype(BF16).reshape(FULL, COLS, 2 * CH)

    steps(FULL, ahead)


def grad_kernel(info, high_in, low_in, x, g, s, sent, sh, acc_in, tacc_in, tb, own_ref, other_ref, wide, v, acc, tacc, both):
    two = is_two(info)
    even = is_set(info, EVEN)
    back = is_set(info, BACK1)
    cross = jnp.logical_and(back, is_set(info, NEXT1))
    before, after = either(even, high_in, low_in), either(even, low_in, high_in)
    down = jnp.where(even, 0, 1)
    acc[...] = acc_in[...]
    tacc[...] = tacc_in[...]
    clear_edges(wide)
    fill_act(wide, lambda t, half: before(pl.ds(t, FILL), half))
    add_spatial(acc, wide, sent.at[down])
    rows = slice(None)

    def two_frames(half):
        return jnp.concatenate([g[0, :, half], jnp.where(two, g[1, :, half], after(rows, half))], axis=-1)

    found = correlate(sh[...], two_frames)
    tacc[:, CH : 2 * CH] += jnp.where(back, found[:, 0:CH], 0.0)
    tacc[:, 2 * CH : 3 * CH] += jnp.where(cross, found[:, CH : 2 * CH], 0.0)

    @pl.when(jnp.logical_and(two, is_set(info, NEXT2)))
    def _():
        fill_act(wide, lambda t, half: x[0, pl.ds(t, FILL), half])

        def up(t):
            at = pl.ds(t, MID)
            v[at] = dot(pair(after(at)), tb[4 * CH : 6 * CH]).astype(BF16).reshape(MID, COLS, 2 * CH)

        steps(MID, up)
        add_spatial(acc, wide, v)
        tacc[:, 2 * CH : 3 * CH] += correlate(s[0], lambda half: after(rows, half))

    at_x, core = info[0, AT_X], info[0, CORE]
    for p in range(3):
        for q in range(3):
            first = (p * 3 + q) * CH
            second = ((p + 1) * 3 + q) * CH
            found = acc[0:CH, first : first + CH] + acc[CH : 2 * CH, second : second + CH]
            n = p * 3 + q
            both[n // 6, (n % 6) * CH : (n % 6 + 1) * CH] = found.T * SCALE
    for k in range(3):
        both[1, (3 + k) * CH : (4 + k) * CH] = tacc[:, k * CH : k * CH + CH] * SCALE
    for i in range(SIDE):
        source = pl.ds(pl.multiple_of(lax.rem(at_x + i, SIDE) * PIECE, PIECE), PIECE)
        own_ref[i] = both[core, source]
        other_ref[i] = both[1 - core, source]


def add_x(x, slot, out, to, sem, t, value):
    at = pl.ds(t, MID)
    value = value.astype(BF16).astype(F32).reshape(MID, COLS, 2 * CH)
    for half in range(2):
        out[at, half] = (x[slot, at, half].astype(F32) + value[:, :, half * CH : half * CH + CH]).astype(BF16)
    pltpu.make_async_copy(out.at[at], to.at[at], sem).start()


def mask_taps(mw, taps, keep1, keep2):
    nothing = jnp.zeros((2 * CH, 2 * CH), BF16)
    mw[0 : 2 * CH] = taps[0 : 2 * CH]
    mw[2 * CH : 4 * CH] = jnp.where(keep1, taps[2 * CH : 4 * CH], nothing)
    mw[4 * CH : 6 * CH] = jnp.where(keep2, taps[4 * CH : 6 * CH], nothing)


def input_rows(wide, wb, upstream, x, g, slot, out, to, sem, first, count):
    clear_edges(wide)

    def up(t, n):
        value = upstream(t, n).reshape(n, COLS, 2 * CH)
        for half in range(2):
            put_row(wide, t, half, value[:, :, half * CH : half * CH + CH])

    def up_full(n, _):
        up(first + n * FILL, FILL)
        return 0

    lax.fori_loop(0, count // FILL, up_full, 0)
    if first > 0:
        up(first - 1, 1)
    if first + count < PAIRS:
        up(first + count, 1)

    def down(n, _):
        t = first + n * MID
        at = pl.ds(t, MID)
        back = conv(wide, wb, t, MID).reshape(MID, COLS, 2 * CH)
        for half in range(2):
            xv = x[slot, at, half].astype(F32)
            sig = jax.nn.sigmoid(xv)
            b = back[:, :, half * CH : half * CH + CH]
            out[at, half] = (g[slot, at, half].astype(F32) + b * (sig * (1.0 + xv * (1.0 - sig)))).astype(BF16)
        pltpu.make_async_copy(out.at[at], to.at[at], sem).start()
        return 0

    lax.fori_loop(0, count // MID, down, 0)


def early_out_kernel(info, x, s, sh, tf, after, out_any, token, mw, out, sem):
    to = out_any.at[1]

    @pl.when(is_two(info))
    def _():
        mask_taps(mw, tf, is_set(info, LBACK1), is_set(info, LBACK2))

        def body(t):
            at = pl.ds(t, MID)
            v = jnp.concatenate([flat(s[1, at]), flat(s[0, at]), flat(sh[at])], axis=-1)
            add_x(x, 1, out, to, sem, t, dot(v, mw[...]))

        steps(MID, body)

    @pl.when(jnp.logical_not(is_two(info)))
    def _():
        out[...] = jnp.zeros_like(out)
        pltpu.make_async_copy(out, to, sem).start()

    token[...] = jnp.zeros_like(token)
    pltpu.make_async_copy(out, to, sem).wait()


def early_in_kernel(info, x, g, high_in, low_in, wb, tb, after, out_any, token, mw, wide, out, sem):
    two = is_two(info)
    coming = either(is_set(info, EVEN), low_in, high_in)

    @pl.when(two)
    def _():
        mask_taps(mw, tb, is_set(info, NEXT1), is_set(info, NEXT2))

        def upstream(t, n):
            at = pl.ds(t, n)
            return dot(jnp.concatenate([pair(g[0, at]), pair(g[1, at]), pair(coming(at))], axis=-1), mw[...])

        input_rows(wide, wb, upstream, x, g, 0, out, out_any.at[0], sem, 0, PAIRS)

    @pl.when(jnp.logical_not(two))
    def _():
        out[...] = jnp.zeros_like(out)
        pltpu.make_async_copy(out, out_any.at[1], sem).start()

    token[...] = jnp.zeros_like(token)
    pltpu.make_async_copy(out, out_any.at[1], sem).wait()


def output_kernel(info, x, s, high_in, low_in, tf, early, out_any, token, out, sem):
    ahead = either(is_set(info, EVEN), high_in, low_in)
    to = out_any.at[0]

    def body(t):
        at = pl.ds(t, MID)
        add_x(x, 0, out, to, sem, t, dot(flat(s[0, at]), tf[0 : 2 * CH]) + flat(ahead(at)).astype(F32))

    steps(MID, body)
    token[...] = jnp.zeros_like(token)
    pltpu.make_async_copy(out, to, sem).wait()


def input_kernel(info, x, g, high_in, low_in, wb, tb, early, out_any, token, wide, out, sem, *, first):
    last = jnp.where(is_two(info), 1, 0)
    share = either(is_set(info, EVEN), low_in, high_in)
    to = out_any.at[last]

    def upstream(t, n):
        at = pl.ds(t, n)
        return dot(pair(g[last, at]), tb[0 : 2 * CH]) + flat(share(at)).astype(F32)

    input_rows(wide, wb, upstream, x, g, last, out, to, sem, first, PAIRS // 2)
    token[...] = jnp.zeros_like(token)
    rows = pl.ds(first, PAIRS // 2)
    pltpu.make_async_copy(out.at[rows], to.at[rows], sem).wait()


def place_kernel(info, mine, theirs, spatial, temporal_out):
    at_x, core = info[0, AT_X], info[0, CORE]
    for half in range(2):
        for i in range(SIDE):
            n = lax.rem(at_x + SIDE - i, SIDE)
            piece = jnp.where(core == half, mine[n], theirs[n])
            row = half * HALF + i * PIECE
            if row < 9 * CH:
                spatial[row : row + PIECE] = piece
            else:
                temporal_out[row - 9 * CH : row - 9 * CH + PIECE] = piece


FRAME = (PAIRS, 2, COLS, CH)
S_SHAPE = (PAIRS, COLS, 2 * CH)
WIDE = pltpu.VMEM((PAIRS + 1, COLS, 6 * CH), BF16)
VALUES = pltpu.VMEM(S_SHAPE, BF16)
W_SHAPE = (12 * CH, 2 * CH)
T_SHAPE = (6 * CH, 2 * CH)
TAPS = pltpu.VMEM(T_SHAPE, BF16)
TAPS2 = pltpu.VMEM((4 * CH, 2 * CH), BF16)
ACC = (2 * CH, 12 * CH)
TACC = (CH, 3 * CH)
PIECES = (SIDE, PIECE, CH)
VMEM = pl.BlockSpec(memory_space=pltpu.VMEM)
ANY = pl.BlockSpec(memory_space=pl.ANY)
HBM = pl.BlockSpec(memory_space=pltpu.HBM)
FRAME1 = pltpu.VMEM(FRAME, BF16)
SEM = pltpu.SemaphoreType.DMA
def shape(s, d=BF16):
    return jax.ShapeDtypeStruct(s, d)


def in_hbm(value):
    return pltpu.with_memory_space_constraint(value, pltpu.HBM)


def call(kernel, in_specs, outs, scratch, name, out_specs=None, aliases=None):
    return pl.pallas_call(
        kernel,
        in_specs=in_specs,
        out_specs=out_specs or [VMEM] * len(outs),
        out_shape=outs,
        scratch_shapes=scratch,
        input_output_aliases=aliases or {},
        compiler_params=pltpu.CompilerParams(vmem_limit_bytes=VMEM_BYTES),
        cost_estimate=pl.CostEstimate(flops=1, transcendentals=0, bytes_accessed=1),
        name=name,
    )


def shifts(value, axis, k):
    return lax.ppermute(value, axis, [(i, (i + k) % SIDE) for i in range(SIDE)])


def to_sum(parts, axis):
    return [parts[0]] + [shifts(parts[k], axis, k) for k in range(1, SIDE)]


def gather(part, axis):
    return [part] + [shifts(part, axis, k) for k in range(1, SIDE)]


def split_call(name, n_sum, n_out, out, n_after=0):
    def kernel(*refs):
        ins, outs = refs[:n_sum], refs[n_sum + n_after :]
        for n, out_ref in enumerate(outs):
            v = [r[n] if n_out > 1 else r[...] for r in ins]
            out_ref[...] = v[0] + v[1] if n_sum == 2 else (v[0] + v[2]) + (v[1] + v[3])

    return call(kernel, [VMEM] * n_sum + [ANY] * n_after, [shape(out, F32)] * n_out, [], name)


def stack_call(name, out, n_after):
    def kernel(*refs):
        for n in range(SIDE):
            refs[-1][n] = refs[n][...]

    run = call(kernel, [VMEM] * SIDE + [ANY] * n_after, [shape(out, F32)], [], name)
    return lambda *a: run(*a)[0]


def local(latents, cotangent, frame_counts, spatial_weight, temporal_weight):
    axes = ("x", "y", "z")
    x = latents.reshape((2,) + FRAME)
    g = cotangent.reshape((2,) + FRAME)
    lows = range(0, N_SP, 2)
    low = [(i, i + 1) for i in lows] + [(i + 1, i) for i in lows]
    high = [(i + 1, (i + 2) % N_SP) for i in lows] + [((i + 2) % N_SP, i + 1) for i in lows]
    swap = [(0, 1), (1, 0)]

    info, for_high, for_low = call(
        prep_kernel,
        [VMEM, HBM, HBM],
        [shape(INFO, jnp.int32), shape(FRAME), shape(FRAME)],
        [SEM((2,))],
        "prep",
        [VMEM, ANY, ANY],
    )(frame_counts, in_hbm(x), in_hbm(g))
    high1 = lax.ppermute(for_high, axes, high)
    low1 = lax.ppermute(for_low, axes, low)

    s, acc, tacc, wf, wb, tf, tb = call(
        forward_kernel,
        [VMEM] * 5,
        [shape((2,) + S_SHAPE), shape(ACC, F32), shape(TACC, F32), shape(W_SHAPE), shape(W_SHAPE), shape(T_SHAPE), shape(T_SHAPE)],
        [WIDE, VALUES, TAPS2],
        "forward",
    )(info, x, g, spatial_weight, temporal_weight)

    sent, sh = call(
        mid_kernel, [VMEM] * 8, [shape((2,) + S_SHAPE), shape(S_SHAPE)], [WIDE, TAPS2], "mid"
    )(info, high1, low1, s, g, wf, tf, tb)
    high2 = lax.ppermute(sent[0], axes, high)
    low2 = lax.ppermute(sent[1], axes, low)

    own, other = call(
        grad_kernel,
        [VMEM] * 11,
        [shape(PIECES, F32), shape(PIECES, F32)],
        [WIDE, VALUES, pltpu.VMEM(ACC, F32), pltpu.VMEM(TACC, F32), pltpu.VMEM((2, HALF, CH), F32)],
        "grads",
    )(info, high1, low1, x, g, s, sent, sh, acc, tacc, tb)

    chunks = split_call("core_sum", 2, SIDE, PIECES[1:])(own, lax.ppermute(other, "dp", swap))
    frames = [pltpu.HBM((2,) + FRAME, BF16), shape((8, CH), F32)]
    early_out, done_a = call(
        early_out_kernel, [VMEM] * 5 + [ANY], frames, [TAPS, FRAME1, SEM], "early_out", [ANY, VMEM]
    )(info, x, s, sh, tf, chunks[0])
    early_in, done_b = call(
        early_in_kernel, [VMEM] * 7 + [ANY], frames, [TAPS, WIDE, FRAME1, SEM], "early_in", [ANY, VMEM]
    )(info, x, g, high1, low1, wb, tb, chunks[0])
    part = split_call("x_sum", SIDE, 1, PIECES[1:], 2)(*to_sum(chunks, "x"), done_a, done_b)[0]
    block_out, done_c = call(
        output_kernel, [VMEM] * 6 + [ANY], frames, [FRAME1, SEM], "output", [ANY, VMEM], {6: 0}
    )(info, x, s, high2, low2, tf, in_hbm(early_out))
    part = split_call("y_sum", SIDE, 1, PIECES[1:], 1)(*gather(part, "y"), done_c)[0]

    def input_half(first, so_far):
        return call(
            functools.partial(input_kernel, first=first),
            [VMEM] * 7 + [ANY],
            frames,
            [WIDE, FRAME1, SEM],
            "input_grad",
            [ANY, VMEM],
            {7: 0},
        )(info, x, g, high2, low2, wb, tb, in_hbm(so_far))

    input_grad, done_d = input_half(0, early_in)
    part = split_call("z_sum", SIDE, 1, PIECES[1:], 1)(*gather(part, "z"), done_d)[0]
    input_grad, done_e = input_half(PAIRS // 2, input_grad)
    own = stack_call("x_stack", PIECES, 1)(*gather(part, "x"), done_e)
    theirs = lax.ppermute(own, "dp", swap)
    spatial_grad, temporal_grad = call(
        place_kernel, [VMEM, VMEM, VMEM], [shape((9 * CH, CH), F32), shape((3 * CH, CH), F32)], [], "place"
    )(info, own, theirs)
    return (
        block_out.reshape(latents.shape),
        input_grad.reshape(latents.shape),
        spatial_grad.reshape(3, 3, CH, CH),
        temporal_grad.reshape(3, CH, CH),
    )


def solution(mesh):
    chips = Mesh(mesh.devices.reshape(2, SIDE, SIDE, SIDE), ("dp", "x", "y", "z"))
    held = P(("dp", "x", "y", "z"), None, None, None)
    return jax.shard_map(
        local,
        mesh=chips,
        in_specs=(held, held, P("dp", None), P(), P()),
        out_specs=(held, held, P(), P()),
        check_vma=False,
    )
```

time: 111 us -> 102 us (0.919)
  Pallas kernels: 43.5 us -> 26.8 us
  waiting for transfers between devices: 27.3 us -> 38.5 us
  starting transfers between devices: 38.7 us -> 33.3 us
  local copies, waits for them, and re-layouts: 0.66 us -> 2.74 us
    pallas_call x14 -> x13, Pallas kernels: 43.4 us -> 26.7 us  [the longest x1 6.35 us: local(): call(forward_kernel, [VMEM] * 5, [shape((2,) + S_SHAPE), shape(ACC, F32),...]
    ppermute x15 -> x12, waiting for transfers between devices: 9.5 us -> 20.3 us  [shifts(): return lax.ppermute(value, axis, [(i, (i + k) % SIDE) for i in range(SIDE)])]
    ppermute x15 -> x12, starting transfers between devices: 15.6 us -> 9.38 us  [shifts(): return lax.ppermute(value, axis, [(i, (i + k) % SIDE) for i in range(SIDE)])]
    unnamed x6 -> x10, local copies, waits for them, and re-layouts: 0.66 us -> 2.5 us
  transfers between devices with their start and end apart: 21 -> 18, of which waited for: 6 -> 13; matrix products, arithmetic and copies ran while one was open for 0% -> 0% of each run, Pallas kernels for 34% -> 19%
where the time goes in v3:
time: 102 us
  waiting for transfers between devices  38.5 us (38%)
  starting transfers between devices  33.3 us (33%)
  Pallas kernels  26.8 us (26%)
  local copies, waits for them, and re-layouts  2.74 us (3%)
    ppermute x12, waiting for transfers between devices, shifts(): return lax.ppermute(value, axis, [(i, (i + k) % SIDE) for i in range(SIDE)])  20.3 us
    ppermute x1, waiting for transfers between devices, local(): high1 = lax.ppermute(for_high, axes, high)  14.7 us
    ppermute x12, starting transfers between devices, shifts(): return lax.ppermute(value, axis, [(i, (i + k) % SIDE) for i in range(SIDE)])  9.38 us
    ppermute x1, starting transfers between devices, local(): high1 = lax.ppermute(for_high, axes, high)  9.31 us
    ppermute x1, starting transfers between devices, local(): theirs = lax.ppermute(own, 'dp', swap)  6.82 us
    pallas_call x1, Pallas kernels, local(): call(forward_kernel, [VMEM] * 5, [shape((2,) + S_SHAPE), shape(ACC, F32),...  6.35 us
    pallas_call x2, Pallas kernels, input_half(): call(functools.partial(input_kernel, first=first), [VMEM] * 7 + [ANY], fr...  5.55 us
    ppermute x1, starting transfers between devices, local(): high2 = lax.ppermute(sent[0], axes, high)  5.52 us
  transfers between devices with their start and end apart: 18, of which 13 were waited for; matrix products, arithmetic and copies ran while one was open for 0% of the time, Pallas kernels for 19%

profile of v3, /device:TPU:1, one launch (start us, length us, event | category | flops | bytes accessed | tf_op | source)
XLA Modules:
  0.0 102.1 jit_solution(4348660584122369298)
XLA Ops:
  1.3 1.7 %prep.1 = (s32[8,128]{1,0:T(8,128)S(1)}, bf16[32,2,64,128]{3,2,1,0:T(8,128)(2,1)S(1)}, bf16[32,2,64,128]{3,2,1,0:T(8,128)(2,1)S(1)}) custom-call(s32[1,64]{1,0:T(1,128)S(1)} %copy-done.4, bf16[2,32,2,64,128]{4,3,2,1,0:T(8,128)(2,1)} %bitcast.10, bf16[2,32,2,64,128]{4,3,2,1,0:T(8,128)(2,1)} %bitcast.18), custom_call_target="tpu_custom_call" | custom-call | flops 1 | bytes 1 | tf_op jit(solution)/shard_map/prep/pallas_call | solution.py:521
  3.0 9.3 %collective-permute-start = (bf16[32,2,64,128]{3,2,1,0:T(8,128)(2,1)S(1)}, bf16[32,2,64,128]{3,2,1,0:T(8,128)(2,1)S(1)}, u32[]{:S(2)}, u32[]{:S(2)}) collective-permute-start(bf16[32,2,64,128]{3,2,1,0:T(8,128)(2,1)S(1)} %get-tuple-element.36), channel_id=1, source_target_pairs={{1,2},{3,4},{5,6},{7,8},{9,10},{11,12},{13,14},{15,16},{17,18},{19... | collective-permute-start | bytes 3145736 | tf_op jit(solution)/shard_map/ppermute | solution.py:529
  12.3 1.0 copy-done.2
  13.3 0.9 copy-done.3
  14.2 6.3 %forward.1 = (bf16[2,32,64,256]{3,2,1,0:T(8,128)(2,1)S(1)}, f32[256,1536]{1,0:T(8,128)S(1)}, f32[128,384]{1,0:T(8,128)S(1)}, bf16[1536,256]{1,0:T(8,128)(2,1)S(1...) custom-call(s32[8,128]{1,0:T(8,128)S(1)} %get-tuple-element.34.info, ...), custom_call_target="tpu_custom_call" | custom-call | flops 1 | bytes 1 | tf_op jit(solution)/shard_map/forward/pallas_call | solution.py:532
  20.6 14.7 %collective-permute-done.high_in = bf16[32,2,64,128]{3,2,1,0:T(8,128)(2,1)S(1)} collective-permute-done((bf16[32,2,64,128]{3,2,1,0:T(8,128)(2,1)S(1)}, bf16[32,2,64,128]{3,2,1,0:T(8,128)(2,1)S(1)}, u32[]{:S(2)}, u32[]{:S(2)}) %collective-permute-start) | collective-permute-done | bytes 1048608 | tf_op jit(solution)/shard_map/ppermute | solution.py:529
  35.2 0.8 collective-permute-done.1.low_in
  36.0 4.2 %mid.1 = (bf16[2,32,64,256]{3,2,1,0:T(8,128)(2,1)S(1)}, bf16[32,64,256]{2,1,0:T(8,128)(2,1)S(1)}) custom-call(s32[8,128]{1,0:T(8,128)S(1)} %get-tuple-element.34.info, bf16[32,2,64,128]{3,2,1,0:T(8,128)(2,1)S(1)} %collective-permute-done.high_in, bf16[32,2,64,128]{3,2,1,0:T(8,128)(2,1)S(1)} %collective-permute-done.1.low_in, ...), custom_call_target="tpu_custom_call" | custom-call | flops 1 | bytes 1 | tf_op jit(solution)/shard_map/mid/pallas_call | solution.py:540
  40.9 5.5 %collective-permute-start.2 = (bf16[32,64,256]{2,1,0:T(8,128)(2,1)S(1)}, bf16[32,64,256]{2,1,0:T(8,128)(2,1)S(1)}, u32[]{:S(2)}, u32[]{:S(2)}) collective-permute-start(bf16[32,64,256]{2,1,0:T(8,128)(2,1)S(1)} %get-tuple-element.65), channel_id=1, source_target_pairs={{1,2},{3,4},{5,6},{7,8},{9,10},{11,12},{13,14},{15,16},{17,18},{19... | collective-permute-start | bytes 3145736 | tf_op jit(solution)/shard_map/ppermute | solution.py:543
  46.4 3.7 %grads.1 = (f32[4,192,128]{2,1,0:T(8,128)S(1)}, f32[4,192,128]{2,1,0:T(8,128)S(1)}) custom-call(s32[8,128]{1,0:T(8,128)S(1)} %get-tuple-element.34.info, bf16[32,2,64,128]{3,2,1,0:T(8,128)(2,1)S(1)} %collective-permute-done.high_in, bf16[32,2,64,128]{3,2,1,0:T(8,128)(2,1)S(1)} %collective-permute-done.1.low_in, bf16[2,32,2,64,128]{4,3,2,1,0:T(8,128)(2,1)S(1)} %bitcast.12, ...), custom_call_target="tpu_custom_call" | custom-call | flops 1 | bytes 1 | tf_op jit(solution)/shard_map/grads/pallas_call | solution.py:546
  50.1 1.9 %collective-permute-start.4 = (f32[4,192,128]{2,1,0:T(8,128)S(1)}, f32[4,192,128]{2,1,0:T(8,128)S(1)}, u32[]{:S(2)}, u32[]{:S(2)}) collective-permute-start(f32[4,192,128]{2,1,0:T(8,128)S(1)} %get-tuple-element.46), channel_id=1, source_target_pairs={{0,64},{64,0},{1,65},{65,1},{2,66},{66,2},{3,67},{67,3},{4,68},{68... | collective-permute-start | bytes 1179656 | tf_op jit(solution)/shard_map/ppermute | solution.py:554
  52.0 1.3 %collective-permute-done.4.refs_1_ = f32[4,192,128]{2,1,0:T(8,128)S(1)} collective-permute-done((f32[4,192,128]{2,1,0:T(8,128)S(1)}, f32[4,192,128]{2,1,0:T(8,128)S(1)}, u32[]{:S(2)}, u32[]{:S(2)}) %collective-permute-start.4) | collective-permute-done | bytes 393248 | tf_op jit(solution)/shard_map/ppermute | solution.py:554
  54.0 2.2 %collective-permute-start.7 = (f32[192,128]{1,0:T(8,128)S(1)}, f32[192,128]{1,0:T(8,128)S(1)}, u32[]{:S(2)}, u32[]{:S(2)}) collective-permute-start(f32[192,128]{1,0:T(8,128)S(1)} %get-tuple-element.56), channel_id=1, source_target_pairs={{0,48},{16,0},{32,16},{48,32},{1,49},{17,1},{33,17},{49,33},{2,50}... | collective-permute-start | bytes 294920 | tf_op jit(solution)/shard_map/ppermute | solution.py:482
  56.2 1.2 %early_out.1 = (bf16[2,32,2,64,128]{4,3,2,1,0:T(8,128)(2,1)}, f32[8,128]{1,0:T(8,128)S(1)}) custom-call(s32[8,128]{1,0:T(8,128)S(1)} %get-tuple-element.34.info, bf16[2,32,2,64,128]{4,3,2,1,0:T(8,128)(2,1)S(1)} %bitcast.13, bf16[2,32,64,256]{3,2,1,0:T(8,128)(2,1)S(1)} %get-tuple-element.35.s, bf16[32,64,256]{2,1,0:T(8,128)(2,1)S(1)} %get-tuple-element.42.sh, ...), custom_call_target="tpu_custom_call" | custom-call | flops 1 | bytes 1 | tf_op jit(solution)/shard_map/early_out/pallas_call | solution.py:556
  57.4 1.2 %early_in.1 = (bf16[2,32,2,64,128]{4,3,2,1,0:T(8,128)(2,1)}, f32[8,128]{1,0:T(8,128)S(1)}) custom-call(s32[8,128]{1,0:T(8,128)S(1)} %get-tuple-element.34.info, bf16[2,32,2,64,128]{4,3,2,1,0:T(8,128)(2,1)S(1)} %bitcast.14, bf16[2,32,2,64,128]{4,3,2,1,0:T(8,128)(2,1)S(1)} %bitcast.22, bf16[32,2,64,128]{3,2,1,0:T(8,128)(2,1)S(1)} %collective-permute-done.high_in, ...), custom_call_target="tpu_custom_call" | custom-call | flops 1 | bytes 1 | tf_op jit(solution)/shard_map/early_in/pallas_call | solution.py:559
  58.6 2.6 %collective-permute-done.5.refs_1_ = f32[192,128]{1,0:T(8,128)S(1)} collective-permute-done((f32[192,128]{1,0:T(8,128)S(1)}, f32[192,128]{1,0:T(8,128)S(1)}, u32[]{:S(2)}, u32[]{:S(2)}) %collective-permute-start.5) | collective-permute-done | bytes 98336 | tf_op jit(solution)/shard_map/ppermute | solution.py:482
  61.2 10.2 %collective-permute-done.7.refs_3_ = f32[192,128]{1,0:T(8,128)S(1)} collective-permute-done((f32[192,128]{1,0:T(8,128)S(1)}, f32[192,128]{1,0:T(8,128)S(1)}, u32[]{:S(2)}, u32[]{:S(2)}) %collective-permute-start.7) | collective-permute-done | bytes 98336 | tf_op jit(solution)/shard_map/ppermute | solution.py:482
  71.6 1.4 %collective-permute-start.8 = (f32[192,128]{1,0:T(8,128)S(1)}, f32[192,128]{1,0:T(8,128)S(1)}, u32[]{:S(2)}, u32[]{:S(2)}) collective-permute-start(f32[192,128]{1,0:T(8,128)S(1)} %x_sum.1.refs_0_), channel_id=1, source_target_pairs={{0,4},{4,8},{8,12},{12,0},{1,5},{5,9},{9,13},{13,1},{2,6},{6,10},{... | collective-permute-start | bytes 294920 | tf_op jit(solution)/shard_map/ppermute | solution.py:482
  72.9 1.7 %output.1 = (bf16[2,32,2,64,128]{4,3,2,1,0:T(8,128)(2,1)}, f32[8,128]{1,0:T(8,128)S(1)}) custom-call(s32[8,128]{1,0:T(8,128)S(1)} %get-tuple-element.34.info, bf16[2,32,2,64,128]{4,3,2,1,0:T(8,128)(2,1)S(1)} %bitcast.15, bf16[2,32,64,256]{3,2,1,0:T(8,128)(2,1)S(1)} %get-tuple-element.35.s, ...), custom_call_target="tpu_custom_call", output_to_operand_aliasing={{0}: (6, {})} | custom-call | flops 1 | bytes 1 | tf_op jit(solution)/shard_map/output/pallas_call | solution.py:563
  74.9 1.6 %collective-permute-done.9.refs_2_ = f32[192,128]{1,0:T(8,128)S(1)} collective-permute-done((f32[192,128]{1,0:T(8,128)S(1)}, f32[192,128]{1,0:T(8,128)S(1)}, u32[]{:S(2)}, u32[]{:S(2)}) %collective-permute-start.9) | collective-permute-done | bytes 98336 | tf_op jit(solution)/shard_map/ppermute | solution.py:482
  76.6 1.0 %collective-permute-done.8.refs_1_ = f32[192,128]{1,0:T(8,128)S(1)} collective-permute-done((f32[192,128]{1,0:T(8,128)S(1)}, f32[192,128]{1,0:T(8,128)S(1)}, u32[]{:S(2)}, u32[]{:S(2)}) %collective-permute-start.8) | collective-permute-done | bytes 98336 | tf_op jit(solution)/shard_map/ppermute | solution.py:482
  77.6 1.3 %collective-permute-start.13 = (f32[192,128]{1,0:T(8,128)S(1)}, f32[192,128]{1,0:T(8,128)S(1)}, u32[]{:S(2)}, u32[]{:S(2)}) collective-permute-start(f32[192,128]{1,0:T(8,128)S(1)} %y_sum.1.refs_0_), channel_id=1, source_target_pairs={{0,3},{1,0},{2,1},{3,2},{4,7},{5,4},{6,5},{7,6},{8,11},{9,8},{10,9... | collective-permute-start | bytes 294920 | tf_op jit(solution)/shard_map/ppermute | solution.py:482
  78.9 0.7 collective-permute-start.11
  79.6 2.8 %input_grad.2 = (bf16[2,32,2,64,128]{4,3,2,1,0:T(8,128)(2,1)}, f32[8,128]{1,0:T(8,128)S(1)}) custom-call(s32[8,128]{1,0:T(8,128)S(1)} %get-tuple-element.34.info, bf16[2,32,2,64,128]{4,3,2,1,0:T(8,128)(2,1)S(1)} %bitcast.16, bf16[2,32,2,64,128]{4,3,2,1,0:T(8,128)(2,1)S(1)} %bitcast.23, ...), custom_call_target="tpu_custom_call", output_to_operand_aliasing={{0}: (7, {})} | custom-call | flops 1 | bytes 1 | tf_op jit(solution)/shard_map/input_grad/pallas_call | solution.py:569
  82.4 1.6 %collective-permute-done.12.refs_2_ = f32[192,128]{1,0:T(8,128)S(1)} collective-permute-done((f32[192,128]{1,0:T(8,128)S(1)}, f32[192,128]{1,0:T(8,128)S(1)}, u32[]{:S(2)}, u32[]{:S(2)}) %collective-permute-start.12) | collective-permute-done | bytes 98336 | tf_op jit(solution)/shard_map/ppermute | solution.py:482
  84.6 2.5 %collective-permute-start.16 = (f32[192,128]{1,0:T(8,128)S(1)}, f32[192,128]{1,0:T(8,128)S(1)}, u32[]{:S(2)}, u32[]{:S(2)}) collective-permute-start(f32[192,128]{1,0:T(8,128)S(1)} %z_sum.1.refs_0_), channel_id=1, source_target_pairs={{0,48},{16,0},{32,16},{48,32},{1,49},{17,1},{33,17},{49,33},{2,50}... | collective-permute-start | bytes 294920 | tf_op jit(solution)/shard_map/ppermute | solution.py:482
  87.2 0.7 collective-permute-start.14
  87.8 2.8 %input_grad.3 = (bf16[2,32,2,64,128]{4,3,2,1,0:T(8,128)(2,1)}, f32[8,128]{1,0:T(8,128)S(1)}) custom-call(s32[8,128]{1,0:T(8,128)S(1)} %get-tuple-element.34.info, bf16[2,32,2,64,128]{4,3,2,1,0:T(8,128)(2,1)S(1)} %bitcast.17, bf16[2,32,2,64,128]{4,3,2,1,0:T(8,128)(2,1)S(1)} %bitcast.24, ...), custom_call_target="tpu_custom_call", output_to_operand_aliasing={{0}: (7, {})} | custom-call | flops 1 | bytes 1 | tf_op jit(solution)/shard_map/input_grad/pallas_call | solution.py:569
  90.6 1.6 %collective-permute-done.15.refs_2_ = f32[192,128]{1,0:T(8,128)S(1)} collective-permute-done((f32[192,128]{1,0:T(8,128)S(1)}, f32[192,128]{1,0:T(8,128)S(1)}, u32[]{:S(2)}, u32[]{:S(2)}) %collective-permute-start.15) | collective-permute-done | bytes 98336 | tf_op jit(solution)/shard_map/ppermute | solution.py:482
  92.9 6.8 %collective-permute-start.17 = (f32[4,192,128]{2,1,0:T(8,128)S(1)}, f32[4,192,128]{2,1,0:T(8,128)S(1)}, u32[]{:S(2)}, u32[]{:S(2)}) collective-permute-start(f32[4,192,128]{2,1,0:T(8,128)S(1)} %x_stack.1.mine), channel_id=1, source_target_pairs={{0,64},{64,0},{1,65},{65,1},{2,66},{66,2},{3,67},{67,3},{4,68},{68... | collective-permute-start | bytes 1179656 | tf_op jit(solution)/shard_map/ppermute | solution.py:583
  99.7 1.3 %collective-permute-done.17.theirs = f32[4,192,128]{2,1,0:T(8,128)S(1)} collective-permute-done((f32[4,192,128]{2,1,0:T(8,128)S(1)}, f32[4,192,128]{2,1,0:T(8,128)S(1)}, u32[]{:S(2)}, u32[]{:S(2)}) %collective-permute-start.17) | collective-permute-done | bytes 393248 | tf_op jit(solution)/shard_map/ppermute | solution.py:583
  101.1 1.0 %place.1 = (f32[1152,128]{1,0:T(8,128)}, f32[384,128]{1,0:T(8,128)}) custom-call(s32[8,128]{1,0:T(8,128)S(1)} %get-tuple-element.34.info, f32[4,192,128]{2,1,0:T(8,128)S(1)} %x_stack.1.mine, f32[4,192,128]{2,1,0:T(8,128)S(1)} %collective-permute-done.17.theirs), custom_call_target="tpu_custom_call" | custom-call | flops 1 | bytes 1 | tf_op jit(solution)/shard_map/place/pallas_call | solution.py:584
  (30 shorter events, 3.9 us)
Async XLA Ops:
  0.6 0.7 copy-start.4
  1.3 11.0 %copy-start = (bf16[2,64,64,128]{3,2,1,0:T(8,128)(2,1)S(1)}, bf16[2,64,64,128]{3,2,1,0:T(8,128)(2,1)}, u32[]{:S(2)}) copy-start(bf16[2,64,64,128]{3,2,1,0:T(8,128)(2,1)} %param.5) | copy-start | bytes 6291460
  1.3 11.0 %copy-start.1 = (bf16[2,64,64,128]{3,2,1,0:T(8,128)(2,1)S(1)}, bf16[2,64,64,128]{3,2,1,0:T(8,128)(2,1)}, u32[]{:S(2)}) copy-start(bf16[2,64,64,128]{3,2,1,0:T(8,128)(2,1)} %param.6) | copy-start | bytes 6291460
  3.0 32.2 %collective-permute-start = (bf16[32,2,64,128]{3,2,1,0:T(8,128)(2,1)S(1)}, bf16[32,2,64,128]{3,2,1,0:T(8,128)(2,1)S(1)}, u32[]{:S(2)}, u32[]{:S(2)}) collective-permute-start(bf16[32,2,64,128]{3,2,1,0:T(8,128)(2,1)S(1)} %get-tuple-element.36), channel_id=1, source_target_pairs={{1,2},{3,4},{5,6},{7,8},{9,10},{11,12},{13,14},{15,16},{17,18},{19... | collective-permute-start | bytes 3145736 | tf_op jit(solution)/shard_map/ppermute | solution.py:529
  12.3 23.7 %collective-permute-start.1 = (bf16[32,2,64,128]{3,2,1,0:T(8,128)(2,1)S(1)}, bf16[32,2,64,128]{3,2,1,0:T(8,128)(2,1)S(1)}, u32[]{:S(2)}, u32[]{:S(2)}) collective-permute-start(bf16[32,2,64,128]{3,2,1,0:T(8,128)(2,1)S(1)} %get-tuple-element.37), channel_id=1, source_target_pairs={{0,1},{2,3},{4,5},{6,7},{8,9},{10,11},{12,13},{14,15},{16,17},{18,... | collective-permute-start | bytes 3145736 | tf_op jit(solution)/shard_map/ppermute | solution.py:530
  12.3 1.0 copy-start.2
  13.3 0.9 copy-start.3
  40.5 32.5 %collective-permute-start.3 = (bf16[32,64,256]{2,1,0:T(8,128)(2,1)S(1)}, bf16[32,64,256]{2,1,0:T(8,128)(2,1)S(1)}, u32[]{:S(2)}, u32[]{:S(2)}) collective-permute-start(bf16[32,64,256]{2,1,0:T(8,128)(2,1)S(1)} %get-tuple-element.64), channel_id=1, source_target_pairs={{0,1},{2,3},{4,5},{6,7},{8,9},{10,11},{12,13},{14,15},{16,17},{18,... | collective-permute-start | bytes 3145736 | tf_op jit(solution)/shard_map/ppermute | solution.py:544
  40.9 32.1 %collective-permute-start.2 = (bf16[32,64,256]{2,1,0:T(8,128)(2,1)S(1)}, bf16[32,64,256]{2,1,0:T(8,128)(2,1)S(1)}, u32[]{:S(2)}, u32[]{:S(2)}) collective-permute-start(bf16[32,64,256]{2,1,0:T(8,128)(2,1)S(1)} %get-tuple-element.65), channel_id=1, source_target_pairs={{1,2},{3,4},{5,6},{7,8},{9,10},{11,12},{13,14},{15,16},{17,18},{19... | collective-permute-start | bytes 3145736 | tf_op jit(solution)/shard_map/ppermute | solution.py:543
  50.1 3.3 %collective-permute-start.4 = (f32[4,192,128]{2,1,0:T(8,128)S(1)}, f32[4,192,128]{2,1,0:T(8,128)S(1)}, u32[]{:S(2)}, u32[]{:S(2)}) collective-permute-start(f32[4,192,128]{2,1,0:T(8,128)S(1)} %get-tuple-element.46), channel_id=1, source_target_pairs={{0,64},{64,0},{1,65},{65,1},{2,66},{66,2},{3,67},{67,3},{4,68},{68... | collective-permute-start | bytes 1179656 | tf_op jit(solution)/shard_map/ppermute | solution.py:554
  53.4 7.7 %collective-permute-start.5 = (f32[192,128]{1,0:T(8,128)S(1)}, f32[192,128]{1,0:T(8,128)S(1)}, u32[]{:S(2)}, u32[]{:S(2)}) collective-permute-start(f32[192,128]{1,0:T(8,128)S(1)} %get-tuple-element.54), channel_id=1, source_target_pairs={{0,16},{16,32},{32,48},{48,0},{1,17},{17,33},{33,49},{49,1},{2,18}... | collective-permute-start | bytes 294920 | tf_op jit(solution)/shard_map/ppermute | solution.py:482
  53.5 7.7 %collective-permute-start.6 = (f32[192,128]{1,0:T(8,128)S(1)}, f32[192,128]{1,0:T(8,128)S(1)}, u32[]{:S(2)}, u32[]{:S(2)}) collective-permute-start(f32[192,128]{1,0:T(8,128)S(1)} %get-tuple-element.55), channel_id=1, source_target_pairs={{0,32},{16,48},{32,0},{48,16},{1,33},{17,49},{33,1},{49,17},{2,34}... | collective-permute-start | bytes 294920 | tf_op jit(solution)/shard_map/ppermute | solution.py:482
  54.0 17.3 %collective-permute-start.7 = (f32[192,128]{1,0:T(8,128)S(1)}, f32[192,128]{1,0:T(8,128)S(1)}, u32[]{:S(2)}, u32[]{:S(2)}) collective-permute-start(f32[192,128]{1,0:T(8,128)S(1)} %get-tuple-element.56), channel_id=1, source_target_pairs={{0,48},{16,0},{32,16},{48,32},{1,49},{17,1},{33,17},{49,33},{2,50}... | collective-permute-start | bytes 294920 | tf_op jit(solution)/shard_map/ppermute | solution.py:482
  71.4 3.5 %collective-permute-start.10 = (f32[192,128]{1,0:T(8,128)S(1)}, f32[192,128]{1,0:T(8,128)S(1)}, u32[]{:S(2)}, u32[]{:S(2)}) collective-permute-start(f32[192,128]{1,0:T(8,128)S(1)} %x_sum.1.refs_0_), channel_id=1, source_target_pairs={{0,12},{4,0},{8,4},{12,8},{1,13},{5,1},{9,5},{13,9},{2,14},{6,2},{... | collective-permute-start | bytes 294920 | tf_op jit(solution)/shard_map/ppermute | solution.py:482
  71.5 5.1 %collective-permute-start.9 = (f32[192,128]{1,0:T(8,128)S(1)}, f32[192,128]{1,0:T(8,128)S(1)}, u32[]{:S(2)}, u32[]{:S(2)}) collective-permute-start(f32[192,128]{1,0:T(8,128)S(1)} %x_sum.1.refs_0_), channel_id=1, source_target_pairs={{0,8},{4,12},{8,0},{12,4},{1,9},{5,13},{9,1},{13,5},{2,10},{6,14},... | collective-permute-start | bytes 294920 | tf_op jit(solution)/shard_map/ppermute | solution.py:482
  71.6 6.0 %collective-permute-start.8 = (f32[192,128]{1,0:T(8,128)S(1)}, f32[192,128]{1,0:T(8,128)S(1)}, u32[]{:S(2)}, u32[]{:S(2)}) collective-permute-start(f32[192,128]{1,0:T(8,128)S(1)} %x_sum.1.refs_0_), channel_id=1, source_target_pairs={{0,4},{4,8},{8,12},{12,0},{1,5},{5,9},{9,13},{13,1},{2,6},{6,10},{... | collective-permute-start | bytes 294920 | tf_op jit(solution)/shard_map/ppermute | solution.py:482
  77.6 4.7 %collective-permute-start.13 = (f32[192,128]{1,0:T(8,128)S(1)}, f32[192,128]{1,0:T(8,128)S(1)}, u32[]{:S(2)}, u32[]{:S(2)}) collective-permute-start(f32[192,128]{1,0:T(8,128)S(1)} %y_sum.1.refs_0_), channel_id=1, source_target_pairs={{0,3},{1,0},{2,1},{3,2},{4,7},{5,4},{6,5},{7,6},{8,11},{9,8},{10,9... | collective-permute-start | bytes 294920 | tf_op jit(solution)/shard_map/ppermute | solution.py:482
  78.9 5.1 %collective-permute-start.12 = (f32[192,128]{1,0:T(8,128)S(1)}, f32[192,128]{1,0:T(8,128)S(1)}, u32[]{:S(2)}, u32[]{:S(2)}) collective-permute-start(f32[192,128]{1,0:T(8,128)S(1)} %y_sum.1.refs_0_), channel_id=1, source_target_pairs={{0,2},{1,3},{2,0},{3,1},{4,6},{5,7},{6,4},{7,5},{8,10},{9,11},{10,... | collective-permute-start | bytes 294920 | tf_op jit(solution)/shard_map/ppermute | solution.py:482
  78.9 5.7 %collective-permute-start.11 = (f32[192,128]{1,0:T(8,128)S(1)}, f32[192,128]{1,0:T(8,128)S(1)}, u32[]{:S(2)}, u32[]{:S(2)}) collective-permute-start(f32[192,128]{1,0:T(8,128)S(1)} %y_sum.1.refs_0_), channel_id=1, source_target_pairs={{0,1},{1,2},{2,3},{3,0},{4,5},{5,6},{6,7},{7,4},{8,9},{9,10},{10,1... | collective-permute-start | bytes 294920 | tf_op jit(solution)/shard_map/ppermute | solution.py:482
  84.6 6.0 %collective-permute-start.16 = (f32[192,128]{1,0:T(8,128)S(1)}, f32[192,128]{1,0:T(8,128)S(1)}, u32[]{:S(2)}, u32[]{:S(2)}) collective-permute-start(f32[192,128]{1,0:T(8,128)S(1)} %z_sum.1.refs_0_), channel_id=1, source_target_pairs={{0,48},{16,0},{32,16},{48,32},{1,49},{17,1},{33,17},{49,33},{2,50}... | collective-permute-start | bytes 294920 | tf_op jit(solution)/shard_map/ppermute | solution.py:482
  87.2 5.1 %collective-permute-start.15 = (f32[192,128]{1,0:T(8,128)S(1)}, f32[192,128]{1,0:T(8,128)S(1)}, u32[]{:S(2)}, u32[]{:S(2)}) collective-permute-start(f32[192,128]{1,0:T(8,128)S(1)} %z_sum.1.refs_0_), channel_id=1, source_target_pairs={{0,32},{16,48},{32,0},{48,16},{1,33},{17,49},{33,1},{49,17},{2,34}... | collective-permute-start | bytes 294920 | tf_op jit(solution)/shard_map/ppermute | solution.py:482
  87.2 5.7 %collective-permute-start.14 = (f32[192,128]{1,0:T(8,128)S(1)}, f32[192,128]{1,0:T(8,128)S(1)}, u32[]{:S(2)}, u32[]{:S(2)}) collective-permute-start(f32[192,128]{1,0:T(8,128)S(1)} %z_sum.1.refs_0_), channel_id=1, source_target_pairs={{0,16},{16,32},{32,48},{48,0},{1,17},{17,33},{33,49},{49,1},{2,18}... | collective-permute-start | bytes 294920 | tf_op jit(solution)/shard_map/ppermute | solution.py:482
  92.9 8.2 %collective-permute-start.17 = (f32[4,192,128]{2,1,0:T(8,128)S(1)}, f32[4,192,128]{2,1,0:T(8,128)S(1)}, u32[]{:S(2)}, u32[]{:S(2)}) collective-permute-start(f32[4,192,128]{2,1,0:T(8,128)S(1)} %x_stack.1.mine), channel_id=1, source_target_pairs={{0,64},{64,0},{1,65},{65,1},{2,66},{66,2},{3,67},{67,3},{4,68},{68... | collective-permute-start | bytes 1179656 | tf_op jit(solution)/shard_map/ppermute | solution.py:583

commit v4 on v3

--- a/solution.py
+++ b/solution.py
@@ -29,6 +29,8 @@
 FILL = 8
 MID = 16
 FULL = 32
+CUT1 = 16
+CUT2 = 15
 
 
 def dot(a, b):
@@ -63,13 +65,15 @@
     wide[at, :, base + 2 * CH : base + 3 * CH] = after.astype(BF16)
 
 
-def fill_act(wide, rows):
-    def body(t):
+def put_act(wide, t, half, x):
+    x = x.astype(F32)
+    put_row(wide, t, half, x * jax.nn.sigmoid(x))
+
+
+def fill_act(wide, rows, first=0, count=PAIRS):
+    for t in range(first, first + count, FILL):
         for half in range(2):
-            x = rows(t, half).astype(F32)
-            put_row(wide, t, half, x * jax.nn.sigmoid(x))
-
-    steps(FILL, body)
+            put_act(wide, t, half, rows(t, FILL, half))
 
 
 def windows(wide, t, block):
@@ -111,9 +115,9 @@
 def correlate(s, gs):
     total = None
     for half in range(2):
-        a = s[:, :, half * CH : half * CH + CH].reshape(PAIRS * COLS, CH)
+        a = s[:, :, half * CH : half * CH + CH].reshape(s.shape[0] * COLS, CH)
         b = gs(half)
-        one = dot_t(a, b.reshape(PAIRS * COLS, b.shape[-1]))
+        one = dot_t(a, b.reshape(s.shape[0] * COLS, b.shape[-1]))
         total = one if total is None else total + one
     return total
 
@@ -142,19 +146,38 @@
     return lambda *at: jnp.where(first, a[at], b[at])
 
 
-def prep_kernel(counts, x_hbm, g_hbm, info, high_ref, low_ref, sems):
+def halves(first, a, b, cut):
+    parts = (either(first, a[0], b[0]), either(first, a[1], b[1]))
+
+    def read(t, n, *at):
+        found = []
+        if t < cut:
+            found.append(parts[0](pl.ds(t, min(n, cut - t)), *at))
+        if t + n > cut:
+            start = max(t, cut)
+            found.append(parts[1](pl.ds(start - cut, t + n - start), *at))
+        return found[0] if len(found) == 1 else jnp.concatenate(found, axis=0)
+
+    return read
+
+
+def prep_kernel(counts, x_hbm, g_hbm, info, high_a, low_a, high_b, low_b, sems):
     here = (lax.axis_index("x") * SIDE + lax.axis_index("y")) * SIDE + lax.axis_index("z")
     even = here % 2 == 0
 
-    def put(source, for_high, sem):
-        return copy_either(for_high, (source, high_ref), (source, low_ref), sem)
-
-    down = put(g_hbm.at[0], even, sems.at[0])
+    top, bottom = pl.ds(0, CUT1), pl.ds(CUT1, PAIRS - CUT1)
+
+    def put(source, slot, for_high, n):
+        a = copy_either(for_high, (source.at[slot, top], high_a), (source.at[slot, top], low_a), sems.at[n])
+        b = copy_either(for_high, (source.at[slot, bottom], high_b), (source.at[slot, bottom], low_b), sems.at[n + 1])
+        return [a, b]
+
+    copies = put(g_hbm, 0, even, 0)
     c = counts[...].astype(F32)
     order = lax.broadcasted_iota(jnp.int32, c.shape, 1)
     start = jnp.sum(jnp.where(order < here, c, 0.0)).astype(jnp.int32)
     count = jnp.sum(jnp.where(order == here, c, 0.0)).astype(jnp.int32)
-    up = put(x_hbm.at[jnp.where(count == 2, 1, 0)], jnp.logical_not(even), sems.at[1])
+    copies += put(x_hbm, jnp.where(count == 2, 1, 0), jnp.logical_not(even), 2)
     first = start % FRAMES
     second = (first + 1) % FRAMES
     final = FRAMES - 1
@@ -175,8 +198,8 @@
     for n, value in values.items():
         found = jnp.where(lane == n, value, found)
     info[...] = found
-    down.wait()
-    up.wait()
+    for c in copies:
+        c.wait()
 
 
 def forward_kernel(info, x_ref, g_ref, w_ref, tw_ref, s_ref, acc, tacc, wf, wb, tf, tb, wide, v_ref, mw):
@@ -205,7 +228,7 @@
     def slot(j, _):
         keep = jnp.logical_and(j == 0, jnp.logical_and(is_two(info), is_set(info, NEXT1)))
         mw[2 * CH : 4 * CH] = jnp.where(keep, tb[2 * CH : 4 * CH], jnp.zeros((2 * CH, 2 * CH), BF16))
-        fill_act(wide, lambda t, half: x_ref[j, pl.ds(t, FILL), half])
+        fill_act(wide, lambda t, n, half: x_ref[j, pl.ds(t, n), half])
         conv_to(s_ref.at[j], wide, wf)
 
         def upstream(t):
@@ -223,71 +246,82 @@
     lax.fori_loop(0, info[0, COUNT], slot, 0)
 
 
-def mid_kernel(info, high_in, low_in, s, g, wf, tf, tb, sent, sh, wide, mw):
+def mid_kernel(info, *refs, first, count):
+    *hops, s, g, wf, tf, tb, sent, sh, wide, mw = refs
+    if len(hops) == 2:
+        hops = hops * 2
     two = is_two(info)
     even = is_set(info, EVEN)
     back = is_set(info, BACK1)
-    before, after = either(even, high_in, low_in), either(even, low_in, high_in)
+    before = halves(even, hops[0::2], hops[1::2], CUT1)
+    after = halves(even, hops[1::2], hops[0::2], CUT1)
     clear_edges(wide)
-    fill_act(wide, lambda t, half: before(pl.ds(t, FILL), half))
-    conv_to(sh, wide, wf)
+    done = max(first - 1, 0)
+    end = min(first + count + 1, PAIRS)
+    while done < end:
+        n = min(FILL - done % FILL, end - done)
+        for half in range(2):
+            put_act(wide, done, half, before(done, n, half))
+        done += n
+    sh[...] = conv(wide, wf, first, count).astype(BF16).reshape(count, COLS, 2 * CH)
 
     down = jnp.where(even, 0, 1)
+    at = pl.ds(first, count)
     nothing = jnp.zeros((2 * CH, 2 * CH), BF16)
     mw[0 : 2 * CH] = jnp.where(back, tb[2 * CH : 4 * CH], nothing)
     mw[2 * CH : 4 * CH] = jnp.where(jnp.logical_and(back, is_set(info, NEXT1)), tb[4 * CH : 6 * CH], nothing)
-
-    def upstream(t):
-        at = pl.ds(t, FULL)
-        v = jnp.concatenate([pair(g[0, at]), pair(jnp.where(two, g[1, at], after(at)))], axis=-1)
-        sent[down, at] = dot(v, mw[...]).astype(BF16).reshape(FULL, COLS, 2 * CH)
-
-    steps(FULL, upstream)
+    v = jnp.concatenate([pair(g[0, at]), pair(jnp.where(two, g[1, at], after(first, count)))], axis=-1)
+    sent[down] = dot(v, mw[...]).astype(BF16).reshape(count, COLS, 2 * CH)
+
     keep1 = jnp.where(two, info[0, LNEXT1], info[0, NEXT1]) == 1
     keep2 = jnp.logical_and(keep1, jnp.where(two, info[0, LBACK1], info[0, BACK1]) == 1)
     mw[0 : 2 * CH] = jnp.where(keep1, tf[2 * CH : 4 * CH], nothing)
     mw[2 * CH : 4 * CH] = jnp.where(keep2, tf[4 * CH : 6 * CH], nothing)
-
-    def ahead(t):
-        at = pl.ds(t, FULL)
-        v = jnp.concatenate([flat(jnp.where(two, s[1, at], s[0, at])), flat(jnp.where(two, s[0, at], sh[at]))], axis=-1)
-        sent[1 - down, at] = dot(v, mw[...]).astype(BF16).reshape(FULL, COLS, 2 * CH)
-
-    steps(FULL, ahead)
-
-
-def grad_kernel(info, high_in, low_in, x, g, s, sent, sh, acc_in, tacc_in, tb, own_ref, other_ref, wide, v, acc, tacc, both):
+    v = jnp.concatenate([flat(jnp.where(two, s[1, at], s[0, at])), flat(jnp.where(two, s[0, at], sh[...]))], axis=-1)
+    sent[1 - down] = dot(v, mw[...]).astype(BF16).reshape(count, COLS, 2 * CH)
+
+
+def grad_kernel(
+    info, high_a, low_a, high_b, low_b, x, g, s, sent_a, sent_b, sh_a, sh_b, acc_in, tacc_in, tb, own_ref, other_ref,
+    wide, v, gn, acc, tacc, both
+):
     two = is_two(info)
     even = is_set(info, EVEN)
     back = is_set(info, BACK1)
     cross = jnp.logical_and(back, is_set(info, NEXT1))
-    before, after = either(even, high_in, low_in), either(even, low_in, high_in)
+    before = halves(even, (high_a, high_b), (low_a, low_b), CUT1)
+    after = halves(even, (low_a, low_b), (high_a, high_b), CUT1)
     down = jnp.where(even, 0, 1)
     acc[...] = acc_in[...]
     tacc[...] = tacc_in[...]
     clear_edges(wide)
-    fill_act(wide, lambda t, half: before(pl.ds(t, FILL), half))
-    add_spatial(acc, wide, sent.at[down])
-    rows = slice(None)
-
-    def two_frames(half):
-        return jnp.concatenate([g[0, :, half], jnp.where(two, g[1, :, half], after(rows, half))], axis=-1)
-
-    found = correlate(sh[...], two_frames)
-    tacc[:, CH : 2 * CH] += jnp.where(back, found[:, 0:CH], 0.0)
-    tacc[:, 2 * CH : 3 * CH] += jnp.where(cross, found[:, CH : 2 * CH], 0.0)
+    fill_act(wide, before)
+    for t in range(0, PAIRS, FILL):
+        gn[pl.ds(t, FILL)] = after(t, FILL)
+    for t, sent, sh in ((0, sent_a, sh_a), (CUT2, sent_b, sh_b)):
+        n = sh.shape[0]
+        at = pl.ds(t, n)
+        v[at] = sent[down]
+
+        def two_frames(half, at=at):
+            return jnp.concatenate([g[0, at, half], jnp.where(two, g[1, at, half], gn[at, half])], axis=-1)
+
+        found = correlate(sh[...], two_frames)
+        tacc[:, CH : 2 * CH] += jnp.where(back, found[:, 0:CH], 0.0)
+        tacc[:, 2 * CH : 3 * CH] += jnp.where(cross, found[:, CH : 2 * CH], 0.0)
+    add_spatial(acc, wide, v)
 
     @pl.when(jnp.logical_and(two, is_set(info, NEXT2)))
     def _():
-        fill_act(wide, lambda t, half: x[0, pl.ds(t, FILL), half])
+        fill_act(wide, lambda t, n, half: x[0, pl.ds(t, n), half])
 
         def up(t):
             at = pl.ds(t, MID)
-            v[at] = dot(pair(after(at)), tb[4 * CH : 6 * CH]).astype(BF16).reshape(MID, COLS, 2 * CH)
+            v[at] = dot(pair(gn[at]), tb[4 * CH : 6 * CH]).astype(BF16).reshape(MID, COLS, 2 * CH)
 
         steps(MID, up)
         add_spatial(acc, wide, v)
-        tacc[:, 2 * CH : 3 * CH] += correlate(s[0], lambda half: after(rows, half))
+        tacc[:, 2 * CH : 3 * CH] += correlate(s[0], lambda half: gn[:, half])
 
     at_x, core = info[0, AT_X], info[0, CORE]
     for p in range(3):
@@ -305,9 +339,9 @@
         other_ref[i] = both[1 - core, source]
 
 
-def add_x(x, slot, out, to, sem, t, value):
-    at = pl.ds(t, MID)
-    value = value.astype(BF16).astype(F32).reshape(MID, COLS, 2 * CH)
+def add_x(x, slot, out, to, sem, t, n, value):
+    at = pl.ds(t, n)
+    value = value.astype(BF16).astype(F32).reshape(n, COLS, 2 * CH)
     for half in range(2):
         out[at, half] = (x[slot, at, half].astype(F32) + value[:, :, half * CH : half * CH + CH]).astype(BF16)
     pltpu.make_async_copy(out.at[at], to.at[at], sem).start()
@@ -320,52 +354,34 @@
     mw[4 * CH : 6 * CH] = jnp.where(keep2, taps[4 * CH : 6 * CH], nothing)
 
 
-def input_rows(wide, wb, upstream, x, g, slot, out, to, sem, first, count):
-    clear_edges(wide)
-
-    def up(t, n):
-        value = upstream(t, n).reshape(n, COLS, 2 * CH)
-        for half in range(2):
-            put_row(wide, t, half, value[:, :, half * CH : half * CH + CH])
-
-    def up_full(n, _):
-        up(first + n * FILL, FILL)
-        return 0
-
-    lax.fori_loop(0, count // FILL, up_full, 0)
-    if first > 0:
-        up(first - 1, 1)
-    if first + count < PAIRS:
-        up(first + count, 1)
-
-    def down(n, _):
-        t = first + n * MID
-        at = pl.ds(t, MID)
-        back = conv(wide, wb, t, MID).reshape(MID, COLS, 2 * CH)
-        for half in range(2):
-            xv = x[slot, at, half].astype(F32)
-            sig = jax.nn.sigmoid(xv)
-            b = back[:, :, half * CH : half * CH + CH]
-            out[at, half] = (g[slot, at, half].astype(F32) + b * (sig * (1.0 + xv * (1.0 - sig)))).astype(BF16)
-        pltpu.make_async_copy(out.at[at], to.at[at], sem).start()
-        return 0
-
-    lax.fori_loop(0, count // MID, down, 0)
-
-
-def early_out_kernel(info, x, s, sh, tf, after, out_any, token, mw, out, sem):
+def put_upstream(wide, t, n, value):
+    value = value.reshape(n, COLS, 2 * CH)
+    for half in range(2):
+        put_row(wide, t, half, value[:, :, half * CH : half * CH + CH])
+
+
+def input_rows(wide, wb, x, g, slot, out, to, sem, first, count):
+    at = pl.ds(first, count)
+    back = conv(wide, wb, first, count).reshape(count, COLS, 2 * CH)
+    for half in range(2):
+        xv = x[slot, at, half].astype(F32)
+        sig = jax.nn.sigmoid(xv)
+        b = back[:, :, half * CH : half * CH + CH]
+        out[at, half] = (g[slot, at, half].astype(F32) + b * (sig * (1.0 + xv * (1.0 - sig)))).astype(BF16)
+    pltpu.make_async_copy(out.at[at], to.at[at], sem).start()
+
+
+def early_out_kernel(info, x, s, sh_a, sh_b, tf, after, out_any, token, mw, out, sem):
     to = out_any.at[1]
 
     @pl.when(is_two(info))
     def _():
         mask_taps(mw, tf, is_set(info, LBACK1), is_set(info, LBACK2))
-
-        def body(t):
-            at = pl.ds(t, MID)
-            v = jnp.concatenate([flat(s[1, at]), flat(s[0, at]), flat(sh[at])], axis=-1)
-            add_x(x, 1, out, to, sem, t, dot(v, mw[...]))
-
-        steps(MID, body)
+        for t, sh in ((0, sh_a), (CUT2, sh_b)):
+            n = sh.shape[0]
+            at = pl.ds(t, n)
+            v = jnp.concatenate([flat(s[1, at]), flat(s[0, at]), flat(sh[...])], axis=-1)
+            add_x(x, 1, out, to, sem, t, n, dot(v, mw[...]))
 
     @pl.when(jnp.logical_not(is_two(info)))
     def _():
@@ -376,19 +392,20 @@
     pltpu.make_async_copy(out, to, sem).wait()
 
 
-def early_in_kernel(info, x, g, high_in, low_in, wb, tb, after, out_any, token, mw, wide, out, sem):
+def early_in_kernel(info, x, g, high_a, low_a, high_b, low_b, wb, tb, after, out_any, token, mw, wide, out, sem):
     two = is_two(info)
-    coming = either(is_set(info, EVEN), low_in, high_in)
+    coming = halves(is_set(info, EVEN), (low_a, low_b), (high_a, high_b), CUT1)
 
     @pl.when(two)
     def _():
         mask_taps(mw, tb, is_set(info, NEXT1), is_set(info, NEXT2))
-
-        def upstream(t, n):
-            at = pl.ds(t, n)
-            return dot(jnp.concatenate([pair(g[0, at]), pair(g[1, at]), pair(coming(at))], axis=-1), mw[...])
-
-        input_rows(wide, wb, upstream, x, g, 0, out, out_any.at[0], sem, 0, PAIRS)
+        clear_edges(wide)
+        for t in range(0, PAIRS, FILL):
+            at = pl.ds(t, FILL)
+            v = jnp.concatenate([pair(g[0, at]), pair(g[1, at]), pair(coming(t, FILL))], axis=-1)
+            put_upstream(wide, t, FILL, dot(v, mw[...]))
+        for t in range(0, PAIRS, MID):
+            input_rows(wide, wb, x, g, 0, out, out_any.at[0], sem, t, MID)
 
     @pl.when(jnp.logical_not(two))
     def _():
@@ -399,32 +416,36 @@
     pltpu.make_async_copy(out, out_any.at[1], sem).wait()
 
 
-def output_kernel(info, x, s, high_in, low_in, tf, early, out_any, token, out, sem):
-    ahead = either(is_set(info, EVEN), high_in, low_in)
+def output_kernel(info, x, s, high_a, low_a, high_b, low_b, tf, early, out_any, token, out, sem):
+    ahead = halves(is_set(info, EVEN), (high_a, high_b), (low_a, low_b), CUT2)
     to = out_any.at[0]
-
-    def body(t):
-        at = pl.ds(t, MID)
-        add_x(x, 0, out, to, sem, t, dot(flat(s[0, at]), tf[0 : 2 * CH]) + flat(ahead(at)).astype(F32))
-
-    steps(MID, body)
+    for t, n in ((0, CUT2), (CUT2, PAIRS - CUT2)):
+        value = dot(flat(s[0, pl.ds(t, n)]), tf[0 : 2 * CH]) + flat(ahead(t, n)).astype(F32)
+        add_x(x, 0, out, to, sem, t, n, value)
     token[...] = jnp.zeros_like(token)
     pltpu.make_async_copy(out, to, sem).wait()
 
 
-def input_kernel(info, x, g, high_in, low_in, wb, tb, early, out_any, token, wide, out, sem, *, first):
+def input_kernel(info, x, g, high_a, low_a, high_b, low_b, wb, tb, early, out_any, token, wide, out, sem, *, first):
     last = jnp.where(is_two(info), 1, 0)
-    share = either(is_set(info, EVEN), low_in, high_in)
+    share = halves(is_set(info, EVEN), (low_a, low_b), (high_a, high_b), CUT2)
     to = out_any.at[last]
-
-    def upstream(t, n):
-        at = pl.ds(t, n)
-        return dot(pair(g[last, at]), tb[0 : 2 * CH]) + flat(share(at)).astype(F32)
-
-    input_rows(wide, wb, upstream, x, g, last, out, to, sem, first, PAIRS // 2)
+    clear_edges(wide)
+    done = max(first - 1, 0)
+    end = min(first + MID + 1, PAIRS)
+    while done < end:
+        n = min(FILL - done % FILL, end - done)
+        value = dot(pair(g[last, pl.ds(done, n)]), tb[0 : 2 * CH]) + flat(share(done, n)).astype(F32)
+        put_upstream(wide, done, n, value)
+        done += n
+    input_rows(wide, wb, x, g, last, out, to, sem, first, MID)
     token[...] = jnp.zeros_like(token)
-    rows = pl.ds(first, PAIRS // 2)
+    rows = pl.ds(first, MID)
     pltpu.make_async_copy(out.at[rows], to.at[rows], sem).wait()
+
+
+def hold_kernel(*refs):
+    pass
 
 
 def place_kernel(info, mine, theirs, spatial, temporal_out):
@@ -432,7 +453,7 @@
     for half in range(2):
         for i in range(SIDE):
             n = lax.rem(at_x + SIDE - i, SIDE)
-            piece = jnp.where(core == half, mine[n], theirs[n])
+            piece = jnp.where(core == half, mine[n], theirs[n]).astype(F32)
             row = half * HALF + i * PIECE
             if row < 9 * CH:
                 spatial[row : row + PIECE] = piece
@@ -490,14 +511,15 @@
     return [part] + [shifts(part, axis, k) for k in range(1, SIDE)]
 
 
-def split_call(name, n_sum, n_out, out, n_after=0):
+def split_call(name, n_sum, n_out, out, n_after=0, kind=F32):
     def kernel(*refs):
         ins, outs = refs[:n_sum], refs[n_sum + n_after :]
         for n, out_ref in enumerate(outs):
-            v = [r[n] if n_out > 1 else r[...] for r in ins]
-            out_ref[...] = v[0] + v[1] if n_sum == 2 else (v[0] + v[2]) + (v[1] + v[3])
-
-    return call(kernel, [VMEM] * n_sum + [ANY] * n_after, [shape(out, F32)] * n_out, [], name)
+            v = [(r[n] if n_out > 1 else r[...]).astype(F32) for r in ins]
+            total = v[0] + v[1] if n_sum == 2 else (v[0] + v[2]) + (v[1] + v[3])
+            out_ref[...] = total.astype(kind)
+
+    return call(kernel, [VMEM] * n_sum + [ANY] * n_after, [shape(out, kind)] * n_out, [], name)
 
 
 def stack_call(name, out, n_after):
@@ -505,7 +527,7 @@
         for n in range(SIDE):
             refs[-1][n] = refs[n][...]
 
-    run = call(kernel, [VMEM] * SIDE + [ANY] * n_after, [shape(out, F32)], [], name)
+    run = call(kernel, [VMEM] * SIDE + [ANY] * n_after, [shape(out)], [], name)
     return lambda *a: run(*a)[0]
 
 
@@ -518,16 +540,17 @@
     high = [(i + 1, (i + 2) % N_SP) for i in lows] + [((i + 2) % N_SP, i + 1) for i in lows]
     swap = [(0, 1), (1, 0)]
 
-    info, for_high, for_low = call(
-        prep_kernel,
-        [VMEM, HBM, HBM],
-        [shape(INFO, jnp.int32), shape(FRAME), shape(FRAME)],
-        [SEM((2,))],
-        "prep",
-        [VMEM, ANY, ANY],
+    parts = [shape((n, 2, COLS, CH)) for n in (CUT1, CUT1, PAIRS - CUT1, PAIRS - CUT1)]
+    info, *sent = call(
+        prep_kernel, [VMEM, HBM, HBM], [shape(INFO, jnp.int32)] + parts, [SEM((4,))], "prep", [VMEM] + [ANY] * 4
     )(frame_counts, in_hbm(x), in_hbm(g))
-    high1 = lax.ppermute(for_high, axes, high)
-    low1 = lax.ppermute(for_low, axes, low)
+
+    def hop(for_high, for_low):
+        return lax.ppermute(for_high, axes, high), lax.ppermute(for_low, axes, low)
+
+    hop1_a = hop(*sent[0:2])
+    hop1_b = hop(*sent[2:4])
+    hop1 = hop1_a + hop1_b
 
     s, acc, tacc, wf, wb, tf, tb = call(
         forward_kernel,
@@ -537,47 +560,57 @@
         "forward",
     )(info, x, g, spatial_weight, temporal_weight)
 
-    sent, sh = call(
-        mid_kernel, [VMEM] * 8, [shape((2,) + S_SHAPE), shape(S_SHAPE)], [WIDE, TAPS2], "mid"
-    )(info, high1, low1, s, g, wf, tf, tb)
-    high2 = lax.ppermute(sent[0], axes, high)
-    low2 = lax.ppermute(sent[1], axes, low)
+    def mid(first, count, hops):
+        return call(
+            functools.partial(mid_kernel, first=first, count=count),
+            [VMEM] * (6 + len(hops)),
+            [shape((2, count) + S_SHAPE[1:]), shape((count,) + S_SHAPE[1:])],
+            [WIDE, TAPS2],
+            "mid",
+        )(info, *hops, s, g, wf, tf, tb)
+
+    sent_a, sh_a = mid(0, CUT2, hop1_a)
+    hop2_a = hop(sent_a[0], sent_a[1])
+    sent_b, sh_b = mid(CUT2, PAIRS - CUT2, hop1)
+    hop2_b = hop(sent_b[0], sent_b[1])
+    hop2 = hop2_a + hop2_b
 
     own, other = call(
         grad_kernel,
-        [VMEM] * 11,
+        [VMEM] * 15,
         [shape(PIECES, F32), shape(PIECES, F32)],
-        [WIDE, VALUES, pltpu.VMEM(ACC, F32), pltpu.VMEM(TACC, F32), pltpu.VMEM((2, HALF, CH), F32)],
+        [WIDE, VALUES, FRAME1, pltpu.VMEM(ACC, F32), pltpu.VMEM(TACC, F32), pltpu.VMEM((2, HALF, CH), F32)],
         "grads",
-    )(info, high1, low1, x, g, s, sent, sh, acc, tacc, tb)
-
+    )(info, *hop1, x, g, s, sent_a, sent_b, sh_a, sh_b, acc, tacc, tb)
+
+    other = call(hold_kernel, [ANY] * 3, [shape(PIECES, F32)], [], "hold", [ANY], {2: 0})(*hop2_a, other)[0]
     chunks = split_call("core_sum", 2, SIDE, PIECES[1:])(own, lax.ppermute(other, "dp", swap))
     frames = [pltpu.HBM((2,) + FRAME, BF16), shape((8, CH), F32)]
     early_out, done_a = call(
-        early_out_kernel, [VMEM] * 5 + [ANY], frames, [TAPS, FRAME1, SEM], "early_out", [ANY, VMEM]
-    )(info, x, s, sh, tf, chunks[0])
+        early_out_kernel, [VMEM] * 6 + [ANY], frames, [TAPS, FRAME1, SEM], "early_out", [ANY, VMEM]
+    )(info, x, s, sh_a, sh_b, tf, chunks[0])
     early_in, done_b = call(
-        early_in_kernel, [VMEM] * 7 + [ANY], frames, [TAPS, WIDE, FRAME1, SEM], "early_in", [ANY, VMEM]
-    )(info, x, g, high1, low1, wb, tb, chunks[0])
-    part = split_call("x_sum", SIDE, 1, PIECES[1:], 2)(*to_sum(chunks, "x"), done_a, done_b)[0]
+        early_in_kernel, [VMEM] * 9 + [ANY], frames, [TAPS, WIDE, FRAME1, SEM], "early_in", [ANY, VMEM]
+    )(info, x, g, *hop1, wb, tb, chunks[0])
+    part = split_call("x_sum", SIDE, 1, PIECES[1:], 2, BF16)(*to_sum(chunks, "x"), done_a, done_b)[0]
     block_out, done_c = call(
-        output_kernel, [VMEM] * 6 + [ANY], frames, [FRAME1, SEM], "output", [ANY, VMEM], {6: 0}
-    )(info, x, s, high2, low2, tf, in_hbm(early_out))
-    part = split_call("y_sum", SIDE, 1, PIECES[1:], 1)(*gather(part, "y"), done_c)[0]
+        output_kernel, [VMEM] * 8 + [ANY], frames, [FRAME1, SEM], "output", [ANY, VMEM], {8: 0}
+    )(info, x, s, *hop2, tf, in_hbm(early_out))
+    part = split_call("y_sum", SIDE, 1, PIECES[1:], 1, BF16)(*gather(part, "y"), done_c)[0]
 
     def input_half(first, so_far):
         return call(
             functools.partial(input_kernel, first=first),
-            [VMEM] * 7 + [ANY],
+            [VMEM] * 9 + [ANY],
             frames,
             [WIDE, FRAME1, SEM],
             "input_grad",
             [ANY, VMEM],
-            {7: 0},
-        )(info, x, g, high2, low2, wb, tb, in_hbm(so_far))
+            {9: 0},
+        )(info, x, g, *hop2, wb, tb, in_hbm(so_far))
 
     input_grad, done_d = input_half(0, early_in)
-    part = split_call("z_sum", SIDE, 1, PIECES[1:], 1)(*gather(part, "z"), done_d)[0]
+    part = split_call("z_sum", SIDE, 1, PIECES[1:], 1, BF16)(*gather(part, "z"), done_d)[0]
     input_grad, done_e = input_half(PAIRS // 2, input_grad)
     own = stack_call("x_stack", PIECES, 1)(*gather(part, "x"), done_e)
     theirs = lax.ppermute(own, "dp", swap)

time: 102 us -> 88.4 us (0.87)
  waiting for transfers between devices: 38.5 us -> 17.7 us
  starting transfers between devices: 33.3 us -> 42.2 us
  Pallas kernels: 26.8 us -> 24.7 us
    ppermute x12, waiting for transfers between devices: 20.3 us -> 8.23 us  [shifts(): return lax.ppermute(value, axis, [(i, (i + k) % SIDE) for i in range(SIDE)])]
    ppermute x4 -> x8, waiting for transfers between devices: 15.5 us -> 7.06 us  [the longest x4 5.41 us: hop(): lax.ppermute(for_high, axes, high)]
    ppermute x4 -> x8, starting transfers between devices: 15.2 us -> 22.8 us  [the longest x4 20.8 us: hop(): lax.ppermute(for_high, axes, high)]
    ppermute x12, starting transfers between devices: 9.38 us -> 12.7 us  [shifts(): return lax.ppermute(value, axis, [(i, (i + k) % SIDE) for i in range(SIDE)])]
    ppermute x1, starting transfers between devices: 6.82 us -> 3.59 us  [local(): theirs = lax.ppermute(own, 'dp', swap)]
    pallas_call x11 -> x13, Pallas kernels: 19.3 us -> 18.1 us  [the longest x2 4.66 us: input_half(): call(functools.partial(input_kernel, first=first), [VMEM] * 9 + [ANY], fr...]
    ppermute x1, starting transfers between devices: 1.9 us -> 3.06 us  [local(): lax.ppermute(other, 'dp', swap)]
  transfers between devices with their start and end apart: 18 -> 22, of which waited for: 13 -> 12; matrix products, arithmetic and copies ran while one was open for 0% -> 0% of each run, Pallas kernels for 19% -> 25%
where the time goes in v4:
time: 88.4 us; the launch traced here: 88.2 us
  starting transfers between devices  42.2 us (48%)
  Pallas kernels  24.7 us (28%)
  waiting for transfers between devices  17.7 us (20%)
  local copies, waits for them, and re-layouts  2.71 us (3%)
    ppermute x4, starting transfers between devices, hop(): lax.ppermute(for_high, axes, high)  20.8 us
    ppermute x12, starting transfers between devices, shifts(): return lax.ppermute(value, axis, [(i, (i + k) % SIDE) for i in range(SIDE)])  12.7 us
    ppermute x12, waiting for transfers between devices, shifts(): return lax.ppermute(value, axis, [(i, (i + k) % SIDE) for i in range(SIDE)])  8.23 us
    pallas_call x1, Pallas kernels, local(): call(forward_kernel, [VMEM] * 5, [shape((2,) + S_SHAPE), shape(ACC, F32),...  5.43 us
    ppermute x4, waiting for transfers between devices, hop(): lax.ppermute(for_high, axes, high)  5.41 us
    pallas_call x2, Pallas kernels, input_half(): call(functools.partial(input_kernel, first=first), [VMEM] * 9 + [ANY], fr...  4.66 us
    pallas_call x2, Pallas kernels, mid(): call(functools.partial(mid_kernel, first=first, count=count), [VMEM] * (6...  3.94 us
    pallas_call x1, Pallas kernels, local(): call(grad_kernel, [VMEM] * 15, [shape(PIECES, F32), shape(PIECES, F32)],...  3.75 us
  transfers between devices with their start and end apart: 22, of which 12 were waited for; matrix products, arithmetic and copies ran while one was open for 0% of the time, Pallas kernels for 25%

profile of v4, /device:TPU:1, one launch (start us, length us, event | category | flops | bytes accessed | tf_op | source)
XLA Modules:
  0.0 88.2 jit_solution(10469882408154942477)
XLA Ops:
  1.3 1.7 %prep.1 = (s32[8,128]{1,0:T(8,128)S(1)}, bf16[16,2,64,128]{3,2,1,0:T(8,128)(2,1)S(1)}, bf16[16,2,64,128]{3,2,1,0:T(8,128)(2,1)S(1)}, bf16[16,2,64,128]{3,2,1,0:T(8,128)(2,1)S(1)}, bf16[16,2,64,128]{3,2,1,0:T(8,128)(2,1)S(1)}) custom-call(s32[1,64]{1,0:T(1,128)S(1)} %copy-done.4, bf16[2,32,2,64,128]{4,3,2,1,0:T(8,128)(2,1)} %bitcast.22, ...), custom_call_target="tpu_custom_call" | custom-call | flops 1 | bytes 1 | tf_op jit(solution)/shard_map/prep/pallas_call | solution.py:544
  3.0 9.3 %collective-permute-start = (bf16[16,2,64,128]{3,2,1,0:T(8,128)(2,1)S(1)}, bf16[16,2,64,128]{3,2,1,0:T(8,128)(2,1)S(1)}, u32[]{:S(2)}, u32[]{:S(2)}) collective-permute-start(bf16[16,2,64,128]{3,2,1,0:T(8,128)(2,1)S(1)} %get-tuple-element.40), channel_id=1, source_target_pairs={{1,2},{3,4},{5,6},{7,8},{9,10},{11,12},{13,14},{15,16},{17,18},{19... | collective-permute-start | bytes 1572872 | tf_op jit(solution)/shard_map/ppermute | solution.py:549
  12.5 1.3 %collective-permute-start.5 = (bf16[16,2,64,128]{3,2,1,0:T(8,128)(2,1)S(1)}, bf16[16,2,64,128]{3,2,1,0:T(8,128)(2,1)S(1)}, u32[]{:S(2)}, u32[]{:S(2)}) collective-permute-start(bf16[16,2,64,128]{3,2,1,0:T(8,128)(2,1)S(1)} %get-tuple-element.47), channel_id=1, source_target_pairs={{0,1},{2,3},{4,5},{6,7},{8,9},{10,11},{12,13},{14,15},{16,17},{18,... | collective-permute-start | bytes 1572872 | tf_op jit(solution)/shard_map/ppermute | solution.py:549
  13.8 1.0 %copy-done.2 = bf16[3,3,128,128]{3,2,1,0:T(8,128)(2,1)S(1)} copy-done((bf16[3,3,128,128]{3,2,1,0:T(8,128)(2,1)S(1)}, bf16[3,3,128,128]{3,2,1,0:T(8,128)(2,1)}, u32[]{:S(2)}) %copy-start.2) | copy-done | bytes 294936
  14.8 0.9 %copy-done.3 = bf16[3,128,128]{2,1,0:T(8,128)(2,1)S(1)} copy-done((bf16[3,128,128]{2,1,0:T(8,128)(2,1)S(1)}, bf16[3,128,128]{2,1,0:T(8,128)(2,1)}, u32[]{:S(2)}) %copy-start.3) | copy-done | bytes 98328
  15.6 5.4 %forward.1 = (bf16[2,32,64,256]{3,2,1,0:T(8,128)(2,1)S(1)}, f32[256,1536]{1,0:T(8,128)S(1)}, f32[128,384]{1,0:T(8,128)S(1)}, bf16[1536,256]{1,0:T(8,128)(2,1)S(1...) custom-call(s32[8,128]{1,0:T(8,128)S(1)} %get-tuple-element.38.info, ...), custom_call_target="tpu_custom_call" | custom-call | flops 1 | bytes 1 | tf_op jit(solution)/shard_map/forward/pallas_call | solution.py:555
  21.1 2.9 %collective-permute-done.refs_0_.high_a = bf16[16,2,64,128]{3,2,1,0:T(8,128)(2,1)S(1)} collective-permute-done((bf16[16,2,64,128]{3,2,1,0:T(8,128)(2,1)S(1)}, bf16[16,2,64,128]{3,2,1,0:T(8,128)(2,1)S(1)}, u32[]{:S(2)}, u32[]{:S(2)}) %collective-permute-start) | collective-permute-done | bytes 524320 | tf_op jit(solution)/shard_map/ppermute | solution.py:549
  24.8 1.9 %mid.2 = (bf16[2,15,64,256]{3,2,1,0:T(8,128)(2,1)S(1)}, bf16[15,64,256]{2,1,0:T(8,128)(2,1)S(1)}) custom-call(s32[8,128]{1,0:T(8,128)S(1)} %get-tuple-element.38.info, bf16[16,2,64,128]{3,2,1,0:T(8,128)(2,1)S(1)} %collective-permute-done.refs_0_.high_a, bf16[16,2,64,128]{3,2,1,0:T(8,128)(2,1)S(1)} %collective-permute-done.1.refs_1_.low_a, ...), custom_call_target="tpu_custom_call" | custom-call | flops 1 | bytes 1 | tf_op jit(solution)/shard_map/mid/pallas_call | solution.py:564
  27.2 5.5 %collective-permute-start.2 = (bf16[15,64,256]{2,1,0:T(8,128)(2,1)S(1)}, bf16[15,64,256]{2,1,0:T(8,128)(2,1)S(1)}, u32[]{:S(2)}, u32[]{:S(2)}) collective-permute-start(bf16[15,64,256]{2,1,0:T(8,128)(2,1)S(1)} %get-tuple-element.75), channel_id=1, source_target_pairs={{1,2},{3,4},{5,6},{7,8},{9,10},{11,12},{13,14},{15,16},{17,18},{19... | collective-permute-start | bytes 1474568 | tf_op jit(solution)/shard_map/ppermute | solution.py:549
  32.7 2.5 %collective-permute-done.4.refs_2_.high_b = bf16[16,2,64,128]{3,2,1,0:T(8,128)(2,1)S(1)} collective-permute-done((bf16[16,2,64,128]{3,2,1,0:T(8,128)(2,1)S(1)}, bf16[16,2,64,128]{3,2,1,0:T(8,128)(2,1)S(1)}, u32[]{:S(2)}, u32[]{:S(2)}) %collective-permute-start.4) | collective-permute-done | bytes 524320 | tf_op jit(solution)/shard_map/ppermute | solution.py:549
  36.0 2.1 %mid.3 = (bf16[2,17,64,256]{3,2,1,0:T(8,128)(2,1)S(1)}, bf16[17,64,256]{2,1,0:T(8,128)(2,1)S(1)}) custom-call(s32[8,128]{1,0:T(8,128)S(1)} %get-tuple-element.38.info, bf16[16,2,64,128]{3,2,1,0:T(8,128)(2,1)S(1)} %collective-permute-done.refs_0_.high_a, bf16[16,2,64,128]{3,2,1,0:T(8,128)(2,1)S(1)} %collective-permute-done.1.refs_1_.low_a, ...), custom_call_target="tpu_custom_call" | custom-call | flops 1 | bytes 1 | tf_op jit(solution)/shard_map/mid/pallas_call | solution.py:564
  38.6 5.7 %collective-permute-start.6 = (bf16[17,64,256]{2,1,0:T(8,128)(2,1)S(1)}, bf16[17,64,256]{2,1,0:T(8,128)(2,1)S(1)}, u32[]{:S(2)}, u32[]{:S(2)}) collective-permute-start(bf16[17,64,256]{2,1,0:T(8,128)(2,1)S(1)} %get-tuple-element.73), channel_id=1, source_target_pairs={{1,2},{3,4},{5,6},{7,8},{9,10},{11,12},{13,14},{15,16},{17,18},{19... | collective-permute-start | bytes 1671176 | tf_op jit(solution)/shard_map/ppermute | solution.py:549
  44.3 3.8 %grads.1 = (f32[4,192,128]{2,1,0:T(8,128)S(1)}, f32[4,192,128]{2,1,0:T(8,128)S(1)}) custom-call(s32[8,128]{1,0:T(8,128)S(1)} %get-tuple-element.38.info, bf16[16,2,64,128]{3,2,1,0:T(8,128)(2,1)S(1)} %collective-permute-done.refs_0_.high_a, bf16[16,2,64,128]{3,2,1,0:T(8,128)(2,1)S(1)} %collective-permute-done.1.refs_1_.low_a, ...), custom_call_target="tpu_custom_call" | custom-call | flops 1 | bytes 1 | tf_op jit(solution)/shard_map/grads/pallas_call | solution.py:578
  48.1 3.1 %collective-permute-start.8 = (f32[4,192,128]{2,1,0:T(8,128)S(1)}, f32[4,192,128]{2,1,0:T(8,128)S(1)}, u32[]{:S(2)}, u32[]{:S(2)}) collective-permute-start(f32[4,192,128]{2,1,0:T(8,128)S(1)} %hold.1), channel_id=1, source_target_pairs={{0,64},{64,0},{1,65},{65,1},{2,66},{66,2},{3,67},{67,3},{4,68},{68... | collective-permute-start | bytes 1179656 | tf_op jit(solution)/shard_map/ppermute | solution.py:587
  51.2 1.3 %collective-permute-done.8.refs_1_ = f32[4,192,128]{2,1,0:T(8,128)S(1)} collective-permute-done((f32[4,192,128]{2,1,0:T(8,128)S(1)}, f32[4,192,128]{2,1,0:T(8,128)S(1)}, u32[]{:S(2)}, u32[]{:S(2)}) %collective-permute-start.8) | collective-permute-done | bytes 393248 | tf_op jit(solution)/shard_map/ppermute | solution.py:587
  52.7 4.1 %collective-permute-start.10 = (f32[192,128]{1,0:T(8,128)S(1)}, f32[192,128]{1,0:T(8,128)S(1)}, u32[]{:S(2)}, u32[]{:S(2)}) collective-permute-start(f32[192,128]{1,0:T(8,128)S(1)} %get-tuple-element.63), channel_id=1, source_target_pairs={{0,32},{16,48},{32,0},{48,16},{1,33},{17,49},{33,1},{49,17},{2,34}... | collective-permute-start | bytes 294920 | tf_op jit(solution)/shard_map/ppermute | solution.py:503
  56.8 1.2 %early_out.1 = (bf16[2,32,2,64,128]{4,3,2,1,0:T(8,128)(2,1)}, f32[8,128]{1,0:T(8,128)S(1)}) custom-call(s32[8,128]{1,0:T(8,128)S(1)} %get-tuple-element.38.info, bf16[2,32,2,64,128]{4,3,2,1,0:T(8,128)(2,1)S(1)} %bitcast.25, bf16[2,32,64,256]{3,2,1,0:T(8,128)(2,1)S(1)} %get-tuple-element.39.refs_2_.refs_4_.s, ...), custom_call_target="tpu_custom_call" | custom-call | flops 1 | bytes 1 | tf_op jit(solution)/shard_map/early_out/pallas_call | solution.py:589
  58.0 1.2 %early_in.1 = (bf16[2,32,2,64,128]{4,3,2,1,0:T(8,128)(2,1)}, f32[8,128]{1,0:T(8,128)S(1)}) custom-call(s32[8,128]{1,0:T(8,128)S(1)} %get-tuple-element.38.info, bf16[2,32,2,64,128]{4,3,2,1,0:T(8,128)(2,1)S(1)} %bitcast.26, bf16[2,32,2,64,128]{4,3,2,1,0:T(8,128)(2,1)S(1)} %bitcast.19, bf16[16,2,64,128]{3,2,1,0:T(8,128)(2,1)S(1)} %collective-permute-done.refs_0_.high_a, ...), custom_call_target="tpu_custom_call" | custom-call | flops 1 | bytes 1 | tf_op jit(solution)/shard_map/early_in/pallas_call | solution.py:592
  59.2 2.2 %collective-permute-done.10.refs_2_ = f32[192,128]{1,0:T(8,128)S(1)} collective-permute-done((f32[192,128]{1,0:T(8,128)S(1)}, f32[192,128]{1,0:T(8,128)S(1)}, u32[]{:S(2)}, u32[]{:S(2)}) %collective-permute-start.10) | collective-permute-done | bytes 98336 | tf_op jit(solution)/shard_map/ppermute | solution.py:503
  61.6 1.4 %collective-permute-start.12 = (bf16[192,128]{1,0:T(8,128)(2,1)S(1)}, bf16[192,128]{1,0:T(8,128)(2,1)S(1)}, u32[]{:S(2)}, u32[]{:S(2)}) collective-permute-start(bf16[192,128]{1,0:T(8,128)(2,1)S(1)} %x_sum.1.refs_0_), channel_id=1, source_target_pairs={{0,4},{4,8},{8,12},{12,0},{1,5},{5,9},{9,13},{13,1},{2,6},{6,10},{... | collective-permute-start | bytes 147464 | tf_op jit(solution)/shard_map/ppermute | solution.py:503
  63.0 1.6 %output.1 = (bf16[2,32,2,64,128]{4,3,2,1,0:T(8,128)(2,1)}, f32[8,128]{1,0:T(8,128)S(1)}) custom-call(s32[8,128]{1,0:T(8,128)S(1)} %get-tuple-element.38.info, bf16[2,32,2,64,128]{4,3,2,1,0:T(8,128)(2,1)S(1)} %bitcast.27, bf16[2,32,64,256]{3,2,1,0:T(8,128)(2,1)S(1)} %get-tuple-element.39.refs_2_.refs_4_.s, ...), custom_call_target="tpu_custom_call", output_to_operand_aliasing={{0}: (8, {})} | custom-call | flops 1 | bytes 1 | tf_op jit(solution)/shard_map/output/pallas_call | solution.py:596
  64.6 1.5 %collective-permute-done.13.refs_2_ = bf16[192,128]{1,0:T(8,128)(2,1)S(1)} collective-permute-done((bf16[192,128]{1,0:T(8,128)(2,1)S(1)}, bf16[192,128]{1,0:T(8,128)(2,1)S(1)}, u32[]{:S(2)}, u32[]{:S(2)}) %collective-permute-start.13) | collective-permute-done | bytes 49184 | tf_op jit(solution)/shard_map/ppermute | solution.py:503
  66.9 0.9 collective-permute-start.17
  68.4 2.3 %input_grad.2 = (bf16[2,32,2,64,128]{4,3,2,1,0:T(8,128)(2,1)}, f32[8,128]{1,0:T(8,128)S(1)}) custom-call(s32[8,128]{1,0:T(8,128)S(1)} %get-tuple-element.38.info, bf16[2,32,2,64,128]{4,3,2,1,0:T(8,128)(2,1)S(1)} %bitcast.28, bf16[2,32,2,64,128]{4,3,2,1,0:T(8,128)(2,1)S(1)} %bitcast.20, ...), custom_call_target="tpu_custom_call", output_to_operand_aliasing={{0}: (9, {})} | custom-call | flops 1 | bytes 1 | tf_op jit(solution)/shard_map/input_grad/pallas_call | solution.py:602
  70.8 1.5 %collective-permute-done.16.refs_2_ = bf16[192,128]{1,0:T(8,128)(2,1)S(1)} collective-permute-done((bf16[192,128]{1,0:T(8,128)(2,1)S(1)}, bf16[192,128]{1,0:T(8,128)(2,1)S(1)}, u32[]{:S(2)}, u32[]{:S(2)}) %collective-permute-start.16) | collective-permute-done | bytes 49184 | tf_op jit(solution)/shard_map/ppermute | solution.py:503
  72.8 2.2 %collective-permute-start.20 = (bf16[192,128]{1,0:T(8,128)(2,1)S(1)}, bf16[192,128]{1,0:T(8,128)(2,1)S(1)}, u32[]{:S(2)}, u32[]{:S(2)}) collective-permute-start(bf16[192,128]{1,0:T(8,128)(2,1)S(1)} %z_sum.1.refs_0_), channel_id=1, source_target_pairs={{0,48},{16,0},{32,16},{48,32},{1,49},{17,1},{33,17},{49,33},{2,50}... | collective-permute-start | bytes 147464 | tf_op jit(solution)/shard_map/ppermute | solution.py:503
  75.0 3.3 %collective-permute-start.19 = (bf16[192,128]{1,0:T(8,128)(2,1)S(1)}, bf16[192,128]{1,0:T(8,128)(2,1)S(1)}, u32[]{:S(2)}, u32[]{:S(2)}) collective-permute-start(bf16[192,128]{1,0:T(8,128)(2,1)S(1)} %z_sum.1.refs_0_), channel_id=1, source_target_pairs={{0,32},{16,48},{32,0},{48,16},{1,33},{17,49},{33,1},{49,17},{2,34}... | collective-permute-start | bytes 147464 | tf_op jit(solution)/shard_map/ppermute | solution.py:503
  78.3 2.3 %input_grad.3 = (bf16[2,32,2,64,128]{4,3,2,1,0:T(8,128)(2,1)}, f32[8,128]{1,0:T(8,128)S(1)}) custom-call(s32[8,128]{1,0:T(8,128)S(1)} %get-tuple-element.38.info, bf16[2,32,2,64,128]{4,3,2,1,0:T(8,128)(2,1)S(1)} %bitcast.29, bf16[2,32,2,64,128]{4,3,2,1,0:T(8,128)(2,1)S(1)} %bitcast.21, ...), custom_call_target="tpu_custom_call", output_to_operand_aliasing={{0}: (9, {})} | custom-call | flops 1 | bytes 1 | tf_op jit(solution)/shard_map/input_grad/pallas_call | solution.py:602
  80.6 1.8 %collective-permute-done.18.refs_1_ = bf16[192,128]{1,0:T(8,128)(2,1)S(1)} collective-permute-done((bf16[192,128]{1,0:T(8,128)(2,1)S(1)}, bf16[192,128]{1,0:T(8,128)(2,1)S(1)}, u32[]{:S(2)}, u32[]{:S(2)}) %collective-permute-start.18) | collective-permute-done | bytes 49184 | tf_op jit(solution)/shard_map/ppermute | solution.py:503
  82.4 3.6 %collective-permute-start.21 = (bf16[4,192,128]{2,1,0:T(8,128)(2,1)S(1)}, bf16[4,192,128]{2,1,0:T(8,128)(2,1)S(1)}, u32[]{:S(2)}, u32[]{:S(2)}) collective-permute-start(bf16[4,192,128]{2,1,0:T(8,128)(2,1)S(1)} %x_stack.1.mine), channel_id=1, source_target_pairs={{0,64},{64,0},{1,65},{65,1},{2,66},{66,2},{3,67},{67,3},{4,68},{68... | collective-permute-start | bytes 589832 | tf_op jit(solution)/shard_map/ppermute | solution.py:616
  86.0 1.1 %collective-permute-done.21.theirs = bf16[4,192,128]{2,1,0:T(8,128)(2,1)S(1)} collective-permute-done((bf16[4,192,128]{2,1,0:T(8,128)(2,1)S(1)}, bf16[4,192,128]{2,1,0:T(8,128)(2,1)S(1)}, u32[]{:S(2)}, u32[]{:S(2)}) %collective-permute-start.21) | collective-permute-done | bytes 196640 | tf_op jit(solution)/shard_map/ppermute | solution.py:616
  87.1 1.1 %place.1 = (f32[1152,128]{1,0:T(8,128)}, f32[384,128]{1,0:T(8,128)}) custom-call(s32[8,128]{1,0:T(8,128)S(1)} %get-tuple-element.38.info, bf16[4,192,128]{2,1,0:T(8,128)(2,1)S(1)} %x_stack.1.mine, bf16[4,192,128]{2,1,0:T(8,128)(2,1)S(1)} %collective-permute-done.21.theirs), custom_call_target="tpu_custom_call" | custom-call | flops 1 | bytes 1 | tf_op jit(solution)/shard_map/place/pallas_call | solution.py:617
  (41 shorter events, 5.9 us)
Async XLA Ops:
  0.6 0.7 copy-start.4
  1.3 12.5 %copy-start = (bf16[2,64,64,128]{3,2,1,0:T(8,128)(2,1)S(1)}, bf16[2,64,64,128]{3,2,1,0:T(8,128)(2,1)}, u32[]{:S(2)}) copy-start(bf16[2,64,64,128]{3,2,1,0:T(8,128)(2,1)} %param.6) | copy-start | bytes 6291460
  1.3 12.5 %copy-start.1 = (bf16[2,64,64,128]{3,2,1,0:T(8,128)(2,1)S(1)}, bf16[2,64,64,128]{3,2,1,0:T(8,128)(2,1)}, u32[]{:S(2)}) copy-start(bf16[2,64,64,128]{3,2,1,0:T(8,128)(2,1)} %param.5) | copy-start | bytes 6291460
  3.0 21.0 %collective-permute-start = (bf16[16,2,64,128]{3,2,1,0:T(8,128)(2,1)S(1)}, bf16[16,2,64,128]{3,2,1,0:T(8,128)(2,1)S(1)}, u32[]{:S(2)}, u32[]{:S(2)}) collective-permute-start(bf16[16,2,64,128]{3,2,1,0:T(8,128)(2,1)S(1)} %get-tuple-element.40), channel_id=1, source_target_pairs={{1,2},{3,4},{5,6},{7,8},{9,10},{11,12},{13,14},{15,16},{17,18},{19... | collective-permute-start | bytes 1572872 | tf_op jit(solution)/shard_map/ppermute | solution.py:549
  12.3 12.5 %collective-permute-start.1 = (bf16[16,2,64,128]{3,2,1,0:T(8,128)(2,1)S(1)}, bf16[16,2,64,128]{3,2,1,0:T(8,128)(2,1)S(1)}, u32[]{:S(2)}, u32[]{:S(2)}) collective-permute-start(bf16[16,2,64,128]{3,2,1,0:T(8,128)(2,1)S(1)} %get-tuple-element.41), channel_id=1, source_target_pairs={{0,1},{2,3},{4,5},{6,7},{8,9},{10,11},{12,13},{14,15},{16,17},{18,... | collective-permute-start | bytes 1572872 | tf_op jit(solution)/shard_map/ppermute | solution.py:549
  12.3 22.9 %collective-permute-start.4 = (bf16[16,2,64,128]{3,2,1,0:T(8,128)(2,1)S(1)}, bf16[16,2,64,128]{3,2,1,0:T(8,128)(2,1)S(1)}, u32[]{:S(2)}, u32[]{:S(2)}) collective-permute-start(bf16[16,2,64,128]{3,2,1,0:T(8,128)(2,1)S(1)} %get-tuple-element.46), channel_id=1, source_target_pairs={{1,2},{3,4},{5,6},{7,8},{9,10},{11,12},{13,14},{15,16},{17,18},{19... | collective-permute-start | bytes 1572872 | tf_op jit(solution)/shard_map/ppermute | solution.py:549
  12.5 23.5 %collective-permute-start.5 = (bf16[16,2,64,128]{3,2,1,0:T(8,128)(2,1)S(1)}, bf16[16,2,64,128]{3,2,1,0:T(8,128)(2,1)S(1)}, u32[]{:S(2)}, u32[]{:S(2)}) collective-permute-start(bf16[16,2,64,128]{3,2,1,0:T(8,128)(2,1)S(1)} %get-tuple-element.47), channel_id=1, source_target_pairs={{0,1},{2,3},{4,5},{6,7},{8,9},{10,11},{12,13},{14,15},{16,17},{18,... | collective-permute-start | bytes 1572872 | tf_op jit(solution)/shard_map/ppermute | solution.py:549
  13.8 1.0 %copy-start.2 = (bf16[3,3,128,128]{3,2,1,0:T(8,128)(2,1)S(1)}, bf16[3,3,128,128]{3,2,1,0:T(8,128)(2,1)}, u32[]{:S(2)}) copy-start(bf16[3,3,128,128]{3,2,1,0:T(8,128)(2,1)} %w_ref.1) | copy-start | bytes 884740
  14.8 0.9 %copy-start.3 = (bf16[3,128,128]{2,1,0:T(8,128)(2,1)S(1)}, bf16[3,128,128]{2,1,0:T(8,128)(2,1)}, u32[]{:S(2)}) copy-start(bf16[3,128,128]{2,1,0:T(8,128)(2,1)} %tw_ref.1) | copy-start | bytes 294916
  26.8 21.4 %collective-permute-start.3 = (bf16[15,64,256]{2,1,0:T(8,128)(2,1)S(1)}, bf16[15,64,256]{2,1,0:T(8,128)(2,1)S(1)}, u32[]{:S(2)}, u32[]{:S(2)}) collective-permute-start(bf16[15,64,256]{2,1,0:T(8,128)(2,1)S(1)} %get-tuple-element.74), channel_id=1, source_target_pairs={{0,1},{2,3},{4,5},{6,7},{8,9},{10,11},{12,13},{14,15},{16,17},{18,... | collective-permute-start | bytes 1474568 | tf_op jit(solution)/shard_map/ppermute | solution.py:549
  27.2 21.0 %collective-permute-start.2 = (bf16[15,64,256]{2,1,0:T(8,128)(2,1)S(1)}, bf16[15,64,256]{2,1,0:T(8,128)(2,1)S(1)}, u32[]{:S(2)}, u32[]{:S(2)}) collective-permute-start(bf16[15,64,256]{2,1,0:T(8,128)(2,1)S(1)} %get-tuple-element.75), channel_id=1, source_target_pairs={{1,2},{3,4},{5,6},{7,8},{9,10},{11,12},{13,14},{15,16},{17,18},{19... | collective-permute-start | bytes 1474568 | tf_op jit(solution)/shard_map/ppermute | solution.py:549
  38.2 24.7 %collective-permute-start.7 = (bf16[17,64,256]{2,1,0:T(8,128)(2,1)S(1)}, bf16[17,64,256]{2,1,0:T(8,128)(2,1)S(1)}, u32[]{:S(2)}, u32[]{:S(2)}) collective-permute-start(bf16[17,64,256]{2,1,0:T(8,128)(2,1)S(1)} %get-tuple-element.72), channel_id=1, source_target_pairs={{0,1},{2,3},{4,5},{6,7},{8,9},{10,11},{12,13},{14,15},{16,17},{18,... | collective-permute-start | bytes 1671176 | tf_op jit(solution)/shard_map/ppermute | solution.py:549
  38.6 24.3 %collective-permute-start.6 = (bf16[17,64,256]{2,1,0:T(8,128)(2,1)S(1)}, bf16[17,64,256]{2,1,0:T(8,128)(2,1)S(1)}, u32[]{:S(2)}, u32[]{:S(2)}) collective-permute-start(bf16[17,64,256]{2,1,0:T(8,128)(2,1)S(1)} %get-tuple-element.73), channel_id=1, source_target_pairs={{1,2},{3,4},{5,6},{7,8},{9,10},{11,12},{13,14},{15,16},{17,18},{19... | collective-permute-start | bytes 1671176 | tf_op jit(solution)/shard_map/ppermute | solution.py:549
  48.1 4.4 %collective-permute-start.8 = (f32[4,192,128]{2,1,0:T(8,128)S(1)}, f32[4,192,128]{2,1,0:T(8,128)S(1)}, u32[]{:S(2)}, u32[]{:S(2)}) collective-permute-start(f32[4,192,128]{2,1,0:T(8,128)S(1)} %hold.1), channel_id=1, source_target_pairs={{0,64},{64,0},{1,65},{65,1},{2,66},{66,2},{3,67},{67,3},{4,68},{68... | collective-permute-start | bytes 1179656 | tf_op jit(solution)/shard_map/ppermute | solution.py:587
  52.6 6.6 %collective-permute-start.9 = (f32[192,128]{1,0:T(8,128)S(1)}, f32[192,128]{1,0:T(8,128)S(1)}, u32[]{:S(2)}, u32[]{:S(2)}) collective-permute-start(f32[192,128]{1,0:T(8,128)S(1)} %get-tuple-element.62), channel_id=1, source_target_pairs={{0,16},{16,32},{32,48},{48,0},{1,17},{17,33},{33,49},{49,1},{2,18}... | collective-permute-start | bytes 294920 | tf_op jit(solution)/shard_map/ppermute | solution.py:503
  52.7 8.7 %collective-permute-start.10 = (f32[192,128]{1,0:T(8,128)S(1)}, f32[192,128]{1,0:T(8,128)S(1)}, u32[]{:S(2)}, u32[]{:S(2)}) collective-permute-start(f32[192,128]{1,0:T(8,128)S(1)} %get-tuple-element.63), channel_id=1, source_target_pairs={{0,32},{16,48},{32,0},{48,16},{1,33},{17,49},{33,1},{49,17},{2,34}... | collective-permute-start | bytes 294920 | tf_op jit(solution)/shard_map/ppermute | solution.py:503
  56.8 4.7 %collective-permute-start.11 = (f32[192,128]{1,0:T(8,128)S(1)}, f32[192,128]{1,0:T(8,128)S(1)}, u32[]{:S(2)}, u32[]{:S(2)}) collective-permute-start(f32[192,128]{1,0:T(8,128)S(1)} %get-tuple-element.64), channel_id=1, source_target_pairs={{0,48},{16,0},{32,16},{48,32},{1,49},{17,1},{33,17},{49,33},{2,50}... | collective-permute-start | bytes 294920 | tf_op jit(solution)/shard_map/ppermute | solution.py:503
  61.4 3.1 %collective-permute-start.14 = (bf16[192,128]{1,0:T(8,128)(2,1)S(1)}, bf16[192,128]{1,0:T(8,128)(2,1)S(1)}, u32[]{:S(2)}, u32[]{:S(2)}) collective-permute-start(bf16[192,128]{1,0:T(8,128)(2,1)S(1)} %x_sum.1.refs_0_), channel_id=1, source_target_pairs={{0,12},{4,0},{8,4},{12,8},{1,13},{5,1},{9,5},{13,9},{2,14},{6,2},{... | collective-permute-start | bytes 147464 | tf_op jit(solution)/shard_map/ppermute | solution.py:503
  61.5 4.5 %collective-permute-start.13 = (bf16[192,128]{1,0:T(8,128)(2,1)S(1)}, bf16[192,128]{1,0:T(8,128)(2,1)S(1)}, u32[]{:S(2)}, u32[]{:S(2)}) collective-permute-start(bf16[192,128]{1,0:T(8,128)(2,1)S(1)} %x_sum.1.refs_0_), channel_id=1, source_target_pairs={{0,8},{4,12},{8,0},{12,4},{1,9},{5,13},{9,1},{13,5},{2,10},{6,14},... | collective-permute-start | bytes 147464 | tf_op jit(solution)/shard_map/ppermute | solution.py:503
  61.6 5.2 %collective-permute-start.12 = (bf16[192,128]{1,0:T(8,128)(2,1)S(1)}, bf16[192,128]{1,0:T(8,128)(2,1)S(1)}, u32[]{:S(2)}, u32[]{:S(2)}) collective-permute-start(bf16[192,128]{1,0:T(8,128)(2,1)S(1)} %x_sum.1.refs_0_), channel_id=1, source_target_pairs={{0,4},{4,8},{8,12},{12,0},{1,5},{5,9},{9,13},{13,1},{2,6},{6,10},{... | collective-permute-start | bytes 147464 | tf_op jit(solution)/shard_map/ppermute | solution.py:503
  66.9 3.9 %collective-permute-start.17 = (bf16[192,128]{1,0:T(8,128)(2,1)S(1)}, bf16[192,128]{1,0:T(8,128)(2,1)S(1)}, u32[]{:S(2)}, u32[]{:S(2)}) collective-permute-start(bf16[192,128]{1,0:T(8,128)(2,1)S(1)} %y_sum.1.refs_0_), channel_id=1, source_target_pairs={{0,3},{1,0},{2,1},{3,2},{4,7},{5,4},{6,5},{7,6},{8,11},{9,8},{10,9... | collective-permute-start | bytes 147464 | tf_op jit(solution)/shard_map/ppermute | solution.py:503
  67.8 4.5 %collective-permute-start.16 = (bf16[192,128]{1,0:T(8,128)(2,1)S(1)}, bf16[192,128]{1,0:T(8,128)(2,1)S(1)}, u32[]{:S(2)}, u32[]{:S(2)}) collective-permute-start(bf16[192,128]{1,0:T(8,128)(2,1)S(1)} %y_sum.1.refs_0_), channel_id=1, source_target_pairs={{0,2},{1,3},{2,0},{3,1},{4,6},{5,7},{6,4},{7,5},{8,10},{9,11},{10,... | collective-permute-start | bytes 147464 | tf_op jit(solution)/shard_map/ppermute | solution.py:503
  67.8 5.0 %collective-permute-start.15 = (bf16[192,128]{1,0:T(8,128)(2,1)S(1)}, bf16[192,128]{1,0:T(8,128)(2,1)S(1)}, u32[]{:S(2)}, u32[]{:S(2)}) collective-permute-start(bf16[192,128]{1,0:T(8,128)(2,1)S(1)} %y_sum.1.refs_0_), channel_id=1, source_target_pairs={{0,1},{1,2},{2,3},{3,0},{4,5},{5,6},{6,7},{7,4},{8,9},{9,10},{10,1... | collective-permute-start | bytes 147464 | tf_op jit(solution)/shard_map/ppermute | solution.py:503
  72.8 7.8 %collective-permute-start.20 = (bf16[192,128]{1,0:T(8,128)(2,1)S(1)}, bf16[192,128]{1,0:T(8,128)(2,1)S(1)}, u32[]{:S(2)}, u32[]{:S(2)}) collective-permute-start(bf16[192,128]{1,0:T(8,128)(2,1)S(1)} %z_sum.1.refs_0_), channel_id=1, source_target_pairs={{0,48},{16,0},{32,16},{48,32},{1,49},{17,1},{33,17},{49,33},{2,50}... | collective-permute-start | bytes 147464 | tf_op jit(solution)/shard_map/ppermute | solution.py:503
  75.0 5.6 %collective-permute-start.19 = (bf16[192,128]{1,0:T(8,128)(2,1)S(1)}, bf16[192,128]{1,0:T(8,128)(2,1)S(1)}, u32[]{:S(2)}, u32[]{:S(2)}) collective-permute-start(bf16[192,128]{1,0:T(8,128)(2,1)S(1)} %z_sum.1.refs_0_), channel_id=1, source_target_pairs={{0,32},{16,48},{32,0},{48,16},{1,33},{17,49},{33,1},{49,17},{2,34}... | collective-permute-start | bytes 147464 | tf_op jit(solution)/shard_map/ppermute | solution.py:503
  78.3 4.2 %collective-permute-start.18 = (bf16[192,128]{1,0:T(8,128)(2,1)S(1)}, bf16[192,128]{1,0:T(8,128)(2,1)S(1)}, u32[]{:S(2)}, u32[]{:S(2)}) collective-permute-start(bf16[192,128]{1,0:T(8,128)(2,1)S(1)} %z_sum.1.refs_0_), channel_id=1, source_target_pairs={{0,16},{16,32},{32,48},{48,0},{1,17},{17,33},{33,49},{49,1},{2,18}... | collective-permute-start | bytes 147464 | tf_op jit(solution)/shard_map/ppermute | solution.py:503
  82.4 4.7 %collective-permute-start.21 = (bf16[4,192,128]{2,1,0:T(8,128)(2,1)S(1)}, bf16[4,192,128]{2,1,0:T(8,128)(2,1)S(1)}, u32[]{:S(2)}, u32[]{:S(2)}) collective-permute-start(bf16[4,192,128]{2,1,0:T(8,128)(2,1)S(1)} %x_stack.1.mine), channel_id=1, source_target_pairs={{0,64},{64,0},{1,65},{65,1},{2,66},{66,2},{3,67},{67,3},{4,68},{68... | collective-permute-start | bytes 589832 | tf_op jit(solution)/shard_map/ppermute | solution.py:616

commit v5 on v4

--- a/solution.py
+++ b/solution.py
@@ -255,15 +255,20 @@
     back = is_set(info, BACK1)
     before = halves(even, hops[0::2], hops[1::2], CUT1)
     after = halves(even, hops[1::2], hops[0::2], CUT1)
-    clear_edges(wide)
-    done = max(first - 1, 0)
-    end = min(first + count + 1, PAIRS)
-    while done < end:
-        n = min(FILL - done % FILL, end - done)
+    end = first + count
+    if first == 0:
+        wide[0, :, 0 : 3 * CH] = jnp.zeros((COLS, 3 * CH), BF16)
+    else:
+        put_act(wide, -1, 1, before(first - 1, 1, 1))
+    for t in range(first, end, FILL):
+        n = min(FILL, end - t)
         for half in range(2):
-            put_act(wide, done, half, before(done, n, half))
-        done += n
-    sh[...] = conv(wide, wf, first, count).astype(BF16).reshape(count, COLS, 2 * CH)
+            put_act(wide, t - first, half, before(t, n, half))
+    if end == PAIRS:
+        wide[count, :, 3 * CH : 6 * CH] = jnp.zeros((COLS, 3 * CH), BF16)
+    else:
+        put_act(wide, count, 0, before(end, 1, 0))
+    sh[...] = conv(wide, wf, 0, count).astype(BF16).reshape(count, COLS, 2 * CH)
 
     down = jnp.where(even, 0, 1)
     at = pl.ds(first, count)
@@ -282,26 +287,22 @@
 
 
 def grad_kernel(
-    info, high_a, low_a, high_b, low_b, x, g, s, sent_a, sent_b, sh_a, sh_b, acc_in, tacc_in, tb, own_ref, other_ref,
-    wide, v, gn, acc, tacc, both
+    info, high_a, low_a, high_b, low_b, x, g, s, sent_a, sent_b, sh_a, sh_b, wide_a, wide_b, acc_in, tacc_in, tb,
+    own_ref, other_ref, wide, v, gn, acc, tacc, both
 ):
     two = is_two(info)
     even = is_set(info, EVEN)
     back = is_set(info, BACK1)
     cross = jnp.logical_and(back, is_set(info, NEXT1))
-    before = halves(even, (high_a, high_b), (low_a, low_b), CUT1)
     after = halves(even, (low_a, low_b), (high_a, high_b), CUT1)
     down = jnp.where(even, 0, 1)
     acc[...] = acc_in[...]
     tacc[...] = tacc_in[...]
-    clear_edges(wide)
-    fill_act(wide, before)
     for t in range(0, PAIRS, FILL):
         gn[pl.ds(t, FILL)] = after(t, FILL)
-    for t, sent, sh in ((0, sent_a, sh_a), (CUT2, sent_b, sh_b)):
+    for t, sent, sh, part in ((0, sent_a, sh_a, wide_a), (CUT2, sent_b, sh_b, wide_b)):
         n = sh.shape[0]
         at = pl.ds(t, n)
-        v[at] = sent[down]
 
         def two_frames(half, at=at):
             return jnp.concatenate([g[0, at, half], jnp.where(two, g[1, at, half], gn[at, half])], axis=-1)
@@ -309,10 +310,14 @@
         found = correlate(sh[...], two_frames)
         tacc[:, CH : 2 * CH] += jnp.where(back, found[:, 0:CH], 0.0)
         tacc[:, 2 * CH : 3 * CH] += jnp.where(cross, found[:, CH : 2 * CH], 0.0)
-    add_spatial(acc, wide, v)
+        low, high = windows(part, 0, n)
+        value = flat(sent[down])
+        acc[:, 0 : 6 * CH] += dot_t(value, low)
+        acc[:, 6 * CH : 12 * CH] += dot_t(value, high)
 
     @pl.when(jnp.logical_and(two, is_set(info, NEXT2)))
     def _():
+        clear_edges(wide)
         fill_act(wide, lambda t, n, half: x[0, pl.ds(t, n), half])
 
         def up(t):
@@ -564,27 +569,27 @@
         return call(
             functools.partial(mid_kernel, first=first, count=count),
             [VMEM] * (6 + len(hops)),
-            [shape((2, count) + S_SHAPE[1:]), shape((count,) + S_SHAPE[1:])],
-            [WIDE, TAPS2],
+            [shape((2, count) + S_SHAPE[1:]), shape((count,) + S_SHAPE[1:]), shape((count + 1, COLS, 6 * CH))],
+            [TAPS2],
             "mid",
         )(info, *hops, s, g, wf, tf, tb)
 
-    sent_a, sh_a = mid(0, CUT2, hop1_a)
+    sent_a, sh_a, wide_a = mid(0, CUT2, hop1_a)
     hop2_a = hop(sent_a[0], sent_a[1])
-    sent_b, sh_b = mid(CUT2, PAIRS - CUT2, hop1)
+    sent_b, sh_b, wide_b = mid(CUT2, PAIRS - CUT2, hop1)
     hop2_b = hop(sent_b[0], sent_b[1])
     hop2 = hop2_a + hop2_b
 
     own, other = call(
         grad_kernel,
-        [VMEM] * 15,
+        [VMEM] * 17,
         [shape(PIECES, F32), shape(PIECES, F32)],
         [WIDE, VALUES, FRAME1, pltpu.VMEM(ACC, F32), pltpu.VMEM(TACC, F32), pltpu.VMEM((2, HALF, CH), F32)],
         "grads",
-    )(info, *hop1, x, g, s, sent_a, sent_b, sh_a, sh_b, acc, tacc, tb)
+    )(info, *hop1, x, g, s, sent_a, sent_b, sh_a, sh_b, wide_a, wide_b, acc, tacc, tb)
 
     other = call(hold_kernel, [ANY] * 3, [shape(PIECES, F32)], [], "hold", [ANY], {2: 0})(*hop2_a, other)[0]
-    chunks = split_call("core_sum", 2, SIDE, PIECES[1:])(own, lax.ppermute(other, "dp", swap))
+    chunks = split_call("core_sum", 2, SIDE, PIECES[1:], 0, BF16)(own, lax.ppermute(other, "dp", swap))
     frames = [pltpu.HBM((2,) + FRAME, BF16), shape((8, CH), F32)]
     early_out, done_a = call(
         early_out_kernel, [VMEM] * 6 + [ANY], frames, [TAPS, FRAME1, SEM], "early_out", [ANY, VMEM]

time: 88.4 us -> 86.6 us (0.980)
  waiting for transfers between devices: 17.7 us -> 13.4 us
  starting transfers between devices: 42.2 us -> 44.8 us
    ppermute x12, waiting for transfers between devices: 8.23 us -> 3.8 us  [shifts(): return lax.ppermute(value, axis, [(i, (i + k) % SIDE) for i in range(SIDE)])]
    ppermute x12, starting transfers between devices: 12.7 us -> 15 us  [shifts(): return lax.ppermute(value, axis, [(i, (i + k) % SIDE) for i in range(SIDE)])]
where the time goes in v5:
time: 86.6 us; the launch traced here: 85.6 us
  starting transfers between devices  44.8 us (52%)
  Pallas kernels  23.9 us (28%)
  waiting for transfers between devices  13.4 us (15%)
  local copies, waits for them, and re-layouts  2.71 us (3%)
    ppermute x4, starting transfers between devices, hop(): lax.ppermute(for_high, axes, high)  21.2 us
    ppermute x12, starting transfers between devices, shifts(): return lax.ppermute(value, axis, [(i, (i + k) % SIDE) for i in range(SIDE)])  15 us
    ppermute x4, waiting for transfers between devices, hop(): lax.ppermute(for_high, axes, high)  5.51 us
    pallas_call x1, Pallas kernels, local(): call(forward_kernel, [VMEM] * 5, [shape((2,) + S_SHAPE), shape(ACC, F32),...  5.43 us
    pallas_call x2, Pallas kernels, input_half(): call(functools.partial(input_kernel, first=first), [VMEM] * 9 + [ANY], fr...  4.66 us
    ppermute x1, starting transfers between devices, local(): theirs = lax.ppermute(own, 'dp', swap)  4.33 us
    pallas_call x2, Pallas kernels, mid(): call(functools.partial(mid_kernel, first=first, count=count), [VMEM] * (6...  3.92 us
    ppermute x12, waiting for transfers between devices, shifts(): return lax.ppermute(value, axis, [(i, (i + k) % SIDE) for i in range(SIDE)])  3.8 us
  transfers between devices with their start and end apart: 22, of which 12 were waited for; matrix products, arithmetic and copies ran while one was open for 0% of the time, Pallas kernels for 25%

profile of v5, /device:TPU:1, one launch (start us, length us, event | category | flops | bytes accessed | tf_op | source)
XLA Modules:
  0.0 85.6 jit_solution(9050302449886357179)
XLA Ops:
  1.3 1.7 %prep.1 = (s32[8,128]{1,0:T(8,128)S(1)}, bf16[16,2,64,128]{3,2,1,0:T(8,128)(2,1)S(1)}, bf16[16,2,64,128]{3,2,1,0:T(8,128)(2,1)S(1)}, bf16[16,2,64,128]{3,2,1,0:T(8,128)(2,1)S(1)}, bf16[16,2,64,128]{3,2,1,0:T(8,128)(2,1)S(1)}) custom-call(s32[1,64]{1,0:T(1,128)S(1)} %copy-done.4, bf16[2,32,2,64,128]{4,3,2,1,0:T(8,128)(2,1)} %bitcast.22, ...), custom_call_target="tpu_custom_call" | custom-call | flops 1 | bytes 1 | tf_op jit(solution)/shard_map/prep/pallas_call | solution.py:549
  3.0 9.3 %collective-permute-start = (bf16[16,2,64,128]{3,2,1,0:T(8,128)(2,1)S(1)}, bf16[16,2,64,128]{3,2,1,0:T(8,128)(2,1)S(1)}, u32[]{:S(2)}, u32[]{:S(2)}) collective-permute-start(bf16[16,2,64,128]{3,2,1,0:T(8,128)(2,1)S(1)} %get-tuple-element.42), channel_id=1, source_target_pairs={{1,2},{3,4},{5,6},{7,8},{9,10},{11,12},{13,14},{15,16},{17,18},{19... | collective-permute-start | bytes 1572872 | tf_op jit(solution)/shard_map/ppermute | solution.py:554
  12.5 1.3 %collective-permute-start.5 = (bf16[16,2,64,128]{3,2,1,0:T(8,128)(2,1)S(1)}, bf16[16,2,64,128]{3,2,1,0:T(8,128)(2,1)S(1)}, u32[]{:S(2)}, u32[]{:S(2)}) collective-permute-start(bf16[16,2,64,128]{3,2,1,0:T(8,128)(2,1)S(1)} %get-tuple-element.49), channel_id=1, source_target_pairs={{0,1},{2,3},{4,5},{6,7},{8,9},{10,11},{12,13},{14,15},{16,17},{18,... | collective-permute-start | bytes 1572872 | tf_op jit(solution)/shard_map/ppermute | solution.py:554
  13.8 1.0 %copy-done.2 = bf16[3,3,128,128]{3,2,1,0:T(8,128)(2,1)S(1)} copy-done((bf16[3,3,128,128]{3,2,1,0:T(8,128)(2,1)S(1)}, bf16[3,3,128,128]{3,2,1,0:T(8,128)(2,1)}, u32[]{:S(2)}) %copy-start.2) | copy-done | bytes 294936
  14.8 0.9 %copy-done.3 = bf16[3,128,128]{2,1,0:T(8,128)(2,1)S(1)} copy-done((bf16[3,128,128]{2,1,0:T(8,128)(2,1)S(1)}, bf16[3,128,128]{2,1,0:T(8,128)(2,1)}, u32[]{:S(2)}) %copy-start.3) | copy-done | bytes 98328
  15.6 5.4 %forward.1 = (bf16[2,32,64,256]{3,2,1,0:T(8,128)(2,1)S(1)}, f32[256,1536]{1,0:T(8,128)S(1)}, f32[128,384]{1,0:T(8,128)S(1)}, bf16[1536,256]{1,0:T(8,128)(2,1)S(1...) custom-call(s32[8,128]{1,0:T(8,128)S(1)} %get-tuple-element.40.info, ...), custom_call_target="tpu_custom_call" | custom-call | flops 1 | bytes 1 | tf_op jit(solution)/shard_map/forward/pallas_call | solution.py:560
  21.1 2.9 %collective-permute-done.refs_0_.high_a = bf16[16,2,64,128]{3,2,1,0:T(8,128)(2,1)S(1)} collective-permute-done((bf16[16,2,64,128]{3,2,1,0:T(8,128)(2,1)S(1)}, bf16[16,2,64,128]{3,2,1,0:T(8,128)(2,1)S(1)}, u32[]{:S(2)}, u32[]{:S(2)}) %collective-permute-start) | collective-permute-done | bytes 524320 | tf_op jit(solution)/shard_map/ppermute | solution.py:554
  24.0 0.8 collective-permute-done.1.refs_1_.low_a
  24.8 1.9 %mid.2 = (bf16[2,15,64,256]{3,2,1,0:T(8,128)(2,1)S(1)}, bf16[15,64,256]{2,1,0:T(8,128)(2,1)S(1)}, bf16[16,64,768]{2,1,0:T(8,128)(2,1)S(1)}) custom-call(s32[8,128]{1,0:T(8,128)S(1)} %get-tuple-element.40.info, bf16[16,2,64,128]{3,2,1,0:T(8,128)(2,1)S(1)} %collective-permute-done.refs_0_.high_a, ...), custom_call_target="tpu_custom_call" | custom-call | flops 1 | bytes 1 | tf_op jit(solution)/shard_map/mid/pallas_call | solution.py:569
  26.7 5.8 %collective-permute-start.2 = (bf16[15,64,256]{2,1,0:T(8,128)(2,1)S(1)}, bf16[15,64,256]{2,1,0:T(8,128)(2,1)S(1)}, u32[]{:S(2)}, u32[]{:S(2)}) collective-permute-start(bf16[15,64,256]{2,1,0:T(8,128)(2,1)S(1)} %get-tuple-element.79), channel_id=1, source_target_pairs={{1,2},{3,4},{5,6},{7,8},{9,10},{11,12},{13,14},{15,16},{17,18},{19... | collective-permute-start | bytes 1474568 | tf_op jit(solution)/shard_map/ppermute | solution.py:554
  32.6 2.6 %collective-permute-done.4.refs_2_.high_b = bf16[16,2,64,128]{3,2,1,0:T(8,128)(2,1)S(1)} collective-permute-done((bf16[16,2,64,128]{3,2,1,0:T(8,128)(2,1)S(1)}, bf16[16,2,64,128]{3,2,1,0:T(8,128)(2,1)S(1)}, u32[]{:S(2)}, u32[]{:S(2)}) %collective-permute-start.4) | collective-permute-done | bytes 524320 | tf_op jit(solution)/shard_map/ppermute | solution.py:554
  35.2 0.8 collective-permute-done.5.refs_3_.low_b
  36.0 2.1 %mid.3 = (bf16[2,17,64,256]{3,2,1,0:T(8,128)(2,1)S(1)}, bf16[17,64,256]{2,1,0:T(8,128)(2,1)S(1)}, bf16[18,64,768]{2,1,0:T(8,128)(2,1)S(1)}) custom-call(s32[8,128]{1,0:T(8,128)S(1)} %get-tuple-element.40.info, bf16[16,2,64,128]{3,2,1,0:T(8,128)(2,1)S(1)} %collective-permute-done.refs_0_.high_a, ...), custom_call_target="tpu_custom_call" | custom-call | flops 1 | bytes 1 | tf_op jit(solution)/shard_map/mid/pallas_call | solution.py:569
  38.2 5.8 %collective-permute-start.6 = (bf16[17,64,256]{2,1,0:T(8,128)(2,1)S(1)}, bf16[17,64,256]{2,1,0:T(8,128)(2,1)S(1)}, u32[]{:S(2)}, u32[]{:S(2)}) collective-permute-start(bf16[17,64,256]{2,1,0:T(8,128)(2,1)S(1)} %get-tuple-element.77), channel_id=1, source_target_pairs={{1,2},{3,4},{5,6},{7,8},{9,10},{11,12},{13,14},{15,16},{17,18},{19... | collective-permute-start | bytes 1671176 | tf_op jit(solution)/shard_map/ppermute | solution.py:554
  44.0 2.9 %grads.1 = (f32[4,192,128]{2,1,0:T(8,128)S(1)}, f32[4,192,128]{2,1,0:T(8,128)S(1)}) custom-call(s32[8,128]{1,0:T(8,128)S(1)} %get-tuple-element.40.info, bf16[16,2,64,128]{3,2,1,0:T(8,128)(2,1)S(1)} %collective-permute-done.refs_0_.high_a, bf16[16,2,64,128]{3,2,1,0:T(8,128)(2,1)S(1)} %collective-permute-done.1.refs_1_.low_a, ...), custom_call_target="tpu_custom_call" | custom-call | flops 1 | bytes 1 | tf_op jit(solution)/shard_map/grads/pallas_call | solution.py:583
  47.0 3.1 %collective-permute-start.8 = (f32[4,192,128]{2,1,0:T(8,128)S(1)}, f32[4,192,128]{2,1,0:T(8,128)S(1)}, u32[]{:S(2)}, u32[]{:S(2)}) collective-permute-start(f32[4,192,128]{2,1,0:T(8,128)S(1)} %hold.1), channel_id=1, source_target_pairs={{0,64},{64,0},{1,65},{65,1},{2,66},{66,2},{3,67},{67,3},{4,68},{68... | collective-permute-start | bytes 1179656 | tf_op jit(solution)/shard_map/ppermute | solution.py:592
  50.1 1.3 %collective-permute-done.8.refs_1_ = f32[4,192,128]{2,1,0:T(8,128)S(1)} collective-permute-done((f32[4,192,128]{2,1,0:T(8,128)S(1)}, f32[4,192,128]{2,1,0:T(8,128)S(1)}, u32[]{:S(2)}, u32[]{:S(2)}) %collective-permute-start.8) | collective-permute-done | bytes 393248 | tf_op jit(solution)/shard_map/ppermute | solution.py:592
  51.9 3.4 %collective-permute-start.11 = (bf16[192,128]{1,0:T(8,128)(2,1)S(1)}, bf16[192,128]{1,0:T(8,128)(2,1)S(1)}, u32[]{:S(2)}, u32[]{:S(2)}) collective-permute-start(bf16[192,128]{1,0:T(8,128)(2,1)S(1)} %get-tuple-element.68), channel_id=1, source_target_pairs={{0,48},{16,0},{32,16},{48,32},{1,49},{17,1},{33,17},{49,33},{2,50}... | collective-permute-start | bytes 147464 | tf_op jit(solution)/shard_map/ppermute | solution.py:508
  55.3 1.2 %early_out.1 = (bf16[2,32,2,64,128]{4,3,2,1,0:T(8,128)(2,1)}, f32[8,128]{1,0:T(8,128)S(1)}) custom-call(s32[8,128]{1,0:T(8,128)S(1)} %get-tuple-element.40.info, bf16[2,32,2,64,128]{4,3,2,1,0:T(8,128)(2,1)S(1)} %bitcast.25, bf16[2,32,64,256]{3,2,1,0:T(8,128)(2,1)S(1)} %get-tuple-element.41.refs_2_.refs_4_.s, ...), custom_call_target="tpu_custom_call" | custom-call | flops 1 | bytes 1 | tf_op jit(solution)/shard_map/early_out/pallas_call | solution.py:594
  56.5 1.2 %early_in.1 = (bf16[2,32,2,64,128]{4,3,2,1,0:T(8,128)(2,1)}, f32[8,128]{1,0:T(8,128)S(1)}) custom-call(s32[8,128]{1,0:T(8,128)S(1)} %get-tuple-element.40.info, bf16[2,32,2,64,128]{4,3,2,1,0:T(8,128)(2,1)S(1)} %bitcast.26, bf16[2,32,2,64,128]{4,3,2,1,0:T(8,128)(2,1)S(1)} %bitcast.19, bf16[16,2,64,128]{3,2,1,0:T(8,128)(2,1)S(1)} %collective-permute-done.refs_0_.high_a, ...), custom_call_target="tpu_custom_call" | custom-call | flops 1 | bytes 1 | tf_op jit(solution)/shard_map/early_in/pallas_call | solution.py:597
  57.7 0.7 collective-permute-done.11.refs_3_
  58.4 1.0 %collective-permute-done.9.refs_1_ = bf16[192,128]{1,0:T(8,128)(2,1)S(1)} collective-permute-done((bf16[192,128]{1,0:T(8,128)(2,1)S(1)}, bf16[192,128]{1,0:T(8,128)(2,1)S(1)}, u32[]{:S(2)}, u32[]{:S(2)}) %collective-permute-start.9) | collective-permute-done | bytes 49184 | tf_op jit(solution)/shard_map/ppermute | solution.py:508
  59.7 2.6 %collective-permute-start.14 = (bf16[192,128]{1,0:T(8,128)(2,1)S(1)}, bf16[192,128]{1,0:T(8,128)(2,1)S(1)}, u32[]{:S(2)}, u32[]{:S(2)}) collective-permute-start(bf16[192,128]{1,0:T(8,128)(2,1)S(1)} %x_sum.1.refs_0_), channel_id=1, source_target_pairs={{0,12},{4,0},{8,4},{12,8},{1,13},{5,1},{9,5},{13,9},{2,14},{6,2},{... | collective-permute-start | bytes 147464 | tf_op jit(solution)/shard_map/ppermute | solution.py:508
  62.3 1.6 %output.1 = (bf16[2,32,2,64,128]{4,3,2,1,0:T(8,128)(2,1)}, f32[8,128]{1,0:T(8,128)S(1)}) custom-call(s32[8,128]{1,0:T(8,128)S(1)} %get-tuple-element.40.info, bf16[2,32,2,64,128]{4,3,2,1,0:T(8,128)(2,1)S(1)} %bitcast.27, bf16[2,32,64,256]{3,2,1,0:T(8,128)(2,1)S(1)} %get-tuple-element.41.refs_2_.refs_4_.s, ...), custom_call_target="tpu_custom_call", output_to_operand_aliasing={{0}: (8, {})} | custom-call | flops 1 | bytes 1 | tf_op jit(solution)/shard_map/output/pallas_call | solution.py:601
  65.2 5.3 %collective-permute-start.16 = (bf16[192,128]{1,0:T(8,128)(2,1)S(1)}, bf16[192,128]{1,0:T(8,128)(2,1)S(1)}, u32[]{:S(2)}, u32[]{:S(2)}) collective-permute-start(bf16[192,128]{1,0:T(8,128)(2,1)S(1)} %y_sum.1.refs_0_), channel_id=1, source_target_pairs={{0,2},{1,3},{2,0},{3,1},{4,6},{5,7},{6,4},{7,5},{8,10},{9,11},{10,... | collective-permute-start | bytes 147464 | tf_op jit(solution)/shard_map/ppermute | solution.py:508
  70.6 2.3 %input_grad.2 = (bf16[2,32,2,64,128]{4,3,2,1,0:T(8,128)(2,1)}, f32[8,128]{1,0:T(8,128)S(1)}) custom-call(s32[8,128]{1,0:T(8,128)S(1)} %get-tuple-element.40.info, bf16[2,32,2,64,128]{4,3,2,1,0:T(8,128)(2,1)S(1)} %bitcast.28, bf16[2,32,2,64,128]{4,3,2,1,0:T(8,128)(2,1)S(1)} %bitcast.20, ...), custom_call_target="tpu_custom_call", output_to_operand_aliasing={{0}: (9, {})} | custom-call | flops 1 | bytes 1 | tf_op jit(solution)/shard_map/input_grad/pallas_call | solution.py:607
  72.9 0.9 %collective-permute-done.17.refs_3_ = bf16[192,128]{1,0:T(8,128)(2,1)S(1)} collective-permute-done((bf16[192,128]{1,0:T(8,128)(2,1)S(1)}, bf16[192,128]{1,0:T(8,128)(2,1)S(1)}, u32[]{:S(2)}, u32[]{:S(2)}) %collective-permute-start.17) | collective-permute-done | bytes 49184 | tf_op jit(solution)/shard_map/ppermute | solution.py:508
  74.0 2.6 %collective-permute-start.20 = (bf16[192,128]{1,0:T(8,128)(2,1)S(1)}, bf16[192,128]{1,0:T(8,128)(2,1)S(1)}, u32[]{:S(2)}, u32[]{:S(2)}) collective-permute-start(bf16[192,128]{1,0:T(8,128)(2,1)S(1)} %z_sum.1.refs_0_), channel_id=1, source_target_pairs={{0,48},{16,0},{32,16},{48,32},{1,49},{17,1},{33,17},{49,33},{2,50}... | collective-permute-start | bytes 147464 | tf_op jit(solution)/shard_map/ppermute | solution.py:508
  76.6 2.3 %input_grad.3 = (bf16[2,32,2,64,128]{4,3,2,1,0:T(8,128)(2,1)}, f32[8,128]{1,0:T(8,128)S(1)}) custom-call(s32[8,128]{1,0:T(8,128)S(1)} %get-tuple-element.40.info, bf16[2,32,2,64,128]{4,3,2,1,0:T(8,128)(2,1)S(1)} %bitcast.29, bf16[2,32,2,64,128]{4,3,2,1,0:T(8,128)(2,1)S(1)} %bitcast.21, ...), custom_call_target="tpu_custom_call", output_to_operand_aliasing={{0}: (9, {})} | custom-call | flops 1 | bytes 1 | tf_op jit(solution)/shard_map/input_grad/pallas_call | solution.py:607
  79.2 4.3 %collective-permute-start.21 = (bf16[4,192,128]{2,1,0:T(8,128)(2,1)S(1)}, bf16[4,192,128]{2,1,0:T(8,128)(2,1)S(1)}, u32[]{:S(2)}, u32[]{:S(2)}) collective-permute-start(bf16[4,192,128]{2,1,0:T(8,128)(2,1)S(1)} %x_stack.1.mine), channel_id=1, source_target_pairs={{0,64},{64,0},{1,65},{65,1},{2,66},{66,2},{3,67},{67,3},{4,68},{68... | collective-permute-start | bytes 589832 | tf_op jit(solution)/shard_map/ppermute | solution.py:621
  83.5 1.1 %collective-permute-done.21.theirs = bf16[4,192,128]{2,1,0:T(8,128)(2,1)S(1)} collective-permute-done((bf16[4,192,128]{2,1,0:T(8,128)(2,1)S(1)}, bf16[4,192,128]{2,1,0:T(8,128)(2,1)S(1)}, u32[]{:S(2)}, u32[]{:S(2)}) %collective-permute-start.21) | collective-permute-done | bytes 196640 | tf_op jit(solution)/shard_map/ppermute | solution.py:621
  84.6 1.1 %place.1 = (f32[1152,128]{1,0:T(8,128)}, f32[384,128]{1,0:T(8,128)}) custom-call(s32[8,128]{1,0:T(8,128)S(1)} %get-tuple-element.40.info, bf16[4,192,128]{2,1,0:T(8,128)(2,1)S(1)} %x_stack.1.mine, bf16[4,192,128]{2,1,0:T(8,128)(2,1)S(1)} %collective-permute-done.21.theirs), custom_call_target="tpu_custom_call" | custom-call | flops 1 | bytes 1 | tf_op jit(solution)/shard_map/place/pallas_call | solution.py:622
  (41 shorter events, 3.6 us)
Async XLA Ops:
  0.6 0.7 copy-start.4
  1.3 12.5 %copy-start = (bf16[2,64,64,128]{3,2,1,0:T(8,128)(2,1)S(1)}, bf16[2,64,64,128]{3,2,1,0:T(8,128)(2,1)}, u32[]{:S(2)}) copy-start(bf16[2,64,64,128]{3,2,1,0:T(8,128)(2,1)} %param.6) | copy-start | bytes 6291460
  1.3 12.5 %copy-start.1 = (bf16[2,64,64,128]{3,2,1,0:T(8,128)(2,1)S(1)}, bf16[2,64,64,128]{3,2,1,0:T(8,128)(2,1)}, u32[]{:S(2)}) copy-start(bf16[2,64,64,128]{3,2,1,0:T(8,128)(2,1)} %param.5) | copy-start | bytes 6291460
  3.0 21.0 %collective-permute-start = (bf16[16,2,64,128]{3,2,1,0:T(8,128)(2,1)S(1)}, bf16[16,2,64,128]{3,2,1,0:T(8,128)(2,1)S(1)}, u32[]{:S(2)}, u32[]{:S(2)}) collective-permute-start(bf16[16,2,64,128]{3,2,1,0:T(8,128)(2,1)S(1)} %get-tuple-element.42), channel_id=1, source_target_pairs={{1,2},{3,4},{5,6},{7,8},{9,10},{11,12},{13,14},{15,16},{17,18},{19... | collective-permute-start | bytes 1572872 | tf_op jit(solution)/shard_map/ppermute | solution.py:554
  12.3 12.5 %collective-permute-start.1 = (bf16[16,2,64,128]{3,2,1,0:T(8,128)(2,1)S(1)}, bf16[16,2,64,128]{3,2,1,0:T(8,128)(2,1)S(1)}, u32[]{:S(2)}, u32[]{:S(2)}) collective-permute-start(bf16[16,2,64,128]{3,2,1,0:T(8,128)(2,1)S(1)} %get-tuple-element.43), channel_id=1, source_target_pairs={{0,1},{2,3},{4,5},{6,7},{8,9},{10,11},{12,13},{14,15},{16,17},{18,... | collective-permute-start | bytes 1572872 | tf_op jit(solution)/shard_map/ppermute | solution.py:554
  12.3 22.9 %collective-permute-start.4 = (bf16[16,2,64,128]{3,2,1,0:T(8,128)(2,1)S(1)}, bf16[16,2,64,128]{3,2,1,0:T(8,128)(2,1)S(1)}, u32[]{:S(2)}, u32[]{:S(2)}) collective-permute-start(bf16[16,2,64,128]{3,2,1,0:T(8,128)(2,1)S(1)} %get-tuple-element.48), channel_id=1, source_target_pairs={{1,2},{3,4},{5,6},{7,8},{9,10},{11,12},{13,14},{15,16},{17,18},{19... | collective-permute-start | bytes 1572872 | tf_op jit(solution)/shard_map/ppermute | solution.py:554
  12.5 23.5 %collective-permute-start.5 = (bf16[16,2,64,128]{3,2,1,0:T(8,128)(2,1)S(1)}, bf16[16,2,64,128]{3,2,1,0:T(8,128)(2,1)S(1)}, u32[]{:S(2)}, u32[]{:S(2)}) collective-permute-start(bf16[16,2,64,128]{3,2,1,0:T(8,128)(2,1)S(1)} %get-tuple-element.49), channel_id=1, source_target_pairs={{0,1},{2,3},{4,5},{6,7},{8,9},{10,11},{12,13},{14,15},{16,17},{18,... | collective-permute-start | bytes 1572872 | tf_op jit(solution)/shard_map/ppermute | solution.py:554
  13.8 1.0 %copy-start.2 = (bf16[3,3,128,128]{3,2,1,0:T(8,128)(2,1)S(1)}, bf16[3,3,128,128]{3,2,1,0:T(8,128)(2,1)}, u32[]{:S(2)}) copy-start(bf16[3,3,128,128]{3,2,1,0:T(8,128)(2,1)} %w_ref.1) | copy-start | bytes 884740
  14.8 0.9 %copy-start.3 = (bf16[3,128,128]{2,1,0:T(8,128)(2,1)S(1)}, bf16[3,128,128]{2,1,0:T(8,128)(2,1)}, u32[]{:S(2)}) copy-start(bf16[3,128,128]{2,1,0:T(8,128)(2,1)} %tw_ref.1) | copy-start | bytes 294916
  26.7 20.2 %collective-permute-start.2 = (bf16[15,64,256]{2,1,0:T(8,128)(2,1)S(1)}, bf16[15,64,256]{2,1,0:T(8,128)(2,1)S(1)}, u32[]{:S(2)}, u32[]{:S(2)}) collective-permute-start(bf16[15,64,256]{2,1,0:T(8,128)(2,1)S(1)} %get-tuple-element.79), channel_id=1, source_target_pairs={{1,2},{3,4},{5,6},{7,8},{9,10},{11,12},{13,14},{15,16},{17,18},{19... | collective-permute-start | bytes 1474568 | tf_op jit(solution)/shard_map/ppermute | solution.py:554
  32.6 14.4 %collective-permute-start.3 = (bf16[15,64,256]{2,1,0:T(8,128)(2,1)S(1)}, bf16[15,64,256]{2,1,0:T(8,128)(2,1)S(1)}, u32[]{:S(2)}, u32[]{:S(2)}) collective-permute-start(bf16[15,64,256]{2,1,0:T(8,128)(2,1)S(1)} %get-tuple-element.78), channel_id=1, source_target_pairs={{0,1},{2,3},{4,5},{6,7},{8,9},{10,11},{12,13},{14,15},{16,17},{18,... | collective-permute-start | bytes 1474568 | tf_op jit(solution)/shard_map/ppermute | solution.py:554
  38.2 24.0 %collective-permute-start.6 = (bf16[17,64,256]{2,1,0:T(8,128)(2,1)S(1)}, bf16[17,64,256]{2,1,0:T(8,128)(2,1)S(1)}, u32[]{:S(2)}, u32[]{:S(2)}) collective-permute-start(bf16[17,64,256]{2,1,0:T(8,128)(2,1)S(1)} %get-tuple-element.77), channel_id=1, source_target_pairs={{1,2},{3,4},{5,6},{7,8},{9,10},{11,12},{13,14},{15,16},{17,18},{19... | collective-permute-start | bytes 1671176 | tf_op jit(solution)/shard_map/ppermute | solution.py:554
  44.0 18.2 %collective-permute-start.7 = (bf16[17,64,256]{2,1,0:T(8,128)(2,1)S(1)}, bf16[17,64,256]{2,1,0:T(8,128)(2,1)S(1)}, u32[]{:S(2)}, u32[]{:S(2)}) collective-permute-start(bf16[17,64,256]{2,1,0:T(8,128)(2,1)S(1)} %get-tuple-element.76), channel_id=1, source_target_pairs={{0,1},{2,3},{4,5},{6,7},{8,9},{10,11},{12,13},{14,15},{16,17},{18,... | collective-permute-start | bytes 1671176 | tf_op jit(solution)/shard_map/ppermute | solution.py:554
  47.0 4.4 %collective-permute-start.8 = (f32[4,192,128]{2,1,0:T(8,128)S(1)}, f32[4,192,128]{2,1,0:T(8,128)S(1)}, u32[]{:S(2)}, u32[]{:S(2)}) collective-permute-start(f32[4,192,128]{2,1,0:T(8,128)S(1)} %hold.1), channel_id=1, source_target_pairs={{0,64},{64,0},{1,65},{65,1},{2,66},{66,2},{3,67},{67,3},{4,68},{68... | collective-permute-start | bytes 1179656 | tf_op jit(solution)/shard_map/ppermute | solution.py:592
  51.5 6.2 %collective-permute-start.10 = (bf16[192,128]{1,0:T(8,128)(2,1)S(1)}, bf16[192,128]{1,0:T(8,128)(2,1)S(1)}, u32[]{:S(2)}, u32[]{:S(2)}) collective-permute-start(bf16[192,128]{1,0:T(8,128)(2,1)S(1)} %get-tuple-element.67), channel_id=1, source_target_pairs={{0,32},{16,48},{32,0},{48,16},{1,33},{17,49},{33,1},{49,17},{2,34}... | collective-permute-start | bytes 147464 | tf_op jit(solution)/shard_map/ppermute | solution.py:508
  51.9 6.5 %collective-permute-start.11 = (bf16[192,128]{1,0:T(8,128)(2,1)S(1)}, bf16[192,128]{1,0:T(8,128)(2,1)S(1)}, u32[]{:S(2)}, u32[]{:S(2)}) collective-permute-start(bf16[192,128]{1,0:T(8,128)(2,1)S(1)} %get-tuple-element.68), channel_id=1, source_target_pairs={{0,48},{16,0},{32,16},{48,32},{1,49},{17,1},{33,17},{49,33},{2,50}... | collective-permute-start | bytes 147464 | tf_op jit(solution)/shard_map/ppermute | solution.py:508
  55.3 4.2 %collective-permute-start.9 = (bf16[192,128]{1,0:T(8,128)(2,1)S(1)}, bf16[192,128]{1,0:T(8,128)(2,1)S(1)}, u32[]{:S(2)}, u32[]{:S(2)}) collective-permute-start(bf16[192,128]{1,0:T(8,128)(2,1)S(1)} %get-tuple-element.66), channel_id=1, source_target_pairs={{0,16},{16,32},{32,48},{48,0},{1,17},{17,33},{33,49},{49,1},{2,18}... | collective-permute-start | bytes 147464 | tf_op jit(solution)/shard_map/ppermute | solution.py:508
  59.5 4.7 %collective-permute-start.12 = (bf16[192,128]{1,0:T(8,128)(2,1)S(1)}, bf16[192,128]{1,0:T(8,128)(2,1)S(1)}, u32[]{:S(2)}, u32[]{:S(2)}) collective-permute-start(bf16[192,128]{1,0:T(8,128)(2,1)S(1)} %x_sum.1.refs_0_), channel_id=1, source_target_pairs={{0,4},{4,8},{8,12},{12,0},{1,5},{5,9},{9,13},{13,1},{2,6},{6,10},{... | collective-permute-start | bytes 147464 | tf_op jit(solution)/shard_map/ppermute | solution.py:508
  59.6 4.7 %collective-permute-start.13 = (bf16[192,128]{1,0:T(8,128)(2,1)S(1)}, bf16[192,128]{1,0:T(8,128)(2,1)S(1)}, u32[]{:S(2)}, u32[]{:S(2)}) collective-permute-start(bf16[192,128]{1,0:T(8,128)(2,1)S(1)} %x_sum.1.refs_0_), channel_id=1, source_target_pairs={{0,8},{4,12},{8,0},{12,4},{1,9},{5,13},{9,1},{13,5},{2,10},{6,14},... | collective-permute-start | bytes 147464 | tf_op jit(solution)/shard_map/ppermute | solution.py:508
  59.7 5.1 %collective-permute-start.14 = (bf16[192,128]{1,0:T(8,128)(2,1)S(1)}, bf16[192,128]{1,0:T(8,128)(2,1)S(1)}, u32[]{:S(2)}, u32[]{:S(2)}) collective-permute-start(bf16[192,128]{1,0:T(8,128)(2,1)S(1)} %x_sum.1.refs_0_), channel_id=1, source_target_pairs={{0,12},{4,0},{8,4},{12,8},{1,13},{5,1},{9,5},{13,9},{2,14},{6,2},{... | collective-permute-start | bytes 147464 | tf_op jit(solution)/shard_map/ppermute | solution.py:508
  64.9 8.1 %collective-permute-start.15 = (bf16[192,128]{1,0:T(8,128)(2,1)S(1)}, bf16[192,128]{1,0:T(8,128)(2,1)S(1)}, u32[]{:S(2)}, u32[]{:S(2)}) collective-permute-start(bf16[192,128]{1,0:T(8,128)(2,1)S(1)} %y_sum.1.refs_0_), channel_id=1, source_target_pairs={{0,1},{1,2},{2,3},{3,0},{4,5},{5,6},{6,7},{7,4},{8,9},{9,10},{10,1... | collective-permute-start | bytes 147464 | tf_op jit(solution)/shard_map/ppermute | solution.py:508
  65.2 7.7 %collective-permute-start.16 = (bf16[192,128]{1,0:T(8,128)(2,1)S(1)}, bf16[192,128]{1,0:T(8,128)(2,1)S(1)}, u32[]{:S(2)}, u32[]{:S(2)}) collective-permute-start(bf16[192,128]{1,0:T(8,128)(2,1)S(1)} %y_sum.1.refs_0_), channel_id=1, source_target_pairs={{0,2},{1,3},{2,0},{3,1},{4,6},{5,7},{6,4},{7,5},{8,10},{9,11},{10,... | collective-permute-start | bytes 147464 | tf_op jit(solution)/shard_map/ppermute | solution.py:508
  70.6 3.2 %collective-permute-start.17 = (bf16[192,128]{1,0:T(8,128)(2,1)S(1)}, bf16[192,128]{1,0:T(8,128)(2,1)S(1)}, u32[]{:S(2)}, u32[]{:S(2)}) collective-permute-start(bf16[192,128]{1,0:T(8,128)(2,1)S(1)} %y_sum.1.refs_0_), channel_id=1, source_target_pairs={{0,3},{1,0},{2,1},{3,2},{4,7},{5,4},{6,5},{7,6},{8,11},{9,8},{10,9... | collective-permute-start | bytes 147464 | tf_op jit(solution)/shard_map/ppermute | solution.py:508
  73.8 5.1 %collective-permute-start.18 = (bf16[192,128]{1,0:T(8,128)(2,1)S(1)}, bf16[192,128]{1,0:T(8,128)(2,1)S(1)}, u32[]{:S(2)}, u32[]{:S(2)}) collective-permute-start(bf16[192,128]{1,0:T(8,128)(2,1)S(1)} %z_sum.1.refs_0_), channel_id=1, source_target_pairs={{0,16},{16,32},{32,48},{48,0},{1,17},{17,33},{33,49},{49,1},{2,18}... | collective-permute-start | bytes 147464 | tf_op jit(solution)/shard_map/ppermute | solution.py:508
  73.9 5.0 %collective-permute-start.19 = (bf16[192,128]{1,0:T(8,128)(2,1)S(1)}, bf16[192,128]{1,0:T(8,128)(2,1)S(1)}, u32[]{:S(2)}, u32[]{:S(2)}) collective-permute-start(bf16[192,128]{1,0:T(8,128)(2,1)S(1)} %z_sum.1.refs_0_), channel_id=1, source_target_pairs={{0,32},{16,48},{32,0},{48,16},{1,33},{17,49},{33,1},{49,17},{2,34}... | collective-permute-start | bytes 147464 | tf_op jit(solution)/shard_map/ppermute | solution.py:508
  74.0 5.1 %collective-permute-start.20 = (bf16[192,128]{1,0:T(8,128)(2,1)S(1)}, bf16[192,128]{1,0:T(8,128)(2,1)S(1)}, u32[]{:S(2)}, u32[]{:S(2)}) collective-permute-start(bf16[192,128]{1,0:T(8,128)(2,1)S(1)} %z_sum.1.refs_0_), channel_id=1, source_target_pairs={{0,48},{16,0},{32,16},{48,32},{1,49},{17,1},{33,17},{49,33},{2,50}... | collective-permute-start | bytes 147464 | tf_op jit(solution)/shard_map/ppermute | solution.py:508
  79.2 5.4 %collective-permute-start.21 = (bf16[4,192,128]{2,1,0:T(8,128)(2,1)S(1)}, bf16[4,192,128]{2,1,0:T(8,128)(2,1)S(1)}, u32[]{:S(2)}, u32[]{:S(2)}) collective-permute-start(bf16[4,192,128]{2,1,0:T(8,128)(2,1)S(1)} %x_stack.1.mine), channel_id=1, source_target_pairs={{0,64},{64,0},{1,65},{65,1},{2,66},{66,2},{3,67},{67,3},{4,68},{68... | collective-permute-start | bytes 589832 | tf_op jit(solution)/shard_map/ppermute | solution.py:621

commit v6 on v5

--- a/solution.py
+++ b/solution.py
@@ -161,23 +161,21 @@
     return read
 
 
-def prep_kernel(counts, x_hbm, g_hbm, info, high_a, low_a, high_b, low_b, sems):
+def prep_kernel(counts, x_hbm, g_hbm, info, high_ref, low_ref, sems):
     here = (lax.axis_index("x") * SIDE + lax.axis_index("y")) * SIDE + lax.axis_index("z")
     even = here % 2 == 0
 
-    top, bottom = pl.ds(0, CUT1), pl.ds(CUT1, PAIRS - CUT1)
+    rows = pl.ds(0, CUT1)
 
     def put(source, slot, for_high, n):
-        a = copy_either(for_high, (source.at[slot, top], high_a), (source.at[slot, top], low_a), sems.at[n])
-        b = copy_either(for_high, (source.at[slot, bottom], high_b), (source.at[slot, bottom], low_b), sems.at[n + 1])
-        return [a, b]
+        return [copy_either(for_high, (source.at[slot, rows], high_ref), (source.at[slot, rows], low_ref), sems.at[n])]
 
     copies = put(g_hbm, 0, even, 0)
     c = counts[...].astype(F32)
     order = lax.broadcasted_iota(jnp.int32, c.shape, 1)
     start = jnp.sum(jnp.where(order < here, c, 0.0)).astype(jnp.int32)
     count = jnp.sum(jnp.where(order == here, c, 0.0)).astype(jnp.int32)
-    copies += put(x_hbm, jnp.where(count == 2, 1, 0), jnp.logical_not(even), 2)
+    copies += put(x_hbm, jnp.where(count == 2, 1, 0), jnp.logical_not(even), 1)
     first = start % FRAMES
     second = (first + 1) % FRAMES
     final = FRAMES - 1
@@ -198,6 +196,19 @@
     for n, value in values.items():
         found = jnp.where(lane == n, value, found)
     info[...] = found
+    for c in copies:
+        c.wait()
+
+
+def prep2_kernel(info, x_hbm, g_hbm, high_ref, low_ref, sems):
+    even = is_set(info, EVEN)
+    last = jnp.where(is_two(info), 1, 0)
+    rows = pl.ds(CUT1, PAIRS - CUT1)
+    down, up = g_hbm.at[0, rows], x_hbm.at[last, rows]
+    copies = [
+        copy_either(even, (down, high_ref), (down, low_ref), sems.at[0]),
+        copy_either(even, (up, low_ref), (up, high_ref), sems.at[1]),
+    ]
     for c in copies:
         c.wait()
 
@@ -545,16 +556,18 @@
     high = [(i + 1, (i + 2) % N_SP) for i in lows] + [((i + 2) % N_SP, i + 1) for i in lows]
     swap = [(0, 1), (1, 0)]
 
-    parts = [shape((n, 2, COLS, CH)) for n in (CUT1, CUT1, PAIRS - CUT1, PAIRS - CUT1)]
-    info, *sent = call(
-        prep_kernel, [VMEM, HBM, HBM], [shape(INFO, jnp.int32)] + parts, [SEM((4,))], "prep", [VMEM] + [ANY] * 4
-    )(frame_counts, in_hbm(x), in_hbm(g))
+    top, bottom = shape((CUT1, 2, COLS, CH)), shape((PAIRS - CUT1, 2, COLS, CH))
+    x_hbm, g_hbm = in_hbm(x), in_hbm(g)
+    info, *sent1 = call(
+        prep_kernel, [VMEM, HBM, HBM], [shape(INFO, jnp.int32), top, top], [SEM((2,))], "prep", [VMEM, ANY, ANY]
+    )(frame_counts, x_hbm, g_hbm)
+    sent2 = call(prep2_kernel, [VMEM, HBM, HBM], [bottom, bottom], [SEM((2,))], "prep2", [ANY, ANY])(info, x_hbm, g_hbm)
 
     def hop(for_high, for_low):
         return lax.ppermute(for_high, axes, high), lax.ppermute(for_low, axes, low)
 
-    hop1_a = hop(*sent[0:2])
-    hop1_b = hop(*sent[2:4])
+    hop1_a = hop(*sent1)
+    hop1_b = hop(*sent2)
     hop1 = hop1_a + hop1_b
 
     s, acc, tacc, wf, wb, tf, tb = call(

time: 86.6 us -> 86.7 us (level); the launches traced: 85.6 us -> 87.2 us
  local copies, waits for them, and re-layouts: 2.71 us -> 0.87 us
  starting transfers between devices: 44.8 us -> 46.3 us
  Pallas kernels: 23.9 us -> 24.9 us
    unnamed x10, local copies, waits for them, and re-layouts: 2.51 us -> 0.66 us
    pallas_call x1 -> x2, Pallas kernels: 1.71 us -> 2.76 us  [the longest x1 1.47 us: local(): call(prep2_kernel, [VMEM, HBM, HBM], [bottom, bottom], [SEM((2,))], 'prep...]
  transfers between devices with their start and end apart: 22 -> 22, of which waited for: 12 -> 13; matrix products, arithmetic and copies ran while one was open for 0% -> 0% of each run, Pallas kernels for 25% -> 26%
where the time goes in v6:
time: 86.7 us; the launch traced here: 87.2 us
  starting transfers between devices  46.3 us (53%)
  Pallas kernels  24.9 us (29%)
  waiting for transfers between devices  14.2 us (16%)
  local copies, waits for them, and re-layouts  0.87 us (1%)
    ppermute x4, starting transfers between devices, hop(): lax.ppermute(for_high, axes, high)  21.3 us
    ppermute x12, starting transfers between devices, shifts(): return lax.ppermute(value, axis, [(i, (i + k) % SIDE) for i in range(SIDE)])  15.6 us
    ppermute x4, waiting for transfers between devices, hop(): lax.ppermute(for_high, axes, high)  5.7 us
    pallas_call x1, Pallas kernels, local(): call(forward_kernel, [VMEM] * 5, [shape((2,) + S_SHAPE), shape(ACC, F32),...  5.43 us
    ppermute x1, starting transfers between devices, local(): theirs = lax.ppermute(own, 'dp', swap)  5.07 us
    pallas_call x2, Pallas kernels, input_half(): call(functools.partial(input_kernel, first=first), [VMEM] * 9 + [ANY], fr...  4.66 us
    ppermute x12, waiting for transfers between devices, shifts(): return lax.ppermute(value, axis, [(i, (i + k) % SIDE) for i in range(SIDE)])  4.46 us
    pallas_call x2, Pallas kernels, mid(): call(functools.partial(mid_kernel, first=first, count=count), [VMEM] * (6...  3.91 us
  transfers between devices with their start and end apart: 22, of which 13 were waited for; matrix products, arithmetic and copies ran while one was open for 0% of the time, Pallas kernels for 26%

profile of v6, /device:TPU:1, one launch (start us, length us, event | category | flops | bytes accessed | tf_op | source)
XLA Modules:
  0.0 87.2 jit_solution(11838562278190880599)
XLA Ops:
  0.6 0.6 copy-done.4
  1.3 1.3 %prep.1 = (s32[8,128]{1,0:T(8,128)S(1)}, bf16[16,2,64,128]{3,2,1,0:T(8,128)(2,1)S(1)}, bf16[16,2,64,128]{3,2,1,0:T(8,128)(2,1)S(1)}) custom-call(s32[1,64]{1,0:T(1,128)S(1)} %copy-done.4, bf16[2,32,2,64,128]{4,3,2,1,0:T(8,128)(2,1)} %bitcast.23, bf16[2,32,2,64,128]{4,3,2,1,0:T(8,128)(2,1)} %bitcast.14), custom_call_target="tpu_custom_call" | custom-call | flops 1 | bytes 1 | tf_op jit(solution)/shard_map/prep/pallas_call | solution.py:561
  2.6 9.3 %collective-permute-start = (bf16[16,2,64,128]{3,2,1,0:T(8,128)(2,1)S(1)}, bf16[16,2,64,128]{3,2,1,0:T(8,128)(2,1)S(1)}, u32[]{:S(2)}, u32[]{:S(2)}) collective-permute-start(bf16[16,2,64,128]{3,2,1,0:T(8,128)(2,1)S(1)} %get-tuple-element.42), channel_id=1, source_target_pairs={{1,2},{3,4},{5,6},{7,8},{9,10},{11,12},{13,14},{15,16},{17,18},{19... | collective-permute-start | bytes 1572872 | tf_op jit(solution)/shard_map/ppermute | solution.py:567
  11.9 1.5 %prep2.1 = (bf16[16,2,64,128]{3,2,1,0:T(8,128)(2,1)S(1)}, bf16[16,2,64,128]{3,2,1,0:T(8,128)(2,1)S(1)}) custom-call(s32[8,128]{1,0:T(8,128)S(1)} %get-tuple-element.40.info, bf16[2,32,2,64,128]{4,3,2,1,0:T(8,128)(2,1)} %bitcast.24, bf16[2,32,2,64,128]{4,3,2,1,0:T(8,128)(2,1)} %bitcast.15), custom_call_target="tpu_custom_call" | custom-call | flops 1 | bytes 1 | tf_op jit(solution)/shard_map/prep2/pallas_call | solution.py:564
  13.7 1.3 %collective-permute-start.5 = (bf16[16,2,64,128]{3,2,1,0:T(8,128)(2,1)S(1)}, bf16[16,2,64,128]{3,2,1,0:T(8,128)(2,1)S(1)}, u32[]{:S(2)}, u32[]{:S(2)}) collective-permute-start(bf16[16,2,64,128]{3,2,1,0:T(8,128)(2,1)S(1)} %get-tuple-element.49), channel_id=1, source_target_pairs={{0,1},{2,3},{4,5},{6,7},{8,9},{10,11},{12,13},{14,15},{16,17},{18,... | collective-permute-start | bytes 1572872 | tf_op jit(solution)/shard_map/ppermute | solution.py:567
  15.0 5.4 %forward.1 = (bf16[2,32,64,256]{3,2,1,0:T(8,128)(2,1)S(1)}, f32[256,1536]{1,0:T(8,128)S(1)}, f32[128,384]{1,0:T(8,128)S(1)}, bf16[1536,256]{1,0:T(8,128)(2,1)S(1...) custom-call(s32[8,128]{1,0:T(8,128)S(1)} %get-tuple-element.40.info, ...), custom_call_target="tpu_custom_call" | custom-call | flops 1 | bytes 1 | tf_op jit(solution)/shard_map/forward/pallas_call | solution.py:573
  20.5 3.1 %collective-permute-done.refs_0_.high_a = bf16[16,2,64,128]{3,2,1,0:T(8,128)(2,1)S(1)} collective-permute-done((bf16[16,2,64,128]{3,2,1,0:T(8,128)(2,1)S(1)}, bf16[16,2,64,128]{3,2,1,0:T(8,128)(2,1)S(1)}, u32[]{:S(2)}, u32[]{:S(2)}) %collective-permute-start) | collective-permute-done | bytes 524320 | tf_op jit(solution)/shard_map/ppermute | solution.py:567
  23.6 0.8 collective-permute-done.1.refs_1_.low_a
  24.4 1.9 %mid.2 = (bf16[2,15,64,256]{3,2,1,0:T(8,128)(2,1)S(1)}, bf16[15,64,256]{2,1,0:T(8,128)(2,1)S(1)}, bf16[16,64,768]{2,1,0:T(8,128)(2,1)S(1)}) custom-call(s32[8,128]{1,0:T(8,128)S(1)} %get-tuple-element.40.info, bf16[16,2,64,128]{3,2,1,0:T(8,128)(2,1)S(1)} %collective-permute-done.refs_0_.high_a, ...), custom_call_target="tpu_custom_call" | custom-call | flops 1 | bytes 1 | tf_op jit(solution)/shard_map/mid/pallas_call | solution.py:582
  26.3 5.8 %collective-permute-start.2 = (bf16[15,64,256]{2,1,0:T(8,128)(2,1)S(1)}, bf16[15,64,256]{2,1,0:T(8,128)(2,1)S(1)}, u32[]{:S(2)}, u32[]{:S(2)}) collective-permute-start(bf16[15,64,256]{2,1,0:T(8,128)(2,1)S(1)} %get-tuple-element.79), channel_id=1, source_target_pairs={{1,2},{3,4},{5,6},{7,8},{9,10},{11,12},{13,14},{15,16},{17,18},{19... | collective-permute-start | bytes 1474568 | tf_op jit(solution)/shard_map/ppermute | solution.py:567
  32.2 2.6 %collective-permute-done.4.refs_2_.high_b = bf16[16,2,64,128]{3,2,1,0:T(8,128)(2,1)S(1)} collective-permute-done((bf16[16,2,64,128]{3,2,1,0:T(8,128)(2,1)S(1)}, bf16[16,2,64,128]{3,2,1,0:T(8,128)(2,1)S(1)}, u32[]{:S(2)}, u32[]{:S(2)}) %collective-permute-start.4) | collective-permute-done | bytes 524320 | tf_op jit(solution)/shard_map/ppermute | solution.py:567
  34.8 0.8 collective-permute-done.5.refs_3_.low_b
  35.6 2.1 %mid.3 = (bf16[2,17,64,256]{3,2,1,0:T(8,128)(2,1)S(1)}, bf16[17,64,256]{2,1,0:T(8,128)(2,1)S(1)}, bf16[18,64,768]{2,1,0:T(8,128)(2,1)S(1)}) custom-call(s32[8,128]{1,0:T(8,128)S(1)} %get-tuple-element.40.info, bf16[16,2,64,128]{3,2,1,0:T(8,128)(2,1)S(1)} %collective-permute-done.refs_0_.high_a, ...), custom_call_target="tpu_custom_call" | custom-call | flops 1 | bytes 1 | tf_op jit(solution)/shard_map/mid/pallas_call | solution.py:582
  37.8 5.8 %collective-permute-start.6 = (bf16[17,64,256]{2,1,0:T(8,128)(2,1)S(1)}, bf16[17,64,256]{2,1,0:T(8,128)(2,1)S(1)}, u32[]{:S(2)}, u32[]{:S(2)}) collective-permute-start(bf16[17,64,256]{2,1,0:T(8,128)(2,1)S(1)} %get-tuple-element.77), channel_id=1, source_target_pairs={{1,2},{3,4},{5,6},{7,8},{9,10},{11,12},{13,14},{15,16},{17,18},{19... | collective-permute-start | bytes 1671176 | tf_op jit(solution)/shard_map/ppermute | solution.py:567
  43.6 2.9 %grads.1 = (f32[4,192,128]{2,1,0:T(8,128)S(1)}, f32[4,192,128]{2,1,0:T(8,128)S(1)}) custom-call(s32[8,128]{1,0:T(8,128)S(1)} %get-tuple-element.40.info, bf16[16,2,64,128]{3,2,1,0:T(8,128)(2,1)S(1)} %collective-permute-done.refs_0_.high_a, bf16[16,2,64,128]{3,2,1,0:T(8,128)(2,1)S(1)} %collective-permute-done.1.refs_1_.low_a, ...), custom_call_target="tpu_custom_call" | custom-call | flops 1 | bytes 1 | tf_op jit(solution)/shard_map/grads/pallas_call | solution.py:596
  46.6 3.1 %collective-permute-start.8 = (f32[4,192,128]{2,1,0:T(8,128)S(1)}, f32[4,192,128]{2,1,0:T(8,128)S(1)}, u32[]{:S(2)}, u32[]{:S(2)}) collective-permute-start(f32[4,192,128]{2,1,0:T(8,128)S(1)} %hold.1), channel_id=1, source_target_pairs={{0,64},{64,0},{1,65},{65,1},{2,66},{66,2},{3,67},{67,3},{4,68},{68... | collective-permute-start | bytes 1179656 | tf_op jit(solution)/shard_map/ppermute | solution.py:605
  49.7 1.3 %collective-permute-done.8.refs_1_ = f32[4,192,128]{2,1,0:T(8,128)S(1)} collective-permute-done((f32[4,192,128]{2,1,0:T(8,128)S(1)}, f32[4,192,128]{2,1,0:T(8,128)S(1)}, u32[]{:S(2)}, u32[]{:S(2)}) %collective-permute-start.8) | collective-permute-done | bytes 393248 | tf_op jit(solution)/shard_map/ppermute | solution.py:605
  51.5 0.9 collective-permute-start.11
  53.0 1.2 %early_out.1 = (bf16[2,32,2,64,128]{4,3,2,1,0:T(8,128)(2,1)}, f32[8,128]{1,0:T(8,128)S(1)}) custom-call(s32[8,128]{1,0:T(8,128)S(1)} %get-tuple-element.40.info, bf16[2,32,2,64,128]{4,3,2,1,0:T(8,128)(2,1)S(1)} %bitcast.27, bf16[2,32,64,256]{3,2,1,0:T(8,128)(2,1)S(1)} %get-tuple-element.41.refs_2_.refs_4_.s, ...), custom_call_target="tpu_custom_call" | custom-call | flops 1 | bytes 1 | tf_op jit(solution)/shard_map/early_out/pallas_call | solution.py:607
  54.2 1.2 %early_in.1 = (bf16[2,32,2,64,128]{4,3,2,1,0:T(8,128)(2,1)}, f32[8,128]{1,0:T(8,128)S(1)}) custom-call(s32[8,128]{1,0:T(8,128)S(1)} %get-tuple-element.40.info, bf16[2,32,2,64,128]{4,3,2,1,0:T(8,128)(2,1)S(1)} %bitcast.28, bf16[2,32,2,64,128]{4,3,2,1,0:T(8,128)(2,1)S(1)} %bitcast.20, bf16[16,2,64,128]{3,2,1,0:T(8,128)(2,1)S(1)} %collective-permute-done.refs_0_.high_a, ...), custom_call_target="tpu_custom_call" | custom-call | flops 1 | bytes 1 | tf_op jit(solution)/shard_map/early_in/pallas_call | solution.py:610
  55.9 2.1 %collective-permute-done.11.refs_3_ = bf16[192,128]{1,0:T(8,128)(2,1)S(1)} collective-permute-done((bf16[192,128]{1,0:T(8,128)(2,1)S(1)}, bf16[192,128]{1,0:T(8,128)(2,1)S(1)}, u32[]{:S(2)}, u32[]{:S(2)}) %collective-permute-start.11) | collective-permute-done | bytes 49184 | tf_op jit(solution)/shard_map/ppermute | solution.py:519
  58.7 2.1 %collective-permute-start.14 = (bf16[192,128]{1,0:T(8,128)(2,1)S(1)}, bf16[192,128]{1,0:T(8,128)(2,1)S(1)}, u32[]{:S(2)}, u32[]{:S(2)}) collective-permute-start(bf16[192,128]{1,0:T(8,128)(2,1)S(1)} %x_sum.1.refs_0_), channel_id=1, source_target_pairs={{0,12},{4,0},{8,4},{12,8},{1,13},{5,1},{9,5},{13,9},{2,14},{6,2},{... | collective-permute-start | bytes 147464 | tf_op jit(solution)/shard_map/ppermute | solution.py:519
  60.8 1.6 %output.1 = (bf16[2,32,2,64,128]{4,3,2,1,0:T(8,128)(2,1)}, f32[8,128]{1,0:T(8,128)S(1)}) custom-call(s32[8,128]{1,0:T(8,128)S(1)} %get-tuple-element.40.info, bf16[2,32,2,64,128]{4,3,2,1,0:T(8,128)(2,1)S(1)} %bitcast.29, bf16[2,32,64,256]{3,2,1,0:T(8,128)(2,1)S(1)} %get-tuple-element.41.refs_2_.refs_4_.s, ...), custom_call_target="tpu_custom_call", output_to_operand_aliasing={{0}: (8, {})} | custom-call | flops 1 | bytes 1 | tf_op jit(solution)/shard_map/output/pallas_call | solution.py:614
  63.4 4.3 %collective-permute-start.15 = (bf16[192,128]{1,0:T(8,128)(2,1)S(1)}, bf16[192,128]{1,0:T(8,128)(2,1)S(1)}, u32[]{:S(2)}, u32[]{:S(2)}) collective-permute-start(bf16[192,128]{1,0:T(8,128)(2,1)S(1)} %y_sum.1.refs_0_), channel_id=1, source_target_pairs={{0,1},{1,2},{2,3},{3,0},{4,5},{5,6},{6,7},{7,4},{8,9},{9,10},{10,1... | collective-permute-start | bytes 147464 | tf_op jit(solution)/shard_map/ppermute | solution.py:519
  67.8 2.5 %collective-permute-start.17 = (bf16[192,128]{1,0:T(8,128)(2,1)S(1)}, bf16[192,128]{1,0:T(8,128)(2,1)S(1)}, u32[]{:S(2)}, u32[]{:S(2)}) collective-permute-start(bf16[192,128]{1,0:T(8,128)(2,1)S(1)} %y_sum.1.refs_0_), channel_id=1, source_target_pairs={{0,3},{1,0},{2,1},{3,2},{4,7},{5,4},{6,5},{7,6},{8,11},{9,8},{10,9... | collective-permute-start | bytes 147464 | tf_op jit(solution)/shard_map/ppermute | solution.py:519
  70.3 2.3 %input_grad.2 = (bf16[2,32,2,64,128]{4,3,2,1,0:T(8,128)(2,1)}, f32[8,128]{1,0:T(8,128)S(1)}) custom-call(s32[8,128]{1,0:T(8,128)S(1)} %get-tuple-element.40.info, bf16[2,32,2,64,128]{4,3,2,1,0:T(8,128)(2,1)S(1)} %bitcast.30, bf16[2,32,2,64,128]{4,3,2,1,0:T(8,128)(2,1)S(1)} %bitcast.21, ...), custom_call_target="tpu_custom_call", output_to_operand_aliasing={{0}: (9, {})} | custom-call | flops 1 | bytes 1 | tf_op jit(solution)/shard_map/input_grad/pallas_call | solution.py:620
  73.1 1.7 %collective-permute-start.18 = (bf16[192,128]{1,0:T(8,128)(2,1)S(1)}, bf16[192,128]{1,0:T(8,128)(2,1)S(1)}, u32[]{:S(2)}, u32[]{:S(2)}) collective-permute-start(bf16[192,128]{1,0:T(8,128)(2,1)S(1)} %z_sum.1.refs_0_), channel_id=1, source_target_pairs={{0,16},{16,32},{32,48},{48,0},{1,17},{17,33},{33,49},{49,1},{2,18}... | collective-permute-start | bytes 147464 | tf_op jit(solution)/shard_map/ppermute | solution.py:519
  74.7 2.3 %collective-permute-start.19 = (bf16[192,128]{1,0:T(8,128)(2,1)S(1)}, bf16[192,128]{1,0:T(8,128)(2,1)S(1)}, u32[]{:S(2)}, u32[]{:S(2)}) collective-permute-start(bf16[192,128]{1,0:T(8,128)(2,1)S(1)} %z_sum.1.refs_0_), channel_id=1, source_target_pairs={{0,32},{16,48},{32,0},{48,16},{1,33},{17,49},{33,1},{49,17},{2,34}... | collective-permute-start | bytes 147464 | tf_op jit(solution)/shard_map/ppermute | solution.py:519
  77.2 2.3 %input_grad.3 = (bf16[2,32,2,64,128]{4,3,2,1,0:T(8,128)(2,1)}, f32[8,128]{1,0:T(8,128)S(1)}) custom-call(s32[8,128]{1,0:T(8,128)S(1)} %get-tuple-element.40.info, bf16[2,32,2,64,128]{4,3,2,1,0:T(8,128)(2,1)S(1)} %bitcast.31, bf16[2,32,2,64,128]{4,3,2,1,0:T(8,128)(2,1)S(1)} %bitcast.22, ...), custom_call_target="tpu_custom_call", output_to_operand_aliasing={{0}: (9, {})} | custom-call | flops 1 | bytes 1 | tf_op jit(solution)/shard_map/input_grad/pallas_call | solution.py:620
  80.0 5.1 %collective-permute-start.21 = (bf16[4,192,128]{2,1,0:T(8,128)(2,1)S(1)}, bf16[4,192,128]{2,1,0:T(8,128)(2,1)S(1)}, u32[]{:S(2)}, u32[]{:S(2)}) collective-permute-start(bf16[4,192,128]{2,1,0:T(8,128)(2,1)S(1)} %x_stack.1.mine), channel_id=1, source_target_pairs={{0,64},{64,0},{1,65},{65,1},{2,66},{66,2},{3,67},{67,3},{4,68},{68... | collective-permute-start | bytes 589832 | tf_op jit(solution)/shard_map/ppermute | solution.py:634
  85.1 1.1 %collective-permute-done.21.theirs = bf16[4,192,128]{2,1,0:T(8,128)(2,1)S(1)} collective-permute-done((bf16[4,192,128]{2,1,0:T(8,128)(2,1)S(1)}, bf16[4,192,128]{2,1,0:T(8,128)(2,1)S(1)}, u32[]{:S(2)}, u32[]{:S(2)}) %collective-permute-start.21) | collective-permute-done | bytes 196640 | tf_op jit(solution)/shard_map/ppermute | solution.py:634
  86.1 1.1 %place.1 = (f32[1152,128]{1,0:T(8,128)}, f32[384,128]{1,0:T(8,128)}) custom-call(s32[8,128]{1,0:T(8,128)S(1)} %get-tuple-element.40.info, bf16[4,192,128]{2,1,0:T(8,128)(2,1)S(1)} %x_stack.1.mine, bf16[4,192,128]{2,1,0:T(8,128)(2,1)S(1)} %collective-permute-done.21.theirs), custom_call_target="tpu_custom_call" | custom-call | flops 1 | bytes 1 | tf_op jit(solution)/shard_map/place/pallas_call | solution.py:635
  (42 shorter events, 4.9 us)
Async XLA Ops:
  0.6 0.7 copy-start.4
  1.3 13.7 %copy-start.2 = (bf16[3,3,128,128]{3,2,1,0:T(8,128)(2,1)S(1)}, bf16[3,3,128,128]{3,2,1,0:T(8,128)(2,1)}, u32[]{:S(2)}) copy-start(bf16[3,3,128,128]{3,2,1,0:T(8,128)(2,1)} %w_ref.1) | copy-start | bytes 884740
  1.3 13.7 %copy-start.3 = (bf16[3,128,128]{2,1,0:T(8,128)(2,1)S(1)}, bf16[3,128,128]{2,1,0:T(8,128)(2,1)}, u32[]{:S(2)}) copy-start(bf16[3,128,128]{2,1,0:T(8,128)(2,1)} %tw_ref.1) | copy-start | bytes 294916
  2.6 21.0 %collective-permute-start = (bf16[16,2,64,128]{3,2,1,0:T(8,128)(2,1)S(1)}, bf16[16,2,64,128]{3,2,1,0:T(8,128)(2,1)S(1)}, u32[]{:S(2)}, u32[]{:S(2)}) collective-permute-start(bf16[16,2,64,128]{3,2,1,0:T(8,128)(2,1)S(1)} %get-tuple-element.42), channel_id=1, source_target_pairs={{1,2},{3,4},{5,6},{7,8},{9,10},{11,12},{13,14},{15,16},{17,18},{19... | collective-permute-start | bytes 1572872 | tf_op jit(solution)/shard_map/ppermute | solution.py:567
  11.9 12.5 %collective-permute-start.1 = (bf16[16,2,64,128]{3,2,1,0:T(8,128)(2,1)S(1)}, bf16[16,2,64,128]{3,2,1,0:T(8,128)(2,1)S(1)}, u32[]{:S(2)}, u32[]{:S(2)}) collective-permute-start(bf16[16,2,64,128]{3,2,1,0:T(8,128)(2,1)S(1)} %get-tuple-element.43), channel_id=1, source_target_pairs={{0,1},{2,3},{4,5},{6,7},{8,9},{10,11},{12,13},{14,15},{16,17},{18,... | collective-permute-start | bytes 1572872 | tf_op jit(solution)/shard_map/ppermute | solution.py:567
  11.9 3.1 %copy-start = (bf16[2,64,64,128]{3,2,1,0:T(8,128)(2,1)S(1)}, bf16[2,64,64,128]{3,2,1,0:T(8,128)(2,1)}, u32[]{:S(2)}) copy-start(bf16[2,64,64,128]{3,2,1,0:T(8,128)(2,1)} %param.6) | copy-start | bytes 6291460
  11.9 3.1 %copy-start.1 = (bf16[2,64,64,128]{3,2,1,0:T(8,128)(2,1)S(1)}, bf16[2,64,64,128]{3,2,1,0:T(8,128)(2,1)}, u32[]{:S(2)}) copy-start(bf16[2,64,64,128]{3,2,1,0:T(8,128)(2,1)} %param.5) | copy-start | bytes 6291460
  13.4 21.4 %collective-permute-start.4 = (bf16[16,2,64,128]{3,2,1,0:T(8,128)(2,1)S(1)}, bf16[16,2,64,128]{3,2,1,0:T(8,128)(2,1)S(1)}, u32[]{:S(2)}, u32[]{:S(2)}) collective-permute-start(bf16[16,2,64,128]{3,2,1,0:T(8,128)(2,1)S(1)} %get-tuple-element.48), channel_id=1, source_target_pairs={{1,2},{3,4},{5,6},{7,8},{9,10},{11,12},{13,14},{15,16},{17,18},{19... | collective-permute-start | bytes 1572872 | tf_op jit(solution)/shard_map/ppermute | solution.py:567
  13.7 21.9 %collective-permute-start.5 = (bf16[16,2,64,128]{3,2,1,0:T(8,128)(2,1)S(1)}, bf16[16,2,64,128]{3,2,1,0:T(8,128)(2,1)S(1)}, u32[]{:S(2)}, u32[]{:S(2)}) collective-permute-start(bf16[16,2,64,128]{3,2,1,0:T(8,128)(2,1)S(1)} %get-tuple-element.49), channel_id=1, source_target_pairs={{0,1},{2,3},{4,5},{6,7},{8,9},{10,11},{12,13},{14,15},{16,17},{18,... | collective-permute-start | bytes 1572872 | tf_op jit(solution)/shard_map/ppermute | solution.py:567
  26.3 20.2 %collective-permute-start.2 = (bf16[15,64,256]{2,1,0:T(8,128)(2,1)S(1)}, bf16[15,64,256]{2,1,0:T(8,128)(2,1)S(1)}, u32[]{:S(2)}, u32[]{:S(2)}) collective-permute-start(bf16[15,64,256]{2,1,0:T(8,128)(2,1)S(1)} %get-tuple-element.79), channel_id=1, source_target_pairs={{1,2},{3,4},{5,6},{7,8},{9,10},{11,12},{13,14},{15,16},{17,18},{19... | collective-permute-start | bytes 1474568 | tf_op jit(solution)/shard_map/ppermute | solution.py:567
  32.2 14.4 %collective-permute-start.3 = (bf16[15,64,256]{2,1,0:T(8,128)(2,1)S(1)}, bf16[15,64,256]{2,1,0:T(8,128)(2,1)S(1)}, u32[]{:S(2)}, u32[]{:S(2)}) collective-permute-start(bf16[15,64,256]{2,1,0:T(8,128)(2,1)S(1)} %get-tuple-element.78), channel_id=1, source_target_pairs={{0,1},{2,3},{4,5},{6,7},{8,9},{10,11},{12,13},{14,15},{16,17},{18,... | collective-permute-start | bytes 1474568 | tf_op jit(solution)/shard_map/ppermute | solution.py:567
  37.8 23.0 %collective-permute-start.6 = (bf16[17,64,256]{2,1,0:T(8,128)(2,1)S(1)}, bf16[17,64,256]{2,1,0:T(8,128)(2,1)S(1)}, u32[]{:S(2)}, u32[]{:S(2)}) collective-permute-start(bf16[17,64,256]{2,1,0:T(8,128)(2,1)S(1)} %get-tuple-element.77), channel_id=1, source_target_pairs={{1,2},{3,4},{5,6},{7,8},{9,10},{11,12},{13,14},{15,16},{17,18},{19... | collective-permute-start | bytes 1671176 | tf_op jit(solution)/shard_map/ppermute | solution.py:567
  43.6 17.2 %collective-permute-start.7 = (bf16[17,64,256]{2,1,0:T(8,128)(2,1)S(1)}, bf16[17,64,256]{2,1,0:T(8,128)(2,1)S(1)}, u32[]{:S(2)}, u32[]{:S(2)}) collective-permute-start(bf16[17,64,256]{2,1,0:T(8,128)(2,1)S(1)} %get-tuple-element.76), channel_id=1, source_target_pairs={{0,1},{2,3},{4,5},{6,7},{8,9},{10,11},{12,13},{14,15},{16,17},{18,... | collective-permute-start | bytes 1671176 | tf_op jit(solution)/shard_map/ppermute | solution.py:567
  46.6 4.4 %collective-permute-start.8 = (f32[4,192,128]{2,1,0:T(8,128)S(1)}, f32[4,192,128]{2,1,0:T(8,128)S(1)}, u32[]{:S(2)}, u32[]{:S(2)}) collective-permute-start(f32[4,192,128]{2,1,0:T(8,128)S(1)} %hold.1), channel_id=1, source_target_pairs={{0,64},{64,0},{1,65},{65,1},{2,66},{66,2},{3,67},{67,3},{4,68},{68... | collective-permute-start | bytes 1179656 | tf_op jit(solution)/shard_map/ppermute | solution.py:605
  51.1 4.8 %collective-permute-start.10 = (bf16[192,128]{1,0:T(8,128)(2,1)S(1)}, bf16[192,128]{1,0:T(8,128)(2,1)S(1)}, u32[]{:S(2)}, u32[]{:S(2)}) collective-permute-start(bf16[192,128]{1,0:T(8,128)(2,1)S(1)} %get-tuple-element.67), channel_id=1, source_target_pairs={{0,32},{16,48},{32,0},{48,16},{1,33},{17,49},{33,1},{49,17},{2,34}... | collective-permute-start | bytes 147464 | tf_op jit(solution)/shard_map/ppermute | solution.py:519
  51.5 6.5 %collective-permute-start.11 = (bf16[192,128]{1,0:T(8,128)(2,1)S(1)}, bf16[192,128]{1,0:T(8,128)(2,1)S(1)}, u32[]{:S(2)}, u32[]{:S(2)}) collective-permute-start(bf16[192,128]{1,0:T(8,128)(2,1)S(1)} %get-tuple-element.68), channel_id=1, source_target_pairs={{0,48},{16,0},{32,16},{48,32},{1,49},{17,1},{33,17},{49,33},{2,50}... | collective-permute-start | bytes 147464 | tf_op jit(solution)/shard_map/ppermute | solution.py:519
  52.4 5.7 %collective-permute-start.9 = (bf16[192,128]{1,0:T(8,128)(2,1)S(1)}, bf16[192,128]{1,0:T(8,128)(2,1)S(1)}, u32[]{:S(2)}, u32[]{:S(2)}) collective-permute-start(bf16[192,128]{1,0:T(8,128)(2,1)S(1)} %get-tuple-element.66), channel_id=1, source_target_pairs={{0,16},{16,32},{32,48},{48,0},{1,17},{17,33},{33,49},{49,1},{2,18}... | collective-permute-start | bytes 147464 | tf_op jit(solution)/shard_map/ppermute | solution.py:519
  58.1 4.4 %collective-permute-start.12 = (bf16[192,128]{1,0:T(8,128)(2,1)S(1)}, bf16[192,128]{1,0:T(8,128)(2,1)S(1)}, u32[]{:S(2)}, u32[]{:S(2)}) collective-permute-start(bf16[192,128]{1,0:T(8,128)(2,1)S(1)} %x_sum.1.refs_0_), channel_id=1, source_target_pairs={{0,4},{4,8},{8,12},{12,0},{1,5},{5,9},{9,13},{13,1},{2,6},{6,10},{... | collective-permute-start | bytes 147464 | tf_op jit(solution)/shard_map/ppermute | solution.py:519
  58.1 5.0 %collective-permute-start.13 = (bf16[192,128]{1,0:T(8,128)(2,1)S(1)}, bf16[192,128]{1,0:T(8,128)(2,1)S(1)}, u32[]{:S(2)}, u32[]{:S(2)}) collective-permute-start(bf16[192,128]{1,0:T(8,128)(2,1)S(1)} %x_sum.1.refs_0_), channel_id=1, source_target_pairs={{0,8},{4,12},{8,0},{12,4},{1,9},{5,13},{9,1},{13,5},{2,10},{6,14},... | collective-permute-start | bytes 147464 | tf_op jit(solution)/shard_map/ppermute | solution.py:519
  58.7 4.7 %collective-permute-start.14 = (bf16[192,128]{1,0:T(8,128)(2,1)S(1)}, bf16[192,128]{1,0:T(8,128)(2,1)S(1)}, u32[]{:S(2)}, u32[]{:S(2)}) collective-permute-start(bf16[192,128]{1,0:T(8,128)(2,1)S(1)} %x_sum.1.refs_0_), channel_id=1, source_target_pairs={{0,12},{4,0},{8,4},{12,8},{1,13},{5,1},{9,5},{13,9},{2,14},{6,2},{... | collective-permute-start | bytes 147464 | tf_op jit(solution)/shard_map/ppermute | solution.py:519
  63.4 9.2 %collective-permute-start.15 = (bf16[192,128]{1,0:T(8,128)(2,1)S(1)}, bf16[192,128]{1,0:T(8,128)(2,1)S(1)}, u32[]{:S(2)}, u32[]{:S(2)}) collective-permute-start(bf16[192,128]{1,0:T(8,128)(2,1)S(1)} %y_sum.1.refs_0_), channel_id=1, source_target_pairs={{0,1},{1,2},{2,3},{3,0},{4,5},{5,6},{6,7},{7,4},{8,9},{9,10},{10,1... | collective-permute-start | bytes 147464 | tf_op jit(solution)/shard_map/ppermute | solution.py:519
  67.8 5.3 %collective-permute-start.16 = (bf16[192,128]{1,0:T(8,128)(2,1)S(1)}, bf16[192,128]{1,0:T(8,128)(2,1)S(1)}, u32[]{:S(2)}, u32[]{:S(2)}) collective-permute-start(bf16[192,128]{1,0:T(8,128)(2,1)S(1)} %y_sum.1.refs_0_), channel_id=1, source_target_pairs={{0,2},{1,3},{2,0},{3,1},{4,6},{5,7},{6,4},{7,5},{8,10},{9,11},{10,... | collective-permute-start | bytes 147464 | tf_op jit(solution)/shard_map/ppermute | solution.py:519
  67.8 5.3 %collective-permute-start.17 = (bf16[192,128]{1,0:T(8,128)(2,1)S(1)}, bf16[192,128]{1,0:T(8,128)(2,1)S(1)}, u32[]{:S(2)}, u32[]{:S(2)}) collective-permute-start(bf16[192,128]{1,0:T(8,128)(2,1)S(1)} %y_sum.1.refs_0_), channel_id=1, source_target_pairs={{0,3},{1,0},{2,1},{3,2},{4,7},{5,4},{6,5},{7,6},{8,11},{9,8},{10,9... | collective-permute-start | bytes 147464 | tf_op jit(solution)/shard_map/ppermute | solution.py:519
  73.1 6.5 %collective-permute-start.18 = (bf16[192,128]{1,0:T(8,128)(2,1)S(1)}, bf16[192,128]{1,0:T(8,128)(2,1)S(1)}, u32[]{:S(2)}, u32[]{:S(2)}) collective-permute-start(bf16[192,128]{1,0:T(8,128)(2,1)S(1)} %z_sum.1.refs_0_), channel_id=1, source_target_pairs={{0,16},{16,32},{32,48},{48,0},{1,17},{17,33},{33,49},{49,1},{2,18}... | collective-permute-start | bytes 147464 | tf_op jit(solution)/shard_map/ppermute | solution.py:519
  74.7 4.8 %collective-permute-start.19 = (bf16[192,128]{1,0:T(8,128)(2,1)S(1)}, bf16[192,128]{1,0:T(8,128)(2,1)S(1)}, u32[]{:S(2)}, u32[]{:S(2)}) collective-permute-start(bf16[192,128]{1,0:T(8,128)(2,1)S(1)} %z_sum.1.refs_0_), channel_id=1, source_target_pairs={{0,32},{16,48},{32,0},{48,16},{1,33},{17,49},{33,1},{49,17},{2,34}... | collective-permute-start | bytes 147464 | tf_op jit(solution)/shard_map/ppermute | solution.py:519
  77.0 2.9 %collective-permute-start.20 = (bf16[192,128]{1,0:T(8,128)(2,1)S(1)}, bf16[192,128]{1,0:T(8,128)(2,1)S(1)}, u32[]{:S(2)}, u32[]{:S(2)}) collective-permute-start(bf16[192,128]{1,0:T(8,128)(2,1)S(1)} %z_sum.1.refs_0_), channel_id=1, source_target_pairs={{0,48},{16,0},{32,16},{48,32},{1,49},{17,1},{33,17},{49,33},{2,50}... | collective-permute-start | bytes 147464 | tf_op jit(solution)/shard_map/ppermute | solution.py:519
  80.0 6.1 %collective-permute-start.21 = (bf16[4,192,128]{2,1,0:T(8,128)(2,1)S(1)}, bf16[4,192,128]{2,1,0:T(8,128)(2,1)S(1)}, u32[]{:S(2)}, u32[]{:S(2)}) collective-permute-start(bf16[4,192,128]{2,1,0:T(8,128)(2,1)S(1)} %x_stack.1.mine), channel_id=1, source_target_pairs={{0,64},{64,0},{1,65},{65,1},{2,66},{66,2},{3,67},{67,3},{4,68},{68... | collective-permute-start | bytes 589832 | tf_op jit(solution)/shard_map/ppermute | solution.py:634
